TPU v7x, 256 devices: a whole 4x4x8 slice. The times are simulated.
256 devices in a mesh: ctx: 32 (over y, z), head: 8 (over x, core).
Axes of the slice: x: 4, y: 4, z: 8, core: 2. Of those that a mesh axis runs over, the one named last changes fastest.
Arguments:
- query: bfloat16 [16384, 64, 128], P('ctx', 'head'), may hold values from -6 to 6
- key: bfloat16 [16384, 64, 128], P('ctx', 'head'), may hold values from -6 to 6
- value: bfloat16 [16384, 64, 128], P('ctx', 'head'), may hold values from -40 to 40
- gain: float32 [64, 128], P('head'), may hold values from 0.1 to 1.9
- cotangent: bfloat16 [16384, 64, 128], P('ctx', 'head'), may hold values from -6 to 6
- query2: bfloat16 [16384, 64, 128], P('ctx', 'head'), may hold values from -5 to 5
- key2: bfloat16 [16384, 8, 128], P('ctx', 'head'), may hold values from -5 to 5
- softmax_values: bfloat16 [16384, 8, 128], P('ctx', 'head'), may hold values from -6 to 6
Outputs:
- normed: bfloat16 [16384, 64, 128], P('ctx', 'head')
- grad_query: bfloat16 [16384, 64, 128], P('ctx', 'head')
- grad_key: bfloat16 [16384, 64, 128], P('ctx', 'head')
- grad_value: bfloat16 [16384, 64, 128], P('ctx', 'head')
- attended: bfloat16 [16384, 64, 128], P('ctx', 'head')
All inputs are finite; a program needn't handle non-finite values.
Results may differ from a plain program's by a relative error of at most 0.02.
Values may be sent and summed in bfloat16 or wider, within the bound.
No kernel may reach another device: no remote copies, remote signals or barrier semaphores. Data moves between devices by JAX's collectives and lax.ppermute only.
A program may use at most 128 MiB of HBM per device.

v0:
```python
import functools
import jax
import jax.numpy as jnp
from jax import lax
from jax.experimental import pallas as pl
from jax.experimental.pallas import tpu as pltpu
from jax.sharding import Mesh, PartitionSpec as P

ATTN_HEADS = 64
HEAD_WIDTH = 128
WINDOW_BLOCKS = 4
CHANNELS = ATTN_HEADS * HEAD_WIDTH
EPSILON = 1e-06
LOG2E = 1.4426950408889634

f32 = jnp.float32
bf16 = jnp.bfloat16
MIB = 1 << 20
HEADS = ("x", "core")
CTX = ("y", "z")


def nn(a, b, precision=None):
    return lax.dot_general(
        a, b, (((1,), (0,)), ((), ())), precision=precision, preferred_element_type=f32
    )


def nt(a, b, precision=None):
    return lax.dot_general(
        a, b, (((1,), (1,)), ((), ())), precision=precision, preferred_element_type=f32
    )


def tn(a, b, precision=None):
    return lax.dot_general(
        a, b, (((0,), (0,)), ((), ())), precision=precision, preferred_element_type=f32
    )


def call(kernel, out_shapes, args, scratch=(), flops=0, smem_first=False, vmem=20, hbm_in=(), hbm_out=()):
    def place(i, far):
        return pl.BlockSpec(memory_space=pltpu.HBM if i in far else pltpu.VMEM)

    specs = [place(i, hbm_in) for i in range(len(args))]
    if smem_first:
        specs[0] = pl.BlockSpec(memory_space=pltpu.SMEM)
    moved = sum(a.size * a.dtype.itemsize for a in (*args, *out_shapes))
    return pl.pallas_call(
        kernel,
        out_shape=out_shapes,
        in_specs=specs,
        out_specs=[place(i, hbm_out) for i in range(len(out_shapes))],
        scratch_shapes=list(scratch),
        compiler_params=pltpu.CompilerParams(vmem_limit_bytes=vmem * MIB),
        cost_estimate=pl.CostEstimate(flops=flops, bytes_accessed=moved, transcendentals=0),
    )(*args)


def shape(dims, dtype):
    return jax.ShapeDtypeStruct(dims, dtype)


def fetch(pairs, sems):
    copies = []
    for i, (src, dst) in enumerate(pairs):
        copy = pltpu.make_async_copy(src, dst, sems.at[i])
        copy.start()
        copies.append(copy)
    return copies


def state_kernel(k_ref, v_ref, kh_ref, vh_ref, st_ref, ks, vs):
    tokens, heads, width = k_ref.shape
    ks[...] = k_ref[...].astype(f32).reshape(tokens * heads, width)
    vs[...] = v_ref[...].astype(f32).reshape(tokens * heads, width)
    for h in range(heads):
        kh = ks[pl.ds(h, tokens, stride=heads), :].astype(bf16)
        vh = vs[pl.ds(h, tokens, stride=heads), :].astype(bf16)
        kh_ref[h] = kh
        vh_ref[h] = vh
        st_ref[h] = tn(kh, vh).astype(bf16)


def each(count, body, unroll=8):
    def step(i, carry):
        body(i)
        return carry

    lax.fori_loop(0, count, step, 0, unroll=unroll)


def causal_below(rows):
    r = lax.broadcasted_iota(jnp.int32, (rows, rows), 0)
    c = lax.broadcasted_iota(jnp.int32, (rows, rows), 1)
    return c <= r


def local_kernel(q_ref, c_ref, gain_ref, kh_ref, vh_ref, qh_ref, gh_ref, loc_ref, qs, cs):
    tokens, heads, width = q_ref.shape
    half = tokens // 2
    qs[...] = q_ref[...].astype(f32).reshape(tokens * heads, width)
    cs[...] = (c_ref[...].astype(f32) * gain_ref[...][None]).reshape(tokens * heads, width)
    causal = causal_below(half)

    def head(h):
        qh = qs[pl.ds(h, tokens, stride=heads), :].astype(bf16)
        qh_ref[h] = qh
        gh_ref[h] = cs[pl.ds(h, tokens, stride=heads), :]
        kh = kh_ref[h]
        vh = vh_ref[h]
        w0 = jnp.where(causal, nt(qh[:half], kh[:half]), 0.0).astype(bf16)
        w10 = nt(qh[half:], kh[:half]).astype(bf16)
        w11 = jnp.where(causal, nt(qh[half:], kh[half:]), 0.0).astype(bf16)
        loc_ref[h, :half] = nn(w0, vh[:half])
        loc_ref[h, half:] = nn(w10, vh[:half]) + nn(w11, vh[half:])

    each(heads, head)


def attention_kernel(loc_ref, qh_ref, gh_ref, pre_ref, att_ref, part_ref):
    heads, tokens, width = loc_ref.shape
    squares = jnp.zeros((tokens, width), f32)
    inner = jnp.zeros((tokens, width), f32)
    for h in range(heads):
        att = loc_ref[h] + nn(qh_ref[h], pre_ref[h])
        att_ref[h] = att
        squares = squares + att * att
        inner = inner + att * gh_ref[h]
    ones = jnp.ones((8, width), f32)
    rows = jnp.concatenate(
        [
            nt(ones, squares, lax.Precision.HIGHEST)[0:1],
            nt(ones, inner, lax.Precision.HIGHEST)[0:1],
        ]
    )
    for j in range(part_ref.shape[0]):
        part_ref[j] = rows


def row_scales(g_ref):
    ones = jnp.ones((g_ref.shape[0], HEAD_WIDTH), f32)
    squares = tn(g_ref[:, 0, :], ones, lax.Precision.HIGHEST)
    inner = tn(g_ref[:, 1, :], ones, lax.Precision.HIGHEST)
    inverse = 1.0 / jnp.sqrt(squares / CHANNELS + EPSILON)
    return inverse, inverse * inner / CHANNELS


def backward_kernel(g_ref, att_ref, gh_ref, qh_ref, da_ref, bg_ref, inv_ref):
    inverse, mean = row_scales(g_ref)
    inv_ref[...] = inverse
    scaled = inverse * mean
    for h in range(att_ref.shape[0]):
        d = ((gh_ref[h] - att_ref[h] * scaled) * inverse).astype(bf16)
        da_ref[h] = d
        bg_ref[h] = tn(qh_ref[h], d).astype(bf16)


def softmax_kernel(
    pos_ref, att_ref, inv_ref, gain_ref, q2_ref, kv0, kv1, kv2, kv3,
    norm_hbm, out_hbm, norm, out, scratch, ahead, sems,
):
    heads, tokens, width = att_ref.shape
    kv = (kv0, kv1, kv2, kv3)
    inverse = inv_ref[...]
    for h in range(heads):
        scratch[pl.ds(h, tokens, stride=heads), :] = (
            gain_ref[h : h + 1, :] * (att_ref[h] * inverse)
        )
    norm[...] = scratch[...].astype(bf16).reshape(tokens, heads, width)
    writes = fetch([(norm, norm_hbm)], sems.at[pl.ds(4, 1)])

    scale = LOG2E * HEAD_WIDTH ** (-0.5)
    ones = jnp.ones((tokens, width), bf16)
    quarters = 4
    quarter = tokens // quarters

    def query_rows(chunk, rows):
        chunk_tokens = rows // heads
        t0 = pl.multiple_of(chunk * chunk_tokens, chunk_tokens)
        n = scratch[pl.ds(pl.multiple_of(chunk * rows, rows), rows), :].astype(bf16).astype(f32)
        q2 = q2_ref[pl.ds(t0, chunk_tokens)].astype(f32).reshape(rows, width)
        return (q2 + n).astype(bf16)

    def scores(chunk, rows, count):
        q = query_rows(chunk, rows)
        row = chunk * rows + lax.broadcasted_iota(jnp.int32, (rows, tokens), 0)
        column = lax.broadcasted_iota(jnp.int32, (rows, tokens), 1)
        own = jnp.where(column <= row // heads, nt(q, kv[0][0]), -1e30)
        return [own] + [nt(q, kv[b][0]) for b in range(1, count)]

    def weigh(parts, chunk, rows):
        top = None
        for s in parts:
            for j in range(0, tokens, 128):
                piece = s[:, j : j + 128]
                top = piece if top is None else jnp.maximum(top, piece)
        top = jnp.max(top, axis=1, keepdims=True) * scale
        total = None
        for b, s in enumerate(parts):
            p = jnp.exp2(s * scale - top).astype(bf16)
            o = nn(p, jnp.concatenate([kv[b][1], ones], axis=1))
            total = o if total is None else total + o
        chunk_tokens = rows // heads
        t0 = pl.multiple_of(chunk * chunk_tokens, chunk_tokens)
        out[pl.ds(t0, chunk_tokens)] = (
            (total[:, :width] / total[:, width:]).astype(bf16).reshape(chunk_tokens, heads, width)
        )

    def store(i):
        part = pl.ds(pl.multiple_of(i * quarter, quarter), quarter)
        return pltpu.make_async_copy(out.at[part], out_hbm.at[part], sems.at[i])

    def run(count):
        rows = 256
        per = quarter * heads // rows

        def body(i, carry):
            for j in range(per):
                chunk = i * per + j
                weigh(scores(chunk, rows, count), chunk, rows)
            store(i).start()
            return carry

        lax.fori_loop(0, quarters, body, 0)

    def run_ahead():
        rows = 512
        per = quarter * heads // rows
        last = quarters * per - 1

        def put(slot, chunk):
            for b, s in enumerate(scores(chunk, rows, WINDOW_BLOCKS)):
                ahead[slot, b] = s

        def body(i, carry):
            for j in range(per):
                chunk = i * per + j
                put((j + 1) % 2, jnp.minimum(chunk + 1, last))
                weigh([ahead[j % 2, b] for b in range(WINDOW_BLOCKS)], chunk, rows)
            store(i).start()
            return carry

        put(0, 0)
        lax.fori_loop(0, quarters, body, 0)

    have = pos_ref[0]
    for count in range(1, WINDOW_BLOCKS):
        pl.when(have == count - 1)(functools.partial(run, count))
    pl.when(have == WINDOW_BLOCKS - 1)(run_ahead)
    for i in range(quarters):
        store(i).wait()
    writes[0].wait()


def query_gradient_kernel(kh_ref, vh_ref, da_ref, pre_ref, gq_hbm, qs, out, sems):
    heads, tokens, width = kh_ref.shape
    half = tokens // 2
    below = causal_below(half)
    lo, hi = slice(0, half), slice(half, tokens)

    def head(h):
        k, v, da = kh_ref[h], vh_ref[h], da_ref[h]
        d00 = jnp.where(below, nt(da[lo], v[lo]), 0.0).astype(bf16)
        d10 = nt(da[hi], v[lo]).astype(bf16)
        d11 = jnp.where(below, nt(da[hi], v[hi]), 0.0).astype(bf16)
        gq = nt(da, pre_ref[h])
        qs[pl.ds(h, half, stride=heads), :] = gq[lo] + nn(d00, k[lo])
        qs[pl.ds(half * heads + h, half, stride=heads), :] = (
            gq[hi] + nn(d10, k[lo]) + nn(d11, k[hi])
        )

    each(heads, head)
    pieces = sems.shape[0]
    rows = tokens // pieces
    copies = []
    for i in range(pieces):
        part = pl.ds(i * rows, rows)
        out[part] = (
            qs[pl.ds(i * rows * heads, rows * heads), :].astype(bf16).reshape(rows, heads, width)
        )
        copies += fetch([(out.at[part], gq_hbm.at[part])], sems.at[pl.ds(i, 1)])
    for copy in copies:
        copy.wait()


def key_value_local_kernel(qh_ref, kh_ref, vh_ref, da_ref, gk_ref, gv_ref):
    heads, tokens, width = qh_ref.shape
    half = tokens // 2
    r = lax.broadcasted_iota(jnp.int32, (half, half), 0)
    c = lax.broadcasted_iota(jnp.int32, (half, half), 1)
    above = r <= c
    lo, hi = slice(0, half), slice(half, tokens)

    def up(x):
        return jnp.where(above, x, 0.0).astype(bf16)

    def head(h):
        q, k, v, da = qh_ref[h], kh_ref[h], vh_ref[h], da_ref[h]
        for out, a, b, other in ((gk_ref, v, da, q), (gv_ref, k, q, da)):
            m00 = up(nt(a[lo], b[lo]))
            m01 = nt(a[lo], b[hi]).astype(bf16)
            m11 = up(nt(a[hi], b[hi]))
            out[h, :half] = nn(m00, other[lo]) + nn(m01, other[hi])
            out[h, half:] = nn(m11, other[hi])

    each(heads, head)


def finish_kernel(
    kh_ref, vh_ref, pk_ref, pv_ref, suf_ref, gk_hbm, gv_hbm, ks, vs, kb, vb, sems
):
    heads, tokens, width = kh_ref.shape
    pieces = sems.shape[0] // 2
    rows = tokens // pieces
    copies = []
    for i in range(pieces):
        part = pl.ds(i * rows, rows)
        for h in range(heads):
            suf = suf_ref[h]
            target = pl.ds(i * rows * heads + h, rows, stride=heads)
            ks[target, :] = pk_ref[h, part] + nt(vh_ref[h, part], suf)
            vs[target, :] = pv_ref[h, part] + nn(kh_ref[h, part], suf)
        flat = pl.ds(i * rows * heads, rows * heads)
        for src, buffer in ((ks, kb), (vs, vb)):
            buffer[part] = src[flat, :].astype(bf16).reshape(rows, heads, width)
        copies += fetch(
            [(kb.at[part], gk_hbm.at[part]), (vb.at[part], gv_hbm.at[part])],
            sems.at[pl.ds(2 * i, 2)],
        )
    for copy in copies:
        copy.wait()


def scan_kernel(back, recv_ref, t1_ref, t2_ref, t3_ref, out_ref):
    count = recv_ref.shape[0]
    running = t1_ref[...].astype(f32) + t2_ref[...].astype(f32) + t3_ref[...].astype(f32)
    order = range(count - 1, -1, -1) if back else range(count)
    for i in order:
        out_ref[i] = running.astype(bf16)
        running = running + recv_ref[i].astype(f32)


def total_kernel(recv_ref, *refs):
    *sources, out_ref = refs[:3]
    for j, source in enumerate(sources):
        refs[3][j] = source[...]
    total = recv_ref[0].astype(f32)
    for i in range(1, recv_ref.shape[0]):
        total = total + recv_ref[i].astype(f32)
    out_ref[...] = total.astype(bf16)


def tied(*values):
    return lax.optimization_barrier(values)


def row_total(pieces):
    return call(total_kernel, [shape(pieces.shape[1:], bf16)], [pieces])[0]


def other_rows(total, back):
    rows = lax.axis_size("y")
    got = []
    for d in (2, 1, 3):
        pairs = [(i + d, i) if back else (i, i + d) for i in range(rows - d)]
        got.append(lax.ppermute(total, "y", pairs))
    return got


def scanned(pieces, totals, back):
    return call(
        functools.partial(scan_kernel, back), [shape(pieces.shape, bf16)], [pieces, *totals]
    )[0]


def spread(x):
    return lax.all_to_all(x, "z", 0, 0, tiled=True)


def local(query, key, value, gain, cotangent, query2, key2, softmax_values):
    tokens, heads, width = query.shape
    flat = (tokens * heads, width)
    head_major = (heads, tokens, width)
    square = (heads, width, width)
    unit = 2 * tokens * tokens * width * heads
    ring = lax.axis_size(CTX)
    members = lax.axis_size(HEADS)
    token_buffer = pltpu.VMEM(query.shape, bf16)
    flat_buffer = pltpu.VMEM(flat, f32)

    def sems(n):
        return pltpu.SemaphoreType.DMA((n,))

    def onward(x):
        return lax.ppermute(x, CTX, [(i, i + 1) for i in range(ring - 1)])

    have = jnp.minimum(lax.axis_index(CTX), WINDOW_BLOCKS - 1).astype(jnp.int32).reshape(1)
    key, value, have = tied(key, value, have)

    kh, vh, states = call(
        state_kernel,
        [shape(head_major, bf16), shape(head_major, bf16), shape(square, bf16)],
        [key, value],
        [flat_buffer, flat_buffer],
        unit // 4,
    )
    states, query, cotangent = tied(states, query, cotangent)
    pieces, kh, vh = tied(spread(states), kh, vh)
    total, kv0 = call(
        total_kernel,
        [shape(square[1:], bf16), shape((2, tokens, width), bf16)],
        [pieces, key2[:, 0], softmax_values[:, 0]],
    )
    total, kh, vh = tied(total, kh, vh)
    totals = other_rows(total, False)
    kv1 = onward(kv0)
    qh, gh, loc = call(
        local_kernel,
        [shape(head_major, bf16), shape(head_major, f32), shape(head_major, f32)],
        [query, cotangent, gain, kh, vh],
        [flat_buffer, flat_buffer],
        2 * unit,
    )
    *totals, kv1, loc = tied(*totals, kv1, loc)
    prefix, kv1 = tied(spread(scanned(pieces, totals, False)), kv1)
    kv2 = onward(kv1)
    att, part = call(
        attention_kernel,
        [shape(head_major, f32), shape((members, 2, tokens), f32)],
        [loc, qh, gh, prefix],
        (),
        unit // 4,
    )
    gathered = lax.all_to_all(part, HEADS, 0, 0, tiled=True)
    gathered, kv2 = tied(gathered, kv2)
    da, block_grad, inverse = call(
        backward_kernel,
        [shape(head_major, bf16), shape(square, bf16), shape((tokens, width), f32)],
        [gathered, att, gh, qh],
        (),
        unit // 4,
    )
    back_pieces, att, da, inverse, kv2 = tied(spread(block_grad), att, da, inverse, kv2)
    back_total, att, da, inverse, kv2 = tied(row_total(back_pieces), att, da, inverse, kv2)
    kv3 = onward(kv2)
    back_totals = other_rows(back_total, True)
    normed, attended = call(
        softmax_kernel,
        [shape(query.shape, bf16), shape(query.shape, bf16)],
        [have, att, inverse, gain, query2, kv0, kv1, kv2, kv3],
        [
            token_buffer,
            token_buffer,
            flat_buffer,
            pltpu.VMEM((2, WINDOW_BLOCKS, tokens, tokens), f32),
            sems(5),
        ],
        8 * unit,
        smem_first=True,
        vmem=40,
        hbm_out=(0, 1),
    )
    (gq,) = call(
        query_gradient_kernel,
        [shape(query.shape, bf16)],
        [kh, vh, da, prefix],
        [flat_buffer, token_buffer, sems(4)],
        2 * unit,
        hbm_out=(0,),
    )
    pk, pv = call(
        key_value_local_kernel, [shape(head_major, f32)] * 2, [qh, kh, vh, da], (), 4 * unit
    )
    *back_totals, normed, attended, gq, pk, pv = tied(
        *back_totals, normed, attended, gq, pk, pv
    )
    suffix = spread(scanned(back_pieces, back_totals, True))
    gk, gv = call(
        finish_kernel,
        [shape(query.shape, bf16)] * 2,
        [kh, vh, pk, pv, suffix],
        [flat_buffer, flat_buffer, token_buffer, token_buffer, sems(8)],
        unit // 2,
        hbm_out=(0, 1),
    )
    return normed, gq, gk, gv, attended


def solution(mesh):
    sizes = (4, 8, 4, 2)
    fine = Mesh(mesh.devices.reshape(sizes), ("y", "z", "x", "core"))
    tokens = P(CTX, HEADS, None)
    return jax.shard_map(
        local,
        mesh=fine,
        in_specs=(tokens, tokens, tokens, P(HEADS, None), tokens, tokens, tokens, tokens),
        out_specs=(tokens,) * 5,
        check_vma=False,
    )
```

profile of v0, /device:TPU:8, one launch (start us, length us, event | category | flops | bytes accessed | tf_op | source)
XLA Modules:
  0.0 130.7 jit_solution(10836359312368442653)
XLA Ops:
  0.6 0.0 copy-start.1
  0.6 0.0 copy-start
  0.7 0.0 copy-start.2
  0.7 1.4 %copy-done.2 = bf16[512,8,128]{2,1,0:T(8,128)(2,1)S(1)} copy-done((bf16[512,8,128]{2,1,0:T(8,128)(2,1)S(1)}, bf16[512,8,128]{2,1,0:T(8,128)(2,1)}, u32[]{:S(2)}) %copy-start.2) | copy-done | bytes 1048600
  2.0 0.0 copy-start.3
  2.0 1.2 copy-done.3
  3.3 0.0 copy-start.4
  3.3 0.0 copy-start.5
  3.3 0.0 copy-start.6
  3.3 1.3 shard_map.119
  4.5 20.1 %all_to_all.25.recv_ref = bf16[8,128,128]{2,1,0:T(8,128)(2,1)S(1)} all-to-all(bf16[8,128,128]{2,1,0:T(8,128)(2,1)S(1)} %get-tuple-element.66), channel_id=1, replica_groups=mesh['y'=4,'z'=8,'x'=4,'core'=2] {'z'}, dimensions={0} | all-to-all | bytes 524288 | tf_op jit(solution)/shard_map/all_to_all | solution.py:378
  24.7 0.0 copy-done.4
  24.7 0.0 copy-done.5
  24.7 0.1 shard_map.120
  24.7 2.5 %collective-permute-start.3 = (bf16[2,512,128]{2,1,0:T(8,128)(2,1)S(1)}, bf16[2,512,128]{2,1,0:T(8,128)(2,1)S(1)}, u32[]{:S(2)}, u32[]{:S(2)}) collective-permute-start(bf16[2,512,128]{2,1,0:T(8,128)(2,1)S(1)} %get-tuple-element.74.kv0), channel_id=1, source_target_pairs={{0,8},{8,16},{16,24},{24,32},{32,40},{40,48},{48,56},{56,64},{64,7... | collective-permute-start | bytes 786440 | tf_op jit(solution)/shard_map/ppermute | solution.py:396
  27.2 0.7 collective-permute-start.2
  27.9 3.5 %collective-permute-start.1 = (bf16[128,128]{1,0:T(8,128)(2,1)S(1)}, bf16[128,128]{1,0:T(8,128)(2,1)S(1)}, u32[]{:S(2)}, u32[]{:S(2)}) collective-permute-start(bf16[128,128]{1,0:T(8,128)(2,1)S(1)} %get-tuple-element.73), channel_id=1, source_target_pairs={{0,64},{64,128},{128,192},{1,65},{65,129},{129,193},{2,66},{66,130... | collective-permute-start | bytes 98312 | tf_op jit(solution)/shard_map/ppermute | solution.py:367
  31.4 2.6 %collective-permute-start = (bf16[128,128]{1,0:T(8,128)(2,1)S(1)}, bf16[128,128]{1,0:T(8,128)(2,1)S(1)}, u32[]{:S(2)}, u32[]{:S(2)}) collective-permute-start(bf16[128,128]{1,0:T(8,128)(2,1)S(1)} %get-tuple-element.73), channel_id=1, source_target_pairs={{0,128},{64,192},{1,129},{65,193},{2,130},{66,194},{3,131},{67,195... | collective-permute-start | bytes 98312 | tf_op jit(solution)/shard_map/ppermute | solution.py:367
  34.0 0.0 copy-done.1
  34.0 0.0 copy-done
  34.0 0.0 copy-done.6
  34.0 2.6 %shard_map.121 = (bf16[8,512,128]{2,1,0:T(8,128)(2,1)S(1)}, f32[8,512,128]{2,1,0:T(8,128)S(1)}, f32[8,512,128]{2,1,0:T(8,128)S(1)}) custom-call(bf16[512,8,128]{2,1,0:T(8,128)(2,1)S(1)} %copy-done, bf16[512,8,128]{2,1,0:T(8,128)(2,1)S(1)} %copy-done.1, f32[8,128]{1,0:T(8,128)S(1)} %copy-done.6, bf16[8,512,128]{2,1,0:T(8,128)(2,1)S(1)} %get-tuple-element.77.kh_ref, ...), custom_call_target="tpu_custom_call" | custom-call | flops 1073741824 | bytes 9441280 | tf_op jit(solution)/shard_map/pallas_call | solution.py:49
  36.6 0.0 collective-permute-done.2.t3_ref
  36.7 0.0 collective-permute-done.1.t2_ref
  36.7 0.0 collective-permute-done.t1_ref
  36.7 0.0 collective-permute-done.3.kv1
  36.7 0.1 shard_map.122
  36.7 13.6 %all_to_all.26.pre_ref = bf16[8,128,128]{2,1,0:T(8,128)(2,1)S(1)} all-to-all(bf16[8,128,128]{2,1,0:T(8,128)(2,1)S(1)} %shard_map.122), channel_id=1, replica_groups=mesh['y'=4,'z'=8,'x'=4,'core'=2] {'z'}, dimensions={0} | all-to-all | bytes 524288 | tf_op jit(solution)/shard_map/all_to_all | solution.py:378
  50.4 2.4 %collective-permute-start.4 = (bf16[2,512,128]{2,1,0:T(8,128)(2,1)S(1)}, bf16[2,512,128]{2,1,0:T(8,128)(2,1)S(1)}, u32[]{:S(2)}, u32[]{:S(2)}) collective-permute-start(bf16[2,512,128]{2,1,0:T(8,128)(2,1)S(1)} %collective-permute-done.3.kv1), channel_id=1, source_target_pairs={{0,8},{8,16},{16,24},{24,32},{32,40},{40,48},{48,56},{56,64},{64,7... | collective-permute-start | bytes 786440 | tf_op jit(solution)/shard_map/ppermute | solution.py:396
  52.8 1.2 shard_map.123
  54.0 9.6 %all_to_all.27.g_ref = f32[8,2,512]{2,1,0:T(2,128)S(1)} all-to-all(f32[8,2,512]{2,1,0:T(2,128)S(1)} %get-tuple-element.88), channel_id=1, replica_groups=mesh['y'=4,'z'=8,'x'=4,'core'=2] {'x','core'}, dimensions={0} | all-to-all | bytes 65536 | tf_op jit(solution)/shard_map/all_to_all | solution.py:435
  63.5 0.0 collective-permute-done.4.kv2
  63.5 1.5 %shard_map.124 = (bf16[8,512,128]{2,1,0:T(8,128)(2,1)S(1)}, bf16[8,128,128]{2,1,0:T(8,128)(2,1)S(1)}, f32[512,128]{1,0:T(8,128)S(1)}) custom-call(f32[8,2,512]{2,1,0:T(2,128)S(1)} %all_to_all.27.g_ref, f32[8,512,128]{2,1,0:T(8,128)S(1)} %get-tuple-element.103.att_ref, f32[8,512,128]{2,1,0:T(8,128)S(1)} %get-tuple-element.82.gh_ref, ...), custom_call_target="tpu_custom_call" | custom-call | flops 134217728 | bytes 6848512 | tf_op jit(solution)/shard_map/pallas_call | solution.py:49
  65.1 18.6 %all_to_all.28.recv_ref = bf16[8,128,128]{2,1,0:T(8,128)(2,1)S(1)} all-to-all(bf16[8,128,128]{2,1,0:T(8,128)(2,1)S(1)} %get-tuple-element.92), channel_id=1, replica_groups=mesh['y'=4,'z'=8,'x'=4,'core'=2] {'z'}, dimensions={0} | all-to-all | bytes 524288 | tf_op jit(solution)/shard_map/all_to_all | solution.py:378
  83.7 0.7 collective-permute-start.7
  84.4 1.9 %collective-permute-start.6 = (bf16[128,128]{1,0:T(8,128)(2,1)S(1)}, bf16[128,128]{1,0:T(8,128)(2,1)S(1)}, u32[]{:S(2)}, u32[]{:S(2)}) collective-permute-start(bf16[128,128]{1,0:T(8,128)(2,1)S(1)} %shard_map.125), channel_id=1, source_target_pairs={{64,0},{128,64},{192,128},{65,1},{129,65},{193,129},{66,2},{130,66... | collective-permute-start | bytes 98312 | tf_op jit(solution)/shard_map/ppermute | solution.py:367
  86.3 1.3 collective-permute-start.5
  87.6 2.7 %collective-permute-start.8 = (bf16[2,512,128]{2,1,0:T(8,128)(2,1)S(1)}, bf16[2,512,128]{2,1,0:T(8,128)(2,1)S(1)}, u32[]{:S(2)}, u32[]{:S(2)}) collective-permute-start(bf16[2,512,128]{2,1,0:T(8,128)(2,1)S(1)} %collective-permute-done.4.kv2), channel_id=1, source_target_pairs={{0,8},{8,16},{16,24},{24,32},{32,40},{40,48},{48,56},{56,64},{64,7... | collective-permute-start | bytes 786440 | tf_op jit(solution)/shard_map/ppermute | solution.py:396
  90.2 3.0 %shard_map.127 = bf16[512,8,128]{2,1,0:T(8,128)(2,1)} custom-call(bf16[8,512,128]{2,1,0:T(8,128)(2,1)S(1)} %get-tuple-element.77.kh_ref, bf16[8,512,128]{2,1,0:T(8,128)(2,1)S(1)} %get-tuple-element.78.vh_ref, bf16[8,512,128]{2,1,0:T(8,128)(2,1)S(1)} %get-tuple-element.108.da_ref, bf16[8,128,128]{2,1,0:T(8,128)(2,1)S(1)} %all_to_all.26.pre_ref), custom_call_target="tpu_custom_call" | custom-call | flops 1073741824 | bytes 4456448 | tf_op jit(solution)/shard_map/pallas_call | solution.py:49
  93.3 0.0 copy-start.7
  93.3 4.3 %shard_map.128 = (f32[8,512,128]{2,1,0:T(8,128)S(1)}, f32[8,512,128]{2,1,0:T(8,128)S(1)}) custom-call(bf16[8,512,128]{2,1,0:T(8,128)(2,1)S(1)} %get-tuple-element.81.qh_ref, bf16[8,512,128]{2,1,0:T(8,128)(2,1)S(1)} %get-tuple-element.77.kh_ref, bf16[8,512,128]{2,1,0:T(8,128)(2,1)S(1)} %get-tuple-element.78.vh_ref, ...), custom_call_target="tpu_custom_call" | custom-call | flops 2147483648 | bytes 8388608 | tf_op jit(solution)/shard_map/pallas_call | solution.py:49
  97.5 0.4 collective-permute-done.8.kv3
  98.0 0.0 copy-done.7
  98.0 14.7 %shard_map.126 = (bf16[512,8,128]{2,1,0:T(8,128)(2,1)}, bf16[512,8,128]{2,1,0:T(8,128)(2,1)}) custom-call(s32[1]{0:T(128)} %bitcast.pos_ref, f32[8,512,128]{2,1,0:T(8,128)S(1)} %get-tuple-element.103.att_ref, f32[512,128]{1,0:T(8,128)S(1)} %get-tuple-element.104.inv_ref, f32[8,128]{1,0:T(8,128)S(1)} %copy-done.6, bf16[512,8,128]{2,1,0:T(8,128)(2,1)S(1)} %copy-done.7, ...), custom_call_target="tpu_custom_call" | custom-call | flops 4294967296 | bytes 6557700 | tf_op jit(solution)/shard_map/pallas_call | solution.py:49
  112.7 0.0 collective-permute-done.7.t3_ref
  112.7 0.0 collective-permute-done.6.t2_ref
  112.7 0.0 collective-permute-done.5.t1_ref
  112.7 0.1 shard_map.129
  112.8 15.3 %all_to_all.29.suf_ref = bf16[8,128,128]{2,1,0:T(8,128)(2,1)S(1)} all-to-all(bf16[8,128,128]{2,1,0:T(8,128)(2,1)S(1)} %shard_map.129), channel_id=1, replica_groups=mesh['y'=4,'z'=8,'x'=4,'core'=2] {'z'}, dimensions={0} | all-to-all | bytes 524288 | tf_op jit(solution)/shard_map/all_to_all | solution.py:378
  128.1 2.5 %shard_map.130 = (bf16[512,8,128]{2,1,0:T(8,128)(2,1)}, bf16[512,8,128]{2,1,0:T(8,128)(2,1)}) custom-call(bf16[8,512,128]{2,1,0:T(8,128)(2,1)S(1)} %get-tuple-element.77.kh_ref, bf16[8,512,128]{2,1,0:T(8,128)(2,1)S(1)} %get-tuple-element.78.vh_ref, f32[8,512,128]{2,1,0:T(8,128)S(1)} %get-tuple-element.113.pk_ref, ...), custom_call_target="tpu_custom_call" | custom-call | flops 268435456 | bytes 8650752 | tf_op jit(solution)/shard_map/pallas_call | solution.py:49
  (1 shorter events, 0.0 us)
Async XLA Ops:
  0.6 33.4 %copy-start.1 = (bf16[512,8,128]{2,1,0:T(8,128)(2,1)S(1)}, bf16[512,8,128]{2,1,0:T(8,128)(2,1)}, u32[]{:S(2)}) copy-start(bf16[512,8,128]{2,1,0:T(8,128)(2,1)} %c_ref) | copy-start | bytes 3145732
  0.6 33.4 %copy-start = (bf16[512,8,128]{2,1,0:T(8,128)(2,1)S(1)}, bf16[512,8,128]{2,1,0:T(8,128)(2,1)}, u32[]{:S(2)}) copy-start(bf16[512,8,128]{2,1,0:T(8,128)(2,1)} %q_ref) | copy-start | bytes 3145732
  0.7 1.4 %copy-start.2 = (bf16[512,8,128]{2,1,0:T(8,128)(2,1)S(1)}, bf16[512,8,128]{2,1,0:T(8,128)(2,1)}, u32[]{:S(2)}) copy-start(bf16[512,8,128]{2,1,0:T(8,128)(2,1)} %k_ref) | copy-start | bytes 3145732
  2.0 1.2 copy-start.3
  3.3 21.4 %copy-start.4 = (bf16[512,1,128]{2,0,1:T(8,128)(2,1)S(1)}, bf16[512,1,128]{2,0,1:T(8,128)(2,1)}, u32[]{:S(2)}) copy-start(bf16[512,1,128]{2,0,1:T(8,128)(2,1)} %param.14) | copy-start | bytes 393220
  3.3 21.4 %copy-start.5 = (bf16[512,1,128]{2,0,1:T(8,128)(2,1)S(1)}, bf16[512,1,128]{2,0,1:T(8,128)(2,1)}, u32[]{:S(2)}) copy-start(bf16[512,1,128]{2,0,1:T(8,128)(2,1)} %param.15) | copy-start | bytes 393220
  3.3 30.8 %copy-start.6 = (f32[8,128]{1,0:T(8,128)S(1)}, f32[8,128]{1,0:T(8,128)}, u32[]{:S(2)}) copy-start(f32[8,128]{1,0:T(8,128)} %gain_ref.3) | copy-start | bytes 12292
  24.7 11.9 %collective-permute-start.3 = (bf16[2,512,128]{2,1,0:T(8,128)(2,1)S(1)}, bf16[2,512,128]{2,1,0:T(8,128)(2,1)S(1)}, u32[]{:S(2)}, u32[]{:S(2)}) collective-permute-start(bf16[2,512,128]{2,1,0:T(8,128)(2,1)S(1)} %get-tuple-element.74.kv0), channel_id=1, source_target_pairs={{0,8},{8,16},{16,24},{24,32},{32,40},{40,48},{48,56},{56,64},{64,7... | collective-permute-start | bytes 786440 | tf_op jit(solution)/shard_map/ppermute | solution.py:396
  27.2 9.4 %collective-permute-start.2 = (bf16[128,128]{1,0:T(8,128)(2,1)S(1)}, bf16[128,128]{1,0:T(8,128)(2,1)S(1)}, u32[]{:S(2)}, u32[]{:S(2)}) collective-permute-start(bf16[128,128]{1,0:T(8,128)(2,1)S(1)} %get-tuple-element.73), channel_id=1, source_target_pairs={{0,192},{1,193},{2,194},{3,195},{4,196},{5,197},{6,198},{7,199},{8... | collective-permute-start | bytes 98312 | tf_op jit(solution)/shard_map/ppermute | solution.py:367
  27.9 8.8 %collective-permute-start.1 = (bf16[128,128]{1,0:T(8,128)(2,1)S(1)}, bf16[128,128]{1,0:T(8,128)(2,1)S(1)}, u32[]{:S(2)}, u32[]{:S(2)}) collective-permute-start(bf16[128,128]{1,0:T(8,128)(2,1)S(1)} %get-tuple-element.73), channel_id=1, source_target_pairs={{0,64},{64,128},{128,192},{1,65},{65,129},{129,193},{2,66},{66,130... | collective-permute-start | bytes 98312 | tf_op jit(solution)/shard_map/ppermute | solution.py:367
  31.4 5.3 %collective-permute-start = (bf16[128,128]{1,0:T(8,128)(2,1)S(1)}, bf16[128,128]{1,0:T(8,128)(2,1)S(1)}, u32[]{:S(2)}, u32[]{:S(2)}) collective-permute-start(bf16[128,128]{1,0:T(8,128)(2,1)S(1)} %get-tuple-element.73), channel_id=1, source_target_pairs={{0,128},{64,192},{1,129},{65,193},{2,130},{66,194},{3,131},{67,195... | collective-permute-start | bytes 98312 | tf_op jit(solution)/shard_map/ppermute | solution.py:367
  50.4 13.2 %collective-permute-start.4 = (bf16[2,512,128]{2,1,0:T(8,128)(2,1)S(1)}, bf16[2,512,128]{2,1,0:T(8,128)(2,1)S(1)}, u32[]{:S(2)}, u32[]{:S(2)}) collective-permute-start(bf16[2,512,128]{2,1,0:T(8,128)(2,1)S(1)} %collective-permute-done.3.kv1), channel_id=1, source_target_pairs={{0,8},{8,16},{16,24},{24,32},{32,40},{40,48},{48,56},{56,64},{64,7... | collective-permute-start | bytes 786440 | tf_op jit(solution)/shard_map/ppermute | solution.py:396
  83.7 29.0 %collective-permute-start.7 = (bf16[128,128]{1,0:T(8,128)(2,1)S(1)}, bf16[128,128]{1,0:T(8,128)(2,1)S(1)}, u32[]{:S(2)}, u32[]{:S(2)}) collective-permute-start(bf16[128,128]{1,0:T(8,128)(2,1)S(1)} %shard_map.125), channel_id=1, source_target_pairs={{192,0},{193,1},{194,2},{195,3},{196,4},{197,5},{198,6},{199,7},{2... | collective-permute-start | bytes 98312 | tf_op jit(solution)/shard_map/ppermute | solution.py:367
  84.4 28.4 %collective-permute-start.6 = (bf16[128,128]{1,0:T(8,128)(2,1)S(1)}, bf16[128,128]{1,0:T(8,128)(2,1)S(1)}, u32[]{:S(2)}, u32[]{:S(2)}) collective-permute-start(bf16[128,128]{1,0:T(8,128)(2,1)S(1)} %shard_map.125), channel_id=1, source_target_pairs={{64,0},{128,64},{192,128},{65,1},{129,65},{193,129},{66,2},{130,66... | collective-permute-start | bytes 98312 | tf_op jit(solution)/shard_map/ppermute | solution.py:367
  86.3 26.4 %collective-permute-start.5 = (bf16[128,128]{1,0:T(8,128)(2,1)S(1)}, bf16[128,128]{1,0:T(8,128)(2,1)S(1)}, u32[]{:S(2)}, u32[]{:S(2)}) collective-permute-start(bf16[128,128]{1,0:T(8,128)(2,1)S(1)} %shard_map.125), channel_id=1, source_target_pairs={{128,0},{192,64},{129,1},{193,65},{130,2},{194,66},{131,3},{195,67... | collective-permute-start | bytes 98312 | tf_op jit(solution)/shard_map/ppermute | solution.py:367
  87.6 10.4 %collective-permute-start.8 = (bf16[2,512,128]{2,1,0:T(8,128)(2,1)S(1)}, bf16[2,512,128]{2,1,0:T(8,128)(2,1)S(1)}, u32[]{:S(2)}, u32[]{:S(2)}) collective-permute-start(bf16[2,512,128]{2,1,0:T(8,128)(2,1)S(1)} %collective-permute-done.4.kv2), channel_id=1, source_target_pairs={{0,8},{8,16},{16,24},{24,32},{32,40},{40,48},{48,56},{56,64},{64,7... | collective-permute-start | bytes 786440 | tf_op jit(solution)/shard_map/ppermute | solution.py:396
  93.3 4.7 %copy-start.7 = (bf16[512,8,128]{2,1,0:T(8,128)(2,1)S(1)}, bf16[512,8,128]{2,1,0:T(8,128)(2,1)}, u32[]{:S(2)}) copy-start(bf16[512,8,128]{2,1,0:T(8,128)(2,1)} %q2_ref.1) | copy-start | bytes 3145732
where the time goes:
time: 132 us; the launch traced here: 131 us
  blocking collectives  77.2 us (58%)
  Pallas kernels  31.2 us (24%)
  starting transfers between devices  18.2 us (14%)
  local copies, waits for them, and re-layouts  2.61 us (2%)
    all_to_all x4, blocking collectives, spread(): return lax.all_to_all(x, 'z', 0, 0, tiled=True)  67.6 us
    pallas_call x12, Pallas kernels, call(): pl.pallas_call(kernel, out_shape=out_shapes, in_specs=specs, out_specs=[p...  31.2 us
    ppermute x6, starting transfers between devices, other_rows(): got.append(lax.ppermute(total, 'y', pairs))  10.7 us
    all_to_all x1, blocking collectives, local(): gathered = lax.all_to_all(part, HEADS, 0, 0, tiled=True)  9.56 us
    ppermute x3, starting transfers between devices, onward(): return lax.ppermute(x, CTX, [(i, i + 1) for i in range(ring - 1)])  7.57 us
  transfers between devices with their start and end apart: 9, of which 1 were waited for; matrix products, arithmetic and copies ran while one was open for 0% of the time, Pallas kernels for 20%

commit v1 on v0

--- a/solution.py
+++ b/solution.py
@@ -332,13 +332,18 @@
         copy.wait()
 
 
-def scan_kernel(back, recv_ref, t1_ref, t2_ref, t3_ref, out_ref):
+def scan_kernel(back, recv_ref, *refs):
+    *others, out_ref = refs
     count = recv_ref.shape[0]
-    running = t1_ref[...].astype(f32) + t2_ref[...].astype(f32) + t3_ref[...].astype(f32)
-    order = range(count - 1, -1, -1) if back else range(count)
+    running = sum(other[...].astype(f32) for other in others)
+    order = range(count) if back else range(count - 1, -1, -1)
     for i in order:
         out_ref[i] = running.astype(bf16)
         running = running + recv_ref[i].astype(f32)
+
+
+def pair_kernel(own_ref, other_ref, out_ref):
+    out_ref[...] = (own_ref[...].astype(f32) + other_ref[...].astype(f32)).astype(bf16)
 
 
 def total_kernel(recv_ref, *refs):
@@ -359,13 +364,13 @@
     return call(total_kernel, [shape(pieces.shape[1:], bf16)], [pieces])[0]
 
 
-def other_rows(total, back):
+def from_row(x, d, back):
     rows = lax.axis_size("y")
-    got = []
-    for d in (2, 1, 3):
-        pairs = [(i + d, i) if back else (i, i + d) for i in range(rows - d)]
-        got.append(lax.ppermute(total, "y", pairs))
-    return got
+    return lax.ppermute(x, "y", [(i + d, i) if back else (i, i + d) for i in range(rows - d)])
+
+
+def pair_total(own, other):
+    return call(pair_kernel, [shape(own.shape, bf16)], [own, other])[0]
 
 
 def scanned(pieces, totals, back):
@@ -375,7 +380,8 @@
 
 
 def spread(x):
-    return lax.all_to_all(x, "z", 0, 0, tiled=True)
+    members = list(range(lax.axis_size("z")))[::-1]
+    return lax.all_to_all(x, "z", 0, 0, tiled=True, axis_index_groups=[members])
 
 
 def local(query, key, value, gain, cotangent, query2, key2, softmax_values):
@@ -413,7 +419,7 @@
         [pieces, key2[:, 0], softmax_values[:, 0]],
     )
     total, kh, vh = tied(total, kh, vh)
-    totals = other_rows(total, False)
+    totals = [from_row(total, d, False) for d in (2, 1, 3)]
     kv1 = onward(kv0)
     qh, gh, loc = call(
         local_kernel,
@@ -442,9 +448,22 @@
         unit // 4,
     )
     back_pieces, att, da, inverse, kv2 = tied(spread(block_grad), att, da, inverse, kv2)
-    back_total, att, da, inverse, kv2 = tied(row_total(back_pieces), att, da, inverse, kv2)
     kv3 = onward(kv2)
-    back_totals = other_rows(back_total, True)
+    (gq,) = call(
+        query_gradient_kernel,
+        [shape(query.shape, bf16)],
+        [kh, vh, da, prefix],
+        [flat_buffer, token_buffer, sems(4)],
+        2 * unit,
+        hbm_out=(0,),
+    )
+    back_total, gq, da = tied(row_total(back_pieces), gq, da)
+    back_near = from_row(back_total, 1, True)
+    pk, pv = call(
+        key_value_local_kernel, [shape(head_major, f32)] * 2, [qh, kh, vh, da], (), 4 * unit
+    )
+    back_near, pk, pv, att = tied(back_near, pk, pv, att)
+    back_far = from_row(pair_total(back_total, back_near), 2, True)
     normed, attended = call(
         softmax_kernel,
         [shape(query.shape, bf16), shape(query.shape, bf16)],
@@ -461,21 +480,8 @@
         vmem=40,
         hbm_out=(0, 1),
     )
-    (gq,) = call(
-        query_gradient_kernel,
-        [shape(query.shape, bf16)],
-        [kh, vh, da, prefix],
-        [flat_buffer, token_buffer, sems(4)],
-        2 * unit,
-        hbm_out=(0,),
-    )
-    pk, pv = call(
-        key_value_local_kernel, [shape(head_major, f32)] * 2, [qh, kh, vh, da], (), 4 * unit
-    )
-    *back_totals, normed, attended, gq, pk, pv = tied(
-        *back_totals, normed, attended, gq, pk, pv
-    )
-    suffix = spread(scanned(back_pieces, back_totals, True))
+    back_far, normed, attended, gq = tied(back_far, normed, attended, gq)
+    suffix = spread(scanned(back_pieces, [back_near, back_far], True))
     gk, gv = call(
         finish_kernel,
         [shape(query.shape, bf16)] * 2,

time: 132 us -> 129 us (0.977)
  blocking collectives: 77.2 us -> 68.2 us
  starting transfers between devices: 18.2 us -> 23.4 us
    all_to_all x4, blocking collectives: 67.6 us -> 58.7 us  [spread(): return lax.all_to_all(x, 'z', 0, 0, tiled=True, axis_index_groups=[members])]
    ppermute x3, starting transfers between devices: 7.57 us -> 11.3 us  [onward(): return lax.ppermute(x, CTX, [(i, i + 1) for i in range(ring - 1)])]
    ppermute x6 -> x5, starting transfers between devices: 10.7 us -> 12.1 us  [from_row(): lax.ppermute(x, 'y', [(i + d, i) if back else (i, i + d) for i in range(r...]
    pallas_call x12 -> x13, Pallas kernels: 31.2 us -> 31.2 us  [call(): pl.pallas_call(kernel, out_shape=out_shapes, in_specs=specs, out_specs=[p...]
  transfers between devices with their start and end apart: 9 -> 8, of which waited for: 1 -> 0; matrix products, arithmetic and copies ran while one was open for 0% -> 0% of each run, Pallas kernels for 20% -> 20%
where the time goes in v1:
time: 129 us; the launch traced here: 127 us
  blocking collectives  68.2 us (53%)
  Pallas kernels  31.2 us (24%)
  starting transfers between devices  23.4 us (18%)
  local copies, waits for them, and re-layouts  2.61 us (2%)
    all_to_all x4, blocking collectives, spread(): return lax.all_to_all(x, 'z', 0, 0, tiled=True, axis_index_groups=[members])  58.7 us
    pallas_call x13, Pallas kernels, call(): pl.pallas_call(kernel, out_shape=out_shapes, in_specs=specs, out_specs=[p...  31.2 us
    ppermute x5, starting transfers between devices, from_row(): lax.ppermute(x, 'y', [(i + d, i) if back else (i, i + d) for i in range(r...  12.1 us
    ppermute x3, starting transfers between devices, onward(): return lax.ppermute(x, CTX, [(i, i + 1) for i in range(ring - 1)])  11.3 us
    all_to_all x1, blocking collectives, local(): gathered = lax.all_to_all(part, HEADS, 0, 0, tiled=True)  9.56 us
    unnamed x16, local copies, waits for them, and re-layouts  2.61 us
  transfers between devices with their start and end apart: 8, of which 0 were waited for; matrix products, arithmetic and copies ran while one was open for 0% of the time, Pallas kernels for 20%

profile of v1, /device:TPU:8, one launch (start us, length us, event | category | flops | bytes accessed | tf_op | source)
XLA Modules:
  0.0 126.6 jit_solution(15822409087077512489)
XLA Ops:
  0.6 0.0 copy-start.1
  0.6 0.0 copy-start
  0.7 0.0 copy-start.2
  0.7 1.4 %copy-done.2 = bf16[512,8,128]{2,1,0:T(8,128)(2,1)S(1)} copy-done((bf16[512,8,128]{2,1,0:T(8,128)(2,1)S(1)}, bf16[512,8,128]{2,1,0:T(8,128)(2,1)}, u32[]{:S(2)}) %copy-start.2) | copy-done | bytes 1048600
  2.0 0.0 copy-start.3
  2.0 1.2 copy-done.3
  3.3 0.0 copy-start.4
  3.3 0.0 copy-start.5
  3.3 0.0 copy-start.6
  3.3 1.3 shard_map.119
  4.5 15.9 %all_to_all.25.recv_ref = bf16[8,128,128]{2,1,0:T(8,128)(2,1)S(1)} all-to-all(bf16[8,128,128]{2,1,0:T(8,128)(2,1)S(1)} %get-tuple-element.64), channel_id=1, replica_groups={{56,48,40,32,24,16,8,0},{57,49,41,33,25,17,9,1},{58,50,42,34,26,18,10,2..., dimensions={0} | all-to-all | bytes 524288 | tf_op jit(solution)/shard_map/all_to_all | solution.py:384
  20.5 0.0 copy-done.4
  20.5 0.0 copy-done.5
  20.5 0.1 shard_map.120
  20.5 4.3 %collective-permute-start.3 = (bf16[2,512,128]{2,1,0:T(8,128)(2,1)S(1)}, bf16[2,512,128]{2,1,0:T(8,128)(2,1)S(1)}, u32[]{:S(2)}, u32[]{:S(2)}) collective-permute-start(bf16[2,512,128]{2,1,0:T(8,128)(2,1)S(1)} %get-tuple-element.72.kv0), channel_id=1, source_target_pairs={{0,8},{8,16},{16,24},{24,32},{32,40},{40,48},{48,56},{56,64},{64,7... | collective-permute-start | bytes 786440 | tf_op jit(solution)/shard_map/ppermute | solution.py:402
  24.9 0.7 collective-permute-start.2
  25.5 3.5 %collective-permute-start.1 = (bf16[128,128]{1,0:T(8,128)(2,1)S(1)}, bf16[128,128]{1,0:T(8,128)(2,1)S(1)}, u32[]{:S(2)}, u32[]{:S(2)}) collective-permute-start(bf16[128,128]{1,0:T(8,128)(2,1)S(1)} %get-tuple-element.71), channel_id=1, source_target_pairs={{0,64},{64,128},{128,192},{1,65},{65,129},{129,193},{2,66},{66,130... | collective-permute-start | bytes 98312 | tf_op jit(solution)/shard_map/ppermute | solution.py:369
  29.0 2.6 %collective-permute-start = (bf16[128,128]{1,0:T(8,128)(2,1)S(1)}, bf16[128,128]{1,0:T(8,128)(2,1)S(1)}, u32[]{:S(2)}, u32[]{:S(2)}) collective-permute-start(bf16[128,128]{1,0:T(8,128)(2,1)S(1)} %get-tuple-element.71), channel_id=1, source_target_pairs={{0,128},{64,192},{1,129},{65,193},{2,130},{66,194},{3,131},{67,195... | collective-permute-start | bytes 98312 | tf_op jit(solution)/shard_map/ppermute | solution.py:369
  31.7 0.0 copy-done.1
  31.7 0.0 copy-done
  31.7 0.0 copy-done.6
  31.7 2.6 %shard_map.121 = (bf16[8,512,128]{2,1,0:T(8,128)(2,1)S(1)}, f32[8,512,128]{2,1,0:T(8,128)S(1)}, f32[8,512,128]{2,1,0:T(8,128)S(1)}) custom-call(bf16[512,8,128]{2,1,0:T(8,128)(2,1)S(1)} %copy-done, bf16[512,8,128]{2,1,0:T(8,128)(2,1)S(1)} %copy-done.1, f32[8,128]{1,0:T(8,128)S(1)} %copy-done.6, bf16[8,512,128]{2,1,0:T(8,128)(2,1)S(1)} %get-tuple-element.75.kh_ref, ...), custom_call_target="tpu_custom_call" | custom-call | flops 1073741824 | bytes 9441280 | tf_op jit(solution)/shard_map/pallas_call | solution.py:49
  34.3 0.0 collective-permute-done.2.refs_2_
  34.3 0.0 collective-permute-done.1.refs_1_
  34.3 0.0 collective-permute-done.refs_0_
  34.3 0.0 collective-permute-done.3.kv1
  34.3 0.1 shard_map.122
  34.4 13.9 %all_to_all.26.pre_ref = bf16[8,128,128]{2,1,0:T(8,128)(2,1)S(1)} all-to-all(bf16[8,128,128]{2,1,0:T(8,128)(2,1)S(1)} %shard_map.122), channel_id=1, replica_groups={{56,48,40,32,24,16,8,0},{57,49,41,33,25,17,9,1},{58,50,42,34,26,18,10,2..., dimensions={0} | all-to-all | bytes 524288 | tf_op jit(solution)/shard_map/all_to_all | solution.py:384
  48.3 2.6 %collective-permute-start.4 = (bf16[2,512,128]{2,1,0:T(8,128)(2,1)S(1)}, bf16[2,512,128]{2,1,0:T(8,128)(2,1)S(1)}, u32[]{:S(2)}, u32[]{:S(2)}) collective-permute-start(bf16[2,512,128]{2,1,0:T(8,128)(2,1)S(1)} %collective-permute-done.3.kv1), channel_id=1, source_target_pairs={{0,8},{8,16},{16,24},{24,32},{32,40},{40,48},{48,56},{56,64},{64,7... | collective-permute-start | bytes 786440 | tf_op jit(solution)/shard_map/ppermute | solution.py:402
  50.9 1.2 shard_map.123
  52.1 9.6 %all_to_all.27.g_ref = f32[8,2,512]{2,1,0:T(2,128)S(1)} all-to-all(f32[8,2,512]{2,1,0:T(2,128)S(1)} %get-tuple-element.86), channel_id=1, replica_groups=mesh['y'=4,'z'=8,'x'=4,'core'=2] {'x','core'}, dimensions={0} | all-to-all | bytes 65536 | tf_op jit(solution)/shard_map/all_to_all | solution.py:441
  61.6 0.0 collective-permute-done.4.kv2
  61.6 1.5 %shard_map.124 = (bf16[8,512,128]{2,1,0:T(8,128)(2,1)S(1)}, bf16[8,128,128]{2,1,0:T(8,128)(2,1)S(1)}, f32[512,128]{1,0:T(8,128)S(1)}) custom-call(f32[8,2,512]{2,1,0:T(2,128)S(1)} %all_to_all.27.g_ref, f32[8,512,128]{2,1,0:T(8,128)S(1)} %get-tuple-element.103.att_ref, f32[8,512,128]{2,1,0:T(8,128)S(1)} %get-tuple-element.80.gh_ref, ...), custom_call_target="tpu_custom_call" | custom-call | flops 134217728 | bytes 6848512 | tf_op jit(solution)/shard_map/pallas_call | solution.py:49
  63.2 15.0 %all_to_all.28.recv_ref = bf16[8,128,128]{2,1,0:T(8,128)(2,1)S(1)} all-to-all(bf16[8,128,128]{2,1,0:T(8,128)(2,1)S(1)} %get-tuple-element.90), channel_id=1, replica_groups={{56,48,40,32,24,16,8,0},{57,49,41,33,25,17,9,1},{58,50,42,34,26,18,10,2..., dimensions={0} | all-to-all | bytes 524288 | tf_op jit(solution)/shard_map/all_to_all | solution.py:384
  78.2 4.4 %collective-permute-start.7 = (bf16[2,512,128]{2,1,0:T(8,128)(2,1)S(1)}, bf16[2,512,128]{2,1,0:T(8,128)(2,1)S(1)}, u32[]{:S(2)}, u32[]{:S(2)}) collective-permute-start(bf16[2,512,128]{2,1,0:T(8,128)(2,1)S(1)} %collective-permute-done.4.kv2), channel_id=1, source_target_pairs={{0,8},{8,16},{16,24},{24,32},{32,40},{40,48},{48,56},{56,64},{64,7... | collective-permute-start | bytes 786440 | tf_op jit(solution)/shard_map/ppermute | solution.py:402
  82.6 3.0 %shard_map.126 = bf16[512,8,128]{2,1,0:T(8,128)(2,1)} custom-call(bf16[8,512,128]{2,1,0:T(8,128)(2,1)S(1)} %get-tuple-element.75.kh_ref, bf16[8,512,128]{2,1,0:T(8,128)(2,1)S(1)} %get-tuple-element.76.vh_ref, bf16[8,512,128]{2,1,0:T(8,128)(2,1)S(1)} %get-tuple-element.97.da_ref, bf16[8,128,128]{2,1,0:T(8,128)(2,1)S(1)} %all_to_all.26.pre_ref), custom_call_target="tpu_custom_call" | custom-call | flops 1073741824 | bytes 4456448 | tf_op jit(solution)/shard_map/pallas_call | solution.py:49
  85.6 0.0 copy-start.7
  85.6 4.0 %collective-permute-start.5 = (bf16[128,128]{1,0:T(8,128)(2,1)S(1)}, bf16[128,128]{1,0:T(8,128)(2,1)S(1)}, u32[]{:S(2)}, u32[]{:S(2)}) collective-permute-start(bf16[128,128]{1,0:T(8,128)(2,1)S(1)} %shard_map.125.own_ref), channel_id=1, source_target_pairs={{64,0},{128,64},{192,128},{65,1},{129,65},{193,129},{66,2},{130,66... | collective-permute-start | bytes 98312 | tf_op jit(solution)/shard_map/ppermute | solution.py:369
  89.6 4.3 %shard_map.127 = (f32[8,512,128]{2,1,0:T(8,128)S(1)}, f32[8,512,128]{2,1,0:T(8,128)S(1)}) custom-call(bf16[8,512,128]{2,1,0:T(8,128)(2,1)S(1)} %get-tuple-element.79.qh_ref, bf16[8,512,128]{2,1,0:T(8,128)(2,1)S(1)} %get-tuple-element.75.kh_ref, bf16[8,512,128]{2,1,0:T(8,128)(2,1)S(1)} %get-tuple-element.76.vh_ref, ...), custom_call_target="tpu_custom_call" | custom-call | flops 2147483648 | bytes 8388608 | tf_op jit(solution)/shard_map/pallas_call | solution.py:49
  93.9 0.0 collective-permute-done.5.other_ref.refs_0_
  93.9 1.3 %collective-permute-start.6 = (bf16[128,128]{1,0:T(8,128)(2,1)S(1)}, bf16[128,128]{1,0:T(8,128)(2,1)S(1)}, u32[]{:S(2)}, u32[]{:S(2)}) collective-permute-start(bf16[128,128]{1,0:T(8,128)(2,1)S(1)} %shard_map.128), channel_id=1, source_target_pairs={{128,0},{192,64},{129,1},{193,65},{130,2},{194,66},{131,3},{195,67... | collective-permute-start | bytes 98312 | tf_op jit(solution)/shard_map/ppermute | solution.py:369
  95.2 0.0 collective-permute-done.7.kv3
  95.2 0.0 copy-done.7
  95.2 14.7 %shard_map.129 = (bf16[512,8,128]{2,1,0:T(8,128)(2,1)}, bf16[512,8,128]{2,1,0:T(8,128)(2,1)}) custom-call(s32[1]{0:T(128)} %bitcast.pos_ref, f32[8,512,128]{2,1,0:T(8,128)S(1)} %get-tuple-element.103.att_ref, f32[512,128]{1,0:T(8,128)S(1)} %get-tuple-element.104.inv_ref, f32[8,128]{1,0:T(8,128)S(1)} %copy-done.6, bf16[512,8,128]{2,1,0:T(8,128)(2,1)S(1)} %copy-done.7, ...), custom_call_target="tpu_custom_call" | custom-call | flops 4294967296 | bytes 6557700 | tf_op jit(solution)/shard_map/pallas_call | solution.py:49
  110.0 0.0 collective-permute-done.6.refs_1_
  110.1 13.9 %all_to_all.29.suf_ref = bf16[8,128,128]{2,1,0:T(8,128)(2,1)S(1)} all-to-all(bf16[8,128,128]{2,1,0:T(8,128)(2,1)S(1)} %shard_map.130), channel_id=1, replica_groups={{56,48,40,32,24,16,8,0},{57,49,41,33,25,17,9,1},{58,50,42,34,26,18,10,2..., dimensions={0} | all-to-all | bytes 524288 | tf_op jit(solution)/shard_map/all_to_all | solution.py:384
  123.9 2.5 %shard_map.131 = (bf16[512,8,128]{2,1,0:T(8,128)(2,1)}, bf16[512,8,128]{2,1,0:T(8,128)(2,1)}) custom-call(bf16[8,512,128]{2,1,0:T(8,128)(2,1)S(1)} %get-tuple-element.75.kh_ref, bf16[8,512,128]{2,1,0:T(8,128)(2,1)S(1)} %get-tuple-element.76.vh_ref, f32[8,512,128]{2,1,0:T(8,128)S(1)} %get-tuple-element.111.pk_ref, ...), custom_call_target="tpu_custom_call" | custom-call | flops 268435456 | bytes 8650752 | tf_op jit(solution)/shard_map/pallas_call | solution.py:49
  (3 shorter events, 0.1 us)
Async XLA Ops:
  0.6 31.0 %copy-start.1 = (bf16[512,8,128]{2,1,0:T(8,128)(2,1)S(1)}, bf16[512,8,128]{2,1,0:T(8,128)(2,1)}, u32[]{:S(2)}) copy-start(bf16[512,8,128]{2,1,0:T(8,128)(2,1)} %c_ref) | copy-start | bytes 3145732
  0.6 31.0 %copy-start = (bf16[512,8,128]{2,1,0:T(8,128)(2,1)S(1)}, bf16[512,8,128]{2,1,0:T(8,128)(2,1)}, u32[]{:S(2)}) copy-start(bf16[512,8,128]{2,1,0:T(8,128)(2,1)} %q_ref) | copy-start | bytes 3145732
  0.7 1.4 %copy-start.2 = (bf16[512,8,128]{2,1,0:T(8,128)(2,1)S(1)}, bf16[512,8,128]{2,1,0:T(8,128)(2,1)}, u32[]{:S(2)}) copy-start(bf16[512,8,128]{2,1,0:T(8,128)(2,1)} %k_ref) | copy-start | bytes 3145732
  2.0 1.2 copy-start.3
  3.3 17.2 %copy-start.4 = (bf16[512,1,128]{2,0,1:T(8,128)(2,1)S(1)}, bf16[512,1,128]{2,0,1:T(8,128)(2,1)}, u32[]{:S(2)}) copy-start(bf16[512,1,128]{2,0,1:T(8,128)(2,1)} %param.14) | copy-start | bytes 393220
  3.3 17.2 %copy-start.5 = (bf16[512,1,128]{2,0,1:T(8,128)(2,1)S(1)}, bf16[512,1,128]{2,0,1:T(8,128)(2,1)}, u32[]{:S(2)}) copy-start(bf16[512,1,128]{2,0,1:T(8,128)(2,1)} %param.15) | copy-start | bytes 393220
  3.3 28.4 %copy-start.6 = (f32[8,128]{1,0:T(8,128)S(1)}, f32[8,128]{1,0:T(8,128)}, u32[]{:S(2)}) copy-start(f32[8,128]{1,0:T(8,128)} %gain_ref.3) | copy-start | bytes 12292
  20.5 13.8 %collective-permute-start.3 = (bf16[2,512,128]{2,1,0:T(8,128)(2,1)S(1)}, bf16[2,512,128]{2,1,0:T(8,128)(2,1)S(1)}, u32[]{:S(2)}, u32[]{:S(2)}) collective-permute-start(bf16[2,512,128]{2,1,0:T(8,128)(2,1)S(1)} %get-tuple-element.72.kv0), channel_id=1, source_target_pairs={{0,8},{8,16},{16,24},{24,32},{32,40},{40,48},{48,56},{56,64},{64,7... | collective-permute-start | bytes 786440 | tf_op jit(solution)/shard_map/ppermute | solution.py:402
  24.9 9.4 %collective-permute-start.2 = (bf16[128,128]{1,0:T(8,128)(2,1)S(1)}, bf16[128,128]{1,0:T(8,128)(2,1)S(1)}, u32[]{:S(2)}, u32[]{:S(2)}) collective-permute-start(bf16[128,128]{1,0:T(8,128)(2,1)S(1)} %get-tuple-element.71), channel_id=1, source_target_pairs={{0,192},{1,193},{2,194},{3,195},{4,196},{5,197},{6,198},{7,199},{8... | collective-permute-start | bytes 98312 | tf_op jit(solution)/shard_map/ppermute | solution.py:369
  25.5 8.8 %collective-permute-start.1 = (bf16[128,128]{1,0:T(8,128)(2,1)S(1)}, bf16[128,128]{1,0:T(8,128)(2,1)S(1)}, u32[]{:S(2)}, u32[]{:S(2)}) collective-permute-start(bf16[128,128]{1,0:T(8,128)(2,1)S(1)} %get-tuple-element.71), channel_id=1, source_target_pairs={{0,64},{64,128},{128,192},{1,65},{65,129},{129,193},{2,66},{66,130... | collective-permute-start | bytes 98312 | tf_op jit(solution)/shard_map/ppermute | solution.py:369
  29.0 5.3 %collective-permute-start = (bf16[128,128]{1,0:T(8,128)(2,1)S(1)}, bf16[128,128]{1,0:T(8,128)(2,1)S(1)}, u32[]{:S(2)}, u32[]{:S(2)}) collective-permute-start(bf16[128,128]{1,0:T(8,128)(2,1)S(1)} %get-tuple-element.71), channel_id=1, source_target_pairs={{0,128},{64,192},{1,129},{65,193},{2,130},{66,194},{3,131},{67,195... | collective-permute-start | bytes 98312 | tf_op jit(solution)/shard_map/ppermute | solution.py:369
  48.3 13.3 %collective-permute-start.4 = (bf16[2,512,128]{2,1,0:T(8,128)(2,1)S(1)}, bf16[2,512,128]{2,1,0:T(8,128)(2,1)S(1)}, u32[]{:S(2)}, u32[]{:S(2)}) collective-permute-start(bf16[2,512,128]{2,1,0:T(8,128)(2,1)S(1)} %collective-permute-done.3.kv1), channel_id=1, source_target_pairs={{0,8},{8,16},{16,24},{24,32},{32,40},{40,48},{48,56},{56,64},{64,7... | collective-permute-start | bytes 786440 | tf_op jit(solution)/shard_map/ppermute | solution.py:402
  78.2 17.1 %collective-permute-start.7 = (bf16[2,512,128]{2,1,0:T(8,128)(2,1)S(1)}, bf16[2,512,128]{2,1,0:T(8,128)(2,1)S(1)}, u32[]{:S(2)}, u32[]{:S(2)}) collective-permute-start(bf16[2,512,128]{2,1,0:T(8,128)(2,1)S(1)} %collective-permute-done.4.kv2), channel_id=1, source_target_pairs={{0,8},{8,16},{16,24},{24,32},{32,40},{40,48},{48,56},{56,64},{64,7... | collective-permute-start | bytes 786440 | tf_op jit(solution)/shard_map/ppermute | solution.py:402
  85.6 9.6 %copy-start.7 = (bf16[512,8,128]{2,1,0:T(8,128)(2,1)S(1)}, bf16[512,8,128]{2,1,0:T(8,128)(2,1)}, u32[]{:S(2)}) copy-start(bf16[512,8,128]{2,1,0:T(8,128)(2,1)} %q2_ref.1) | copy-start | bytes 3145732
  85.6 8.3 %collective-permute-start.5 = (bf16[128,128]{1,0:T(8,128)(2,1)S(1)}, bf16[128,128]{1,0:T(8,128)(2,1)S(1)}, u32[]{:S(2)}, u32[]{:S(2)}) collective-permute-start(bf16[128,128]{1,0:T(8,128)(2,1)S(1)} %shard_map.125.own_ref), channel_id=1, source_target_pairs={{64,0},{128,64},{192,128},{65,1},{129,65},{193,129},{66,2},{130,66... | collective-permute-start | bytes 98312 | tf_op jit(solution)/shard_map/ppermute | solution.py:369
  93.9 16.1 %collective-permute-start.6 = (bf16[128,128]{1,0:T(8,128)(2,1)S(1)}, bf16[128,128]{1,0:T(8,128)(2,1)S(1)}, u32[]{:S(2)}, u32[]{:S(2)}) collective-permute-start(bf16[128,128]{1,0:T(8,128)(2,1)S(1)} %shard_map.128), channel_id=1, source_target_pairs={{128,0},{192,64},{129,1},{193,65},{130,2},{194,66},{131,3},{195,67... | collective-permute-start | bytes 98312 | tf_op jit(solution)/shard_map/ppermute | solution.py:369

commit v2 on v1

--- a/solution.py
+++ b/solution.py
@@ -156,34 +156,16 @@
         bg_ref[h] = tn(qh_ref[h], d).astype(bf16)
 
 
-def softmax_kernel(
-    pos_ref, att_ref, inv_ref, gain_ref, q2_ref, kv0, kv1, kv2, kv3,
-    norm_hbm, out_hbm, norm, out, scratch, ahead, sems,
-):
-    heads, tokens, width = att_ref.shape
+def softmax_kernel(pos_ref, sq_ref, kv0, kv1, kv2, kv3, out_hbm, out, ahead, sems):
+    tokens, heads, width = out.shape
     kv = (kv0, kv1, kv2, kv3)
-    inverse = inv_ref[...]
-    for h in range(heads):
-        scratch[pl.ds(h, tokens, stride=heads), :] = (
-            gain_ref[h : h + 1, :] * (att_ref[h] * inverse)
-        )
-    norm[...] = scratch[...].astype(bf16).reshape(tokens, heads, width)
-    writes = fetch([(norm, norm_hbm)], sems.at[pl.ds(4, 1)])
-
     scale = LOG2E * HEAD_WIDTH ** (-0.5)
     ones = jnp.ones((tokens, width), bf16)
     quarters = 4
     quarter = tokens // quarters
 
-    def query_rows(chunk, rows):
-        chunk_tokens = rows // heads
-        t0 = pl.multiple_of(chunk * chunk_tokens, chunk_tokens)
-        n = scratch[pl.ds(pl.multiple_of(chunk * rows, rows), rows), :].astype(bf16).astype(f32)
-        q2 = q2_ref[pl.ds(t0, chunk_tokens)].astype(f32).reshape(rows, width)
-        return (q2 + n).astype(bf16)
-
     def scores(chunk, rows, count):
-        q = query_rows(chunk, rows)
+        q = sq_ref[pl.ds(pl.multiple_of(chunk * rows, rows), rows), :]
         row = chunk * rows + lax.broadcasted_iota(jnp.int32, (rows, tokens), 0)
         column = lax.broadcasted_iota(jnp.int32, (rows, tokens), 1)
         own = jnp.where(column <= row // heads, nt(q, kv[0][0]), -1e30)
@@ -250,36 +232,42 @@
     pl.when(have == WINDOW_BLOCKS - 1)(run_ahead)
     for i in range(quarters):
         store(i).wait()
-    writes[0].wait()
-
-
-def query_gradient_kernel(kh_ref, vh_ref, da_ref, pre_ref, gq_hbm, qs, out, sems):
+
+
+def query_gradient_kernel(
+    kh_ref, vh_ref, da_ref, pre_ref, att_ref, inv_ref, gain_ref, q2_ref,
+    gq_hbm, norm_hbm, sq_ref, qs, ns, out, norm, sems,
+):
     heads, tokens, width = kh_ref.shape
     half = tokens // 2
     below = causal_below(half)
     lo, hi = slice(0, half), slice(half, tokens)
-
-    def head(h):
+    inverse = inv_ref[...]
+    for h in range(heads):
         k, v, da = kh_ref[h], vh_ref[h], da_ref[h]
         d00 = jnp.where(below, nt(da[lo], v[lo]), 0.0).astype(bf16)
         d10 = nt(da[hi], v[lo]).astype(bf16)
         d11 = jnp.where(below, nt(da[hi], v[hi]), 0.0).astype(bf16)
         gq = nt(da, pre_ref[h])
+        ns[pl.ds(h, tokens, stride=heads), :] = gain_ref[h : h + 1, :] * (att_ref[h] * inverse)
         qs[pl.ds(h, half, stride=heads), :] = gq[lo] + nn(d00, k[lo])
         qs[pl.ds(half * heads + h, half, stride=heads), :] = (
             gq[hi] + nn(d10, k[lo]) + nn(d11, k[hi])
         )
-
-    each(heads, head)
-    pieces = sems.shape[0]
+    pieces = sems.shape[0] // 2
     rows = tokens // pieces
     copies = []
     for i in range(pieces):
-        part = pl.ds(i * rows, rows)
-        out[part] = (
-            qs[pl.ds(i * rows * heads, rows * heads), :].astype(bf16).reshape(rows, heads, width)
+        part, flat = pl.ds(i * rows, rows), pl.ds(i * rows * heads, rows * heads)
+        out[part] = qs[flat, :].astype(bf16).reshape(rows, heads, width)
+        n = ns[flat, :].astype(bf16)
+        norm[part] = n.reshape(rows, heads, width)
+        copies += fetch(
+            [(out.at[part], gq_hbm.at[part]), (norm.at[part], norm_hbm.at[part])],
+            sems.at[pl.ds(2 * i, 2)],
         )
-        copies += fetch([(out.at[part], gq_hbm.at[part])], sems.at[pl.ds(i, 1)])
+        q2 = q2_ref[part].astype(f32).reshape(rows * heads, width)
+        sq_ref[flat, :] = (q2 + n.astype(f32)).astype(bf16)
     for copy in copies:
         copy.wait()
 
@@ -419,8 +407,8 @@
         [pieces, key2[:, 0], softmax_values[:, 0]],
     )
     total, kh, vh = tied(total, kh, vh)
-    totals = [from_row(total, d, False) for d in (2, 1, 3)]
     kv1 = onward(kv0)
+    totals = [from_row(total, d, False) for d in (1, 3, 2)]
     qh, gh, loc = call(
         local_kernel,
         [shape(head_major, bf16), shape(head_major, f32), shape(head_major, f32)],
@@ -449,36 +437,30 @@
     )
     back_pieces, att, da, inverse, kv2 = tied(spread(block_grad), att, da, inverse, kv2)
     kv3 = onward(kv2)
-    (gq,) = call(
+    gq, normed, sq = call(
         query_gradient_kernel,
-        [shape(query.shape, bf16)],
-        [kh, vh, da, prefix],
-        [flat_buffer, token_buffer, sems(4)],
+        [shape(query.shape, bf16), shape(query.shape, bf16), shape(flat, bf16)],
+        [kh, vh, da, prefix, att, inverse, gain, query2],
+        [flat_buffer, flat_buffer, token_buffer, token_buffer, sems(8)],
         2 * unit,
-        hbm_out=(0,),
+        hbm_out=(0, 1),
     )
     back_total, gq, da = tied(row_total(back_pieces), gq, da)
     back_near = from_row(back_total, 1, True)
     pk, pv = call(
         key_value_local_kernel, [shape(head_major, f32)] * 2, [qh, kh, vh, da], (), 4 * unit
     )
-    back_near, pk, pv, att = tied(back_near, pk, pv, att)
+    back_near, pk, pv, sq = tied(back_near, pk, pv, sq)
     back_far = from_row(pair_total(back_total, back_near), 2, True)
-    normed, attended = call(
+    (attended,) = call(
         softmax_kernel,
-        [shape(query.shape, bf16), shape(query.shape, bf16)],
-        [have, att, inverse, gain, query2, kv0, kv1, kv2, kv3],
-        [
-            token_buffer,
-            token_buffer,
-            flat_buffer,
-            pltpu.VMEM((2, WINDOW_BLOCKS, tokens, tokens), f32),
-            sems(5),
-        ],
+        [shape(query.shape, bf16)],
+        [have, sq, kv0, kv1, kv2, kv3],
+        [token_buffer, pltpu.VMEM((2, WINDOW_BLOCKS, tokens, tokens), f32), sems(4)],
         8 * unit,
         smem_first=True,
         vmem=40,
-        hbm_out=(0, 1),
+        hbm_out=(0,),
     )
     back_far, normed, attended, gq = tied(back_far, normed, attended, gq)
     suffix = spread(scanned(back_pieces, [back_near, back_far], True))

time: 129 us -> 128 us (level)
  no operation moved by 1% of the time
where the time goes in v2:
time: 128 us; the launch traced here: 126 us
  blocking collectives  67.6 us (53%)
  Pallas kernels  31 us (24%)
  starting transfers between devices  23.3 us (18%)
  local copies, waits for them, and re-layouts  2.61 us (2%)
    all_to_all x4, blocking collectives, spread(): return lax.all_to_all(x, 'z', 0, 0, tiled=True, axis_index_groups=[members])  58 us
    pallas_call x13, Pallas kernels, call(): pl.pallas_call(kernel, out_shape=out_shapes, in_specs=specs, out_specs=[p...  31 us
    ppermute x5, starting transfers between devices, from_row(): lax.ppermute(x, 'y', [(i + d, i) if back else (i, i + d) for i in range(r...  12 us
    ppermute x3, starting transfers between devices, onward(): return lax.ppermute(x, CTX, [(i, i + 1) for i in range(ring - 1)])  11.3 us
    all_to_all x1, blocking collectives, local(): gathered = lax.all_to_all(part, HEADS, 0, 0, tiled=True)  9.57 us
    unnamed x16, local copies, waits for them, and re-layouts  2.61 us
  transfers between devices with their start and end apart: 8, of which 0 were waited for; matrix products, arithmetic and copies ran while one was open for 0% of the time, Pallas kernels for 20%

profile of v2, /device:TPU:8, one launch (start us, length us, event | category | flops | bytes accessed | tf_op | source)
XLA Modules:
  0.0 125.6 jit_solution(17697594977302273182)
XLA Ops:
  0.6 0.0 copy-start.1
  0.6 0.0 copy-start
  0.7 0.0 copy-start.2
  0.7 1.4 %copy-done.2 = bf16[512,8,128]{2,1,0:T(8,128)(2,1)S(1)} copy-done((bf16[512,8,128]{2,1,0:T(8,128)(2,1)S(1)}, bf16[512,8,128]{2,1,0:T(8,128)(2,1)}, u32[]{:S(2)}) %copy-start.2) | copy-done | bytes 1048600
  2.0 0.0 copy-start.3
  2.0 1.2 copy-done.3
  3.3 0.0 copy-start.5
  3.3 0.0 copy-start.6
  3.3 0.0 copy-start.7
  3.3 1.3 %shard_map.119 = (bf16[8,512,128]{2,1,0:T(8,128)(2,1)S(1)}, bf16[8,512,128]{2,1,0:T(8,128)(2,1)S(1)}, bf16[8,128,128]{2,1,0:T(8,128)(2,1)S(1)}) custom-call(bf16[512,8,128]{2,1,0:T(8,128)(2,1)S(1)} %copy-done.2, bf16[512,8,128]{2,1,0:T(8,128)(2,1)S(1)} %copy-done.3), custom_call_target="tpu_custom_call" | custom-call | flops 134217728 | bytes 4456448 | tf_op jit(solution)/shard_map/pallas_call | solution.py:49
  4.5 15.9 %all_to_all.25.recv_ref = bf16[8,128,128]{2,1,0:T(8,128)(2,1)S(1)} all-to-all(bf16[8,128,128]{2,1,0:T(8,128)(2,1)S(1)} %get-tuple-element.65), channel_id=1, replica_groups={{56,48,40,32,24,16,8,0},{57,49,41,33,25,17,9,1},{58,50,42,34,26,18,10,2..., dimensions={0} | all-to-all | bytes 524288 | tf_op jit(solution)/shard_map/all_to_all | solution.py:372
  20.5 0.0 copy-done.5
  20.5 0.0 copy-done.6
  20.5 0.1 shard_map.120
  20.5 4.3 %collective-permute-start.3 = (bf16[2,512,128]{2,1,0:T(8,128)(2,1)S(1)}, bf16[2,512,128]{2,1,0:T(8,128)(2,1)S(1)}, u32[]{:S(2)}, u32[]{:S(2)}) collective-permute-start(bf16[2,512,128]{2,1,0:T(8,128)(2,1)S(1)} %get-tuple-element.73.kv0), channel_id=1, source_target_pairs={{0,8},{8,16},{16,24},{24,32},{32,40},{40,48},{48,56},{56,64},{64,7... | collective-permute-start | bytes 786440 | tf_op jit(solution)/shard_map/ppermute | solution.py:390
  24.9 3.5 %collective-permute-start = (bf16[128,128]{1,0:T(8,128)(2,1)S(1)}, bf16[128,128]{1,0:T(8,128)(2,1)S(1)}, u32[]{:S(2)}, u32[]{:S(2)}) collective-permute-start(bf16[128,128]{1,0:T(8,128)(2,1)S(1)} %get-tuple-element.72), channel_id=1, source_target_pairs={{0,64},{64,128},{128,192},{1,65},{65,129},{129,193},{2,66},{66,130... | collective-permute-start | bytes 98312 | tf_op jit(solution)/shard_map/ppermute | solution.py:357
  28.4 0.7 collective-permute-start.1
  29.0 2.6 %collective-permute-start.2 = (bf16[128,128]{1,0:T(8,128)(2,1)S(1)}, bf16[128,128]{1,0:T(8,128)(2,1)S(1)}, u32[]{:S(2)}, u32[]{:S(2)}) collective-permute-start(bf16[128,128]{1,0:T(8,128)(2,1)S(1)} %get-tuple-element.72), channel_id=1, source_target_pairs={{0,128},{64,192},{1,129},{65,193},{2,130},{66,194},{3,131},{67,195... | collective-permute-start | bytes 98312 | tf_op jit(solution)/shard_map/ppermute | solution.py:357
  31.7 0.0 copy-done.1
  31.7 0.0 copy-done
  31.7 0.0 copy-done.7
  31.7 2.6 %shard_map.121 = (bf16[8,512,128]{2,1,0:T(8,128)(2,1)S(1)}, f32[8,512,128]{2,1,0:T(8,128)S(1)}, f32[8,512,128]{2,1,0:T(8,128)S(1)}) custom-call(bf16[512,8,128]{2,1,0:T(8,128)(2,1)S(1)} %copy-done, bf16[512,8,128]{2,1,0:T(8,128)(2,1)S(1)} %copy-done.1, f32[8,128]{1,0:T(8,128)S(1)} %copy-done.7, bf16[8,512,128]{2,1,0:T(8,128)(2,1)S(1)} %get-tuple-element.76.kh_ref, ...), custom_call_target="tpu_custom_call" | custom-call | flops 1073741824 | bytes 9441280 | tf_op jit(solution)/shard_map/pallas_call | solution.py:49
  34.3 0.0 collective-permute-done.refs_0_
  34.3 0.0 collective-permute-done.1.refs_1_
  34.3 0.0 collective-permute-done.2.refs_2_
  34.3 0.0 collective-permute-done.3.kv1
  34.3 0.1 shard_map.122
  34.4 13.9 %all_to_all.26.pre_ref = bf16[8,128,128]{2,1,0:T(8,128)(2,1)S(1)} all-to-all(bf16[8,128,128]{2,1,0:T(8,128)(2,1)S(1)} %shard_map.122), channel_id=1, replica_groups={{56,48,40,32,24,16,8,0},{57,49,41,33,25,17,9,1},{58,50,42,34,26,18,10,2..., dimensions={0} | all-to-all | bytes 524288 | tf_op jit(solution)/shard_map/all_to_all | solution.py:372
  48.3 2.6 %collective-permute-start.4 = (bf16[2,512,128]{2,1,0:T(8,128)(2,1)S(1)}, bf16[2,512,128]{2,1,0:T(8,128)(2,1)S(1)}, u32[]{:S(2)}, u32[]{:S(2)}) collective-permute-start(bf16[2,512,128]{2,1,0:T(8,128)(2,1)S(1)} %collective-permute-done.3.kv1), channel_id=1, source_target_pairs={{0,8},{8,16},{16,24},{24,32},{32,40},{40,48},{48,56},{56,64},{64,7... | collective-permute-start | bytes 786440 | tf_op jit(solution)/shard_map/ppermute | solution.py:390
  50.9 1.2 shard_map.123
  52.1 9.6 %all_to_all.27.g_ref = f32[8,2,512]{2,1,0:T(2,128)S(1)} all-to-all(f32[8,2,512]{2,1,0:T(2,128)S(1)} %get-tuple-element.87), channel_id=1, replica_groups=mesh['y'=4,'z'=8,'x'=4,'core'=2] {'x','core'}, dimensions={0} | all-to-all | bytes 65536 | tf_op jit(solution)/shard_map/all_to_all | solution.py:429
  61.6 0.0 collective-permute-done.4.kv2
  61.6 0.0 copy-start.4
  61.6 1.5 %shard_map.124 = (bf16[8,512,128]{2,1,0:T(8,128)(2,1)S(1)}, bf16[8,128,128]{2,1,0:T(8,128)(2,1)S(1)}, f32[512,128]{1,0:T(8,128)S(1)}) custom-call(f32[8,2,512]{2,1,0:T(2,128)S(1)} %all_to_all.27.g_ref, f32[8,512,128]{2,1,0:T(8,128)S(1)} %get-tuple-element.97.att_ref, f32[8,512,128]{2,1,0:T(8,128)S(1)} %get-tuple-element.81.gh_ref, ...), custom_call_target="tpu_custom_call" | custom-call | flops 134217728 | bytes 6848512 | tf_op jit(solution)/shard_map/pallas_call | solution.py:49
  63.1 14.3 %all_to_all.28.recv_ref = bf16[8,128,128]{2,1,0:T(8,128)(2,1)S(1)} all-to-all(bf16[8,128,128]{2,1,0:T(8,128)(2,1)S(1)} %get-tuple-element.91), channel_id=1, replica_groups={{56,48,40,32,24,16,8,0},{57,49,41,33,25,17,9,1},{58,50,42,34,26,18,10,2..., dimensions={0} | all-to-all | bytes 524288 | tf_op jit(solution)/shard_map/all_to_all | solution.py:372
  77.5 4.4 %collective-permute-start.7 = (bf16[2,512,128]{2,1,0:T(8,128)(2,1)S(1)}, bf16[2,512,128]{2,1,0:T(8,128)(2,1)S(1)}, u32[]{:S(2)}, u32[]{:S(2)}) collective-permute-start(bf16[2,512,128]{2,1,0:T(8,128)(2,1)S(1)} %collective-permute-done.4.kv2), channel_id=1, source_target_pairs={{0,8},{8,16},{16,24},{24,32},{32,40},{40,48},{48,56},{56,64},{64,7... | collective-permute-start | bytes 786440 | tf_op jit(solution)/shard_map/ppermute | solution.py:390
  81.9 0.0 copy-done.4
  81.9 4.0 %shard_map.126 = (bf16[512,8,128]{2,1,0:T(8,128)(2,1)}, bf16[512,8,128]{2,1,0:T(8,128)(2,1)}, bf16[4096,128]{1,0:T(8,128)(2,1)S(1)}) custom-call(bf16[8,512,128]{2,1,0:T(8,128)(2,1)S(1)} %get-tuple-element.76.kh_ref, bf16[8,512,128]{2,1,0:T(8,128)(2,1)S(1)} %get-tuple-element.77.vh_ref, bf16[8,512,128]{2,1,0:T(8,128)(2,1)S(1)} %get-tuple-element.101.da_ref, ...), custom_call_target="tpu_custom_call" | custom-call | flops 1073741824 | bytes 9965568 | tf_op jit(solution)/shard_map/pallas_call | solution.py:49
  85.9 3.9 %collective-permute-start.5 = (bf16[128,128]{1,0:T(8,128)(2,1)S(1)}, bf16[128,128]{1,0:T(8,128)(2,1)S(1)}, u32[]{:S(2)}, u32[]{:S(2)}) collective-permute-start(bf16[128,128]{1,0:T(8,128)(2,1)S(1)} %shard_map.125.own_ref), channel_id=1, source_target_pairs={{64,0},{128,64},{192,128},{65,1},{129,65},{193,129},{66,2},{130,66... | collective-permute-start | bytes 98312 | tf_op jit(solution)/shard_map/ppermute | solution.py:357
  89.8 4.3 %shard_map.127 = (f32[8,512,128]{2,1,0:T(8,128)S(1)}, f32[8,512,128]{2,1,0:T(8,128)S(1)}) custom-call(bf16[8,512,128]{2,1,0:T(8,128)(2,1)S(1)} %get-tuple-element.80.qh_ref, bf16[8,512,128]{2,1,0:T(8,128)(2,1)S(1)} %get-tuple-element.76.kh_ref, bf16[8,512,128]{2,1,0:T(8,128)(2,1)S(1)} %get-tuple-element.77.vh_ref, ...), custom_call_target="tpu_custom_call" | custom-call | flops 2147483648 | bytes 8388608 | tf_op jit(solution)/shard_map/pallas_call | solution.py:49
  94.1 0.0 collective-permute-done.5.other_ref.refs_0_
  94.1 1.3 %collective-permute-start.6 = (bf16[128,128]{1,0:T(8,128)(2,1)S(1)}, bf16[128,128]{1,0:T(8,128)(2,1)S(1)}, u32[]{:S(2)}, u32[]{:S(2)}) collective-permute-start(bf16[128,128]{1,0:T(8,128)(2,1)S(1)} %shard_map.128), channel_id=1, source_target_pairs={{128,0},{192,64},{129,1},{193,65},{130,2},{194,66},{131,3},{195,67... | collective-permute-start | bytes 98312 | tf_op jit(solution)/shard_map/ppermute | solution.py:357
  95.4 0.0 collective-permute-done.7.kv3
  95.4 13.6 %shard_map.129 = bf16[512,8,128]{2,1,0:T(8,128)(2,1)} custom-call(s32[1]{0:T(128)} %bitcast.pos_ref, bf16[4096,128]{1,0:T(8,128)(2,1)S(1)} %get-tuple-element.108.sq_ref, bf16[2,512,128]{2,1,0:T(8,128)(2,1)S(1)} %get-tuple-element.73.kv0, bf16[2,512,128]{2,1,0:T(8,128)(2,1)S(1)} %collective-permute-done.3.kv1, ...), custom_call_target="tpu_custom_call" | custom-call | flops 4294967296 | bytes 3145732 | tf_op jit(solution)/shard_map/pallas_call | solution.py:49
  109.0 0.0 collective-permute-done.6.refs_1_
  109.1 13.8 %all_to_all.29.suf_ref = bf16[8,128,128]{2,1,0:T(8,128)(2,1)S(1)} all-to-all(bf16[8,128,128]{2,1,0:T(8,128)(2,1)S(1)} %shard_map.130), channel_id=1, replica_groups={{56,48,40,32,24,16,8,0},{57,49,41,33,25,17,9,1},{58,50,42,34,26,18,10,2..., dimensions={0} | all-to-all | bytes 524288 | tf_op jit(solution)/shard_map/all_to_all | solution.py:372
  122.9 2.5 %shard_map.131 = (bf16[512,8,128]{2,1,0:T(8,128)(2,1)}, bf16[512,8,128]{2,1,0:T(8,128)(2,1)}) custom-call(bf16[8,512,128]{2,1,0:T(8,128)(2,1)S(1)} %get-tuple-element.76.kh_ref, bf16[8,512,128]{2,1,0:T(8,128)(2,1)S(1)} %get-tuple-element.77.vh_ref, f32[8,512,128]{2,1,0:T(8,128)S(1)} %get-tuple-element.113.pk_ref, ...), custom_call_target="tpu_custom_call" | custom-call | flops 268435456 | bytes 8650752 | tf_op jit(solution)/shard_map/pallas_call | solution.py:49
  (3 shorter events, 0.1 us)
Async XLA Ops:
  0.6 31.0 %copy-start.1 = (bf16[512,8,128]{2,1,0:T(8,128)(2,1)S(1)}, bf16[512,8,128]{2,1,0:T(8,128)(2,1)}, u32[]{:S(2)}) copy-start(bf16[512,8,128]{2,1,0:T(8,128)(2,1)} %c_ref) | copy-start | bytes 3145732
  0.6 31.0 %copy-start = (bf16[512,8,128]{2,1,0:T(8,128)(2,1)S(1)}, bf16[512,8,128]{2,1,0:T(8,128)(2,1)}, u32[]{:S(2)}) copy-start(bf16[512,8,128]{2,1,0:T(8,128)(2,1)} %q_ref) | copy-start | bytes 3145732
  0.7 1.4 %copy-start.2 = (bf16[512,8,128]{2,1,0:T(8,128)(2,1)S(1)}, bf16[512,8,128]{2,1,0:T(8,128)(2,1)}, u32[]{:S(2)}) copy-start(bf16[512,8,128]{2,1,0:T(8,128)(2,1)} %k_ref) | copy-start | bytes 3145732
  2.0 1.2 copy-start.3
  3.3 17.2 %copy-start.5 = (bf16[512,1,128]{2,0,1:T(8,128)(2,1)S(1)}, bf16[512,1,128]{2,0,1:T(8,128)(2,1)}, u32[]{:S(2)}) copy-start(bf16[512,1,128]{2,0,1:T(8,128)(2,1)} %param.14) | copy-start | bytes 393220
  3.3 17.2 %copy-start.6 = (bf16[512,1,128]{2,0,1:T(8,128)(2,1)S(1)}, bf16[512,1,128]{2,0,1:T(8,128)(2,1)}, u32[]{:S(2)}) copy-start(bf16[512,1,128]{2,0,1:T(8,128)(2,1)} %param.15) | copy-start | bytes 393220
  3.3 28.4 %copy-start.7 = (f32[8,128]{1,0:T(8,128)S(1)}, f32[8,128]{1,0:T(8,128)}, u32[]{:S(2)}) copy-start(f32[8,128]{1,0:T(8,128)} %gain_ref.3) | copy-start | bytes 12292
  20.5 13.8 %collective-permute-start.3 = (bf16[2,512,128]{2,1,0:T(8,128)(2,1)S(1)}, bf16[2,512,128]{2,1,0:T(8,128)(2,1)S(1)}, u32[]{:S(2)}, u32[]{:S(2)}) collective-permute-start(bf16[2,512,128]{2,1,0:T(8,128)(2,1)S(1)} %get-tuple-element.73.kv0), channel_id=1, source_target_pairs={{0,8},{8,16},{16,24},{24,32},{32,40},{40,48},{48,56},{56,64},{64,7... | collective-permute-start | bytes 786440 | tf_op jit(solution)/shard_map/ppermute | solution.py:390
  24.9 9.4 %collective-permute-start = (bf16[128,128]{1,0:T(8,128)(2,1)S(1)}, bf16[128,128]{1,0:T(8,128)(2,1)S(1)}, u32[]{:S(2)}, u32[]{:S(2)}) collective-permute-start(bf16[128,128]{1,0:T(8,128)(2,1)S(1)} %get-tuple-element.72), channel_id=1, source_target_pairs={{0,64},{64,128},{128,192},{1,65},{65,129},{129,193},{2,66},{66,130... | collective-permute-start | bytes 98312 | tf_op jit(solution)/shard_map/ppermute | solution.py:357
  28.4 6.0 %collective-permute-start.1 = (bf16[128,128]{1,0:T(8,128)(2,1)S(1)}, bf16[128,128]{1,0:T(8,128)(2,1)S(1)}, u32[]{:S(2)}, u32[]{:S(2)}) collective-permute-start(bf16[128,128]{1,0:T(8,128)(2,1)S(1)} %get-tuple-element.72), channel_id=1, source_target_pairs={{0,192},{1,193},{2,194},{3,195},{4,196},{5,197},{6,198},{7,199},{8... | collective-permute-start | bytes 98312 | tf_op jit(solution)/shard_map/ppermute | solution.py:357
  29.0 5.3 %collective-permute-start.2 = (bf16[128,128]{1,0:T(8,128)(2,1)S(1)}, bf16[128,128]{1,0:T(8,128)(2,1)S(1)}, u32[]{:S(2)}, u32[]{:S(2)}) collective-permute-start(bf16[128,128]{1,0:T(8,128)(2,1)S(1)} %get-tuple-element.72), channel_id=1, source_target_pairs={{0,128},{64,192},{1,129},{65,193},{2,130},{66,194},{3,131},{67,195... | collective-permute-start | bytes 98312 | tf_op jit(solution)/shard_map/ppermute | solution.py:357
  48.3 13.3 %collective-permute-start.4 = (bf16[2,512,128]{2,1,0:T(8,128)(2,1)S(1)}, bf16[2,512,128]{2,1,0:T(8,128)(2,1)S(1)}, u32[]{:S(2)}, u32[]{:S(2)}) collective-permute-start(bf16[2,512,128]{2,1,0:T(8,128)(2,1)S(1)} %collective-permute-done.3.kv1), channel_id=1, source_target_pairs={{0,8},{8,16},{16,24},{24,32},{32,40},{40,48},{48,56},{56,64},{64,7... | collective-permute-start | bytes 786440 | tf_op jit(solution)/shard_map/ppermute | solution.py:390
  61.6 20.3 %copy-start.4 = (bf16[512,8,128]{2,1,0:T(8,128)(2,1)S(1)}, bf16[512,8,128]{2,1,0:T(8,128)(2,1)}, u32[]{:S(2)}) copy-start(bf16[512,8,128]{2,1,0:T(8,128)(2,1)} %q2_ref.1) | copy-start | bytes 3145732
  77.5 18.0 %collective-permute-start.7 = (bf16[2,512,128]{2,1,0:T(8,128)(2,1)S(1)}, bf16[2,512,128]{2,1,0:T(8,128)(2,1)S(1)}, u32[]{:S(2)}, u32[]{:S(2)}) collective-permute-start(bf16[2,512,128]{2,1,0:T(8,128)(2,1)S(1)} %collective-permute-done.4.kv2), channel_id=1, source_target_pairs={{0,8},{8,16},{16,24},{24,32},{32,40},{40,48},{48,56},{56,64},{64,7... | collective-permute-start | bytes 786440 | tf_op jit(solution)/shard_map/ppermute | solution.py:390
  85.9 8.2 %collective-permute-start.5 = (bf16[128,128]{1,0:T(8,128)(2,1)S(1)}, bf16[128,128]{1,0:T(8,128)(2,1)S(1)}, u32[]{:S(2)}, u32[]{:S(2)}) collective-permute-start(bf16[128,128]{1,0:T(8,128)(2,1)S(1)} %shard_map.125.own_ref), channel_id=1, source_target_pairs={{64,0},{128,64},{192,128},{65,1},{129,65},{193,129},{66,2},{130,66... | collective-permute-start | bytes 98312 | tf_op jit(solution)/shard_map/ppermute | solution.py:357
  94.1 14.9 %collective-permute-start.6 = (bf16[128,128]{1,0:T(8,128)(2,1)S(1)}, bf16[128,128]{1,0:T(8,128)(2,1)S(1)}, u32[]{:S(2)}, u32[]{:S(2)}) collective-permute-start(bf16[128,128]{1,0:T(8,128)(2,1)S(1)} %shard_map.128), channel_id=1, source_target_pairs={{128,0},{192,64},{129,1},{193,65},{130,2},{194,66},{131,3},{195,67... | collective-permute-start | bytes 98312 | tf_op jit(solution)/shard_map/ppermute | solution.py:357

commit v3 on v2

--- a/solution.py
+++ b/solution.py
@@ -156,9 +156,29 @@
         bg_ref[h] = tn(qh_ref[h], d).astype(bf16)
 
 
-def softmax_kernel(pos_ref, sq_ref, kv0, kv1, kv2, kv3, out_hbm, out, ahead, sems):
+def final_kernel(
+    pos_ref, sq_ref, kv0, kv1, kv2, kv3,
+    kh_ref, vh_ref, pk_ref, pv_ref, suf_ref, gq_ref, norm_ref,
+    norm_hbm, gq_hbm, gk_hbm, gv_hbm, out_hbm,
+    out, ahead, ks, vs, kb, vb, sems, done_sems, grad_sems,
+):
     tokens, heads, width = out.shape
     kv = (kv0, kv1, kv2, kv3)
+    copies = fetch([(norm_ref, norm_hbm), (gq_ref, gq_hbm)], done_sems)
+    pieces = grad_sems.shape[0]
+    rows = tokens // pieces
+    for i in range(pieces):
+        part, flat = pl.ds(i * rows, rows), pl.ds(i * rows * heads, rows * heads)
+        for h in range(heads):
+            suf = suf_ref[h]
+            target = pl.ds(i * rows * heads + h, rows, stride=heads)
+            ks[target, :] = pk_ref[h, part].astype(f32) + nt(vh_ref[h, part], suf)
+            vs[target, :] = pv_ref[h, part].astype(f32) + nn(kh_ref[h, part], suf)
+        for src, buffer in ((ks, kb), (vs, vb)):
+            buffer[part] = src[flat, :].astype(bf16).reshape(rows, heads, width)
+        copies += fetch(
+            [(kb.at[part], gk_hbm.at[part]), (vb.at[part], gv_hbm.at[part])], grad_sems.at[i]
+        )
     scale = LOG2E * HEAD_WIDTH ** (-0.5)
     ones = jnp.ones((tokens, width), bf16)
     quarters = 4
@@ -232,11 +252,13 @@
     pl.when(have == WINDOW_BLOCKS - 1)(run_ahead)
     for i in range(quarters):
         store(i).wait()
+    for copy in copies:
+        copy.wait()
 
 
 def query_gradient_kernel(
     kh_ref, vh_ref, da_ref, pre_ref, att_ref, inv_ref, gain_ref, q2_ref,
-    gq_hbm, norm_hbm, sq_ref, qs, ns, out, norm, sems,
+    gq_ref, norm_ref, sq_ref, qs, ns,
 ):
     heads, tokens, width = kh_ref.shape
     half = tokens // 2
@@ -254,22 +276,11 @@
         qs[pl.ds(half * heads + h, half, stride=heads), :] = (
             gq[hi] + nn(d10, k[lo]) + nn(d11, k[hi])
         )
-    pieces = sems.shape[0] // 2
-    rows = tokens // pieces
-    copies = []
-    for i in range(pieces):
-        part, flat = pl.ds(i * rows, rows), pl.ds(i * rows * heads, rows * heads)
-        out[part] = qs[flat, :].astype(bf16).reshape(rows, heads, width)
-        n = ns[flat, :].astype(bf16)
-        norm[part] = n.reshape(rows, heads, width)
-        copies += fetch(
-            [(out.at[part], gq_hbm.at[part]), (norm.at[part], norm_hbm.at[part])],
-            sems.at[pl.ds(2 * i, 2)],
-        )
-        q2 = q2_ref[part].astype(f32).reshape(rows * heads, width)
-        sq_ref[flat, :] = (q2 + n.astype(f32)).astype(bf16)
-    for copy in copies:
-        copy.wait()
+    gq_ref[...] = qs[...].astype(bf16).reshape(tokens, heads, width)
+    n = ns[...].astype(bf16)
+    norm_ref[...] = n.reshape(tokens, heads, width)
+    q2 = q2_ref[...].astype(f32).reshape(tokens * heads, width)
+    sq_ref[...] = (q2 + n.astype(f32)).astype(bf16)
 
 
 def key_value_local_kernel(qh_ref, kh_ref, vh_ref, da_ref, gk_ref, gv_ref):
@@ -289,35 +300,10 @@
             m00 = up(nt(a[lo], b[lo]))
             m01 = nt(a[lo], b[hi]).astype(bf16)
             m11 = up(nt(a[hi], b[hi]))
-            out[h, :half] = nn(m00, other[lo]) + nn(m01, other[hi])
-            out[h, half:] = nn(m11, other[hi])
+            out[h, :half] = (nn(m00, other[lo]) + nn(m01, other[hi])).astype(bf16)
+            out[h, half:] = nn(m11, other[hi]).astype(bf16)
 
     each(heads, head)
-
-
-def finish_kernel(
-    kh_ref, vh_ref, pk_ref, pv_ref, suf_ref, gk_hbm, gv_hbm, ks, vs, kb, vb, sems
-):
-    heads, tokens, width = kh_ref.shape
-    pieces = sems.shape[0] // 2
-    rows = tokens // pieces
-    copies = []
-    for i in range(pieces):
-        part = pl.ds(i * rows, rows)
-        for h in range(heads):
-            suf = suf_ref[h]
-            target = pl.ds(i * rows * heads + h, rows, stride=heads)
-            ks[target, :] = pk_ref[h, part] + nt(vh_ref[h, part], suf)
-            vs[target, :] = pv_ref[h, part] + nn(kh_ref[h, part], suf)
-        flat = pl.ds(i * rows * heads, rows * heads)
-        for src, buffer in ((ks, kb), (vs, vb)):
-            buffer[part] = src[flat, :].astype(bf16).reshape(rows, heads, width)
-        copies += fetch(
-            [(kb.at[part], gk_hbm.at[part]), (vb.at[part], gv_hbm.at[part])],
-            sems.at[pl.ds(2 * i, 2)],
-        )
-    for copy in copies:
-        copy.wait()
 
 
 def scan_kernel(back, recv_ref, *refs):
@@ -437,40 +423,41 @@
     )
     back_pieces, att, da, inverse, kv2 = tied(spread(block_grad), att, da, inverse, kv2)
     kv3 = onward(kv2)
+    back_total = row_total(back_pieces)
+    back_near = from_row(back_total, 1, True)
     gq, normed, sq = call(
         query_gradient_kernel,
         [shape(query.shape, bf16), shape(query.shape, bf16), shape(flat, bf16)],
         [kh, vh, da, prefix, att, inverse, gain, query2],
-        [flat_buffer, flat_buffer, token_buffer, token_buffer, sems(8)],
+        [flat_buffer, flat_buffer],
         2 * unit,
-        hbm_out=(0, 1),
-    )
-    back_total, gq, da = tied(row_total(back_pieces), gq, da)
-    back_near = from_row(back_total, 1, True)
+    )
+    back_near, gq, da = tied(back_near, gq, da)
+    back_far = from_row(pair_total(back_total, back_near), 2, True)
     pk, pv = call(
-        key_value_local_kernel, [shape(head_major, f32)] * 2, [qh, kh, vh, da], (), 4 * unit
-    )
-    back_near, pk, pv, sq = tied(back_near, pk, pv, sq)
-    back_far = from_row(pair_total(back_total, back_near), 2, True)
-    (attended,) = call(
-        softmax_kernel,
-        [shape(query.shape, bf16)],
-        [have, sq, kv0, kv1, kv2, kv3],
-        [token_buffer, pltpu.VMEM((2, WINDOW_BLOCKS, tokens, tokens), f32), sems(4)],
-        8 * unit,
+        key_value_local_kernel, [shape(head_major, bf16)] * 2, [qh, kh, vh, da], (), 4 * unit
+    )
+    back_far, pk, sq, kv3 = tied(back_far, pk, sq, kv3)
+    suffix, sq = tied(spread(scanned(back_pieces, [back_near, back_far], True)), sq)
+    normed, gq, gk, gv, attended = call(
+        final_kernel,
+        [shape(query.shape, bf16)] * 5,
+        [have, sq, kv0, kv1, kv2, kv3, kh, vh, pk, pv, suffix, gq, normed],
+        [
+            token_buffer,
+            pltpu.VMEM((2, WINDOW_BLOCKS, tokens, tokens), f32),
+            flat_buffer,
+            flat_buffer,
+            token_buffer,
+            token_buffer,
+            sems(4),
+            sems(2),
+            pltpu.SemaphoreType.DMA((4, 2)),
+        ],
+        9 * unit,
         smem_first=True,
-        vmem=40,
-        hbm_out=(0,),
-    )
-    back_far, normed, attended, gq = tied(back_far, normed, attended, gq)
-    suffix = spread(scanned(back_pieces, [back_near, back_far], True))
-    gk, gv = call(
-        finish_kernel,
-        [shape(query.shape, bf16)] * 2,
-        [kh, vh, pk, pv, suffix],
-        [flat_buffer, flat_buffer, token_buffer, token_buffer, sems(8)],
-        unit // 2,
-        hbm_out=(0, 1),
+        vmem=32,
+        hbm_out=range(5),
     )
     return normed, gq, gk, gv, attended
 

time: 128 us -> 126 us (0.984); the launches traced: 126 us -> 125 us
  waiting for transfers between devices: 0.02 us -> 2.81 us
  blocking collectives: 67.6 us -> 65.8 us
    ppermute x5, waiting for transfers between devices: 0.01 us -> 2.81 us  [from_row(): lax.ppermute(x, 'y', [(i + d, i) if back else (i, i + d) for i in range(r...]
    all_to_all x4, blocking collectives: 58 us -> 56.3 us  [spread(): return lax.all_to_all(x, 'z', 0, 0, tiled=True, axis_index_groups=[members])]
    pallas_call x13 -> x12, Pallas kernels: 31 us -> 30.1 us  [call(): pl.pallas_call(kernel, out_shape=out_shapes, in_specs=specs, out_specs=[p...]
  transfers between devices with their start and end apart: 8 -> 8, of which waited for: 0 -> 2; matrix products, arithmetic and copies ran while one was open for 0% -> 0% of each run, Pallas kernels for 20% -> 9%
where the time goes in v3:
time: 126 us; the launch traced here: 125 us
  blocking collectives  65.8 us (52%)
  Pallas kernels  30.1 us (24%)
  starting transfers between devices  22.6 us (18%)
  waiting for transfers between devices  2.81 us (2%)
  local copies, waits for them, and re-layouts  2.61 us (2%)
    all_to_all x4, blocking collectives, spread(): return lax.all_to_all(x, 'z', 0, 0, tiled=True, axis_index_groups=[members])  56.3 us
    pallas_call x12, Pallas kernels, call(): pl.pallas_call(kernel, out_shape=out_shapes, in_specs=specs, out_specs=[p...  30.1 us
    ppermute x3, starting transfers between devices, onward(): return lax.ppermute(x, CTX, [(i, i + 1) for i in range(ring - 1)])  11.7 us
    ppermute x5, starting transfers between devices, from_row(): lax.ppermute(x, 'y', [(i + d, i) if back else (i, i + d) for i in range(r...  10.9 us
    all_to_all x1, blocking collectives, local(): gathered = lax.all_to_all(part, HEADS, 0, 0, tiled=True)  9.56 us
    ppermute x5, waiting for transfers between devices, from_row(): lax.ppermute(x, 'y', [(i + d, i) if back else (i, i + d) for i in range(r...  2.81 us
    unnamed x16, local copies, waits for them, and re-layouts  2.61 us
  transfers between devices with their start and end apart: 8, of which 2 were waited for; matrix products, arithmetic and copies ran while one was open for 0% of the time, Pallas kernels for 9%

profile of v3, /device:TPU:8, one launch (start us, length us, event | category | flops | bytes accessed | tf_op | source)
XLA Modules:
  0.0 125.0 jit_solution(5140617719417375483)
XLA Ops:
  0.6 0.0 copy-start.1
  0.6 0.0 copy-start
  0.7 0.0 copy-start.2
  0.7 1.4 %copy-done.2 = bf16[512,8,128]{2,1,0:T(8,128)(2,1)S(1)} copy-done((bf16[512,8,128]{2,1,0:T(8,128)(2,1)S(1)}, bf16[512,8,128]{2,1,0:T(8,128)(2,1)}, u32[]{:S(2)}) %copy-start.2) | copy-done | bytes 1048600
  2.0 0.0 copy-start.3
  2.0 1.2 copy-done.3
  3.3 0.0 copy-start.5
  3.3 0.0 copy-start.6
  3.3 0.0 copy-start.7
  3.3 1.3 %shard_map.119 = (bf16[8,512,128]{2,1,0:T(8,128)(2,1)S(1)}, bf16[8,512,128]{2,1,0:T(8,128)(2,1)S(1)}, bf16[8,128,128]{2,1,0:T(8,128)(2,1)S(1)}) custom-call(bf16[512,8,128]{2,1,0:T(8,128)(2,1)S(1)} %copy-done.2, bf16[512,8,128]{2,1,0:T(8,128)(2,1)S(1)} %copy-done.3), custom_call_target="tpu_custom_call" | custom-call | flops 134217728 | bytes 4456448 | tf_op jit(solution)/shard_map/pallas_call | solution.py:49
  4.5 15.9 %all_to_all.25.recv_ref = bf16[8,128,128]{2,1,0:T(8,128)(2,1)S(1)} all-to-all(bf16[8,128,128]{2,1,0:T(8,128)(2,1)S(1)} %get-tuple-element.62), channel_id=1, replica_groups={{56,48,40,32,24,16,8,0},{57,49,41,33,25,17,9,1},{58,50,42,34,26,18,10,2..., dimensions={0} | all-to-all | bytes 524288 | tf_op jit(solution)/shard_map/all_to_all | solution.py:358
  20.5 0.0 copy-done.5
  20.5 0.0 copy-done.6
  20.5 0.1 shard_map.120
  20.5 4.3 %collective-permute-start.3 = (bf16[2,512,128]{2,1,0:T(8,128)(2,1)S(1)}, bf16[2,512,128]{2,1,0:T(8,128)(2,1)S(1)}, u32[]{:S(2)}, u32[]{:S(2)}) collective-permute-start(bf16[2,512,128]{2,1,0:T(8,128)(2,1)S(1)} %get-tuple-element.70.kv0), channel_id=1, source_target_pairs={{0,8},{8,16},{16,24},{24,32},{32,40},{40,48},{48,56},{56,64},{64,7... | collective-permute-start | bytes 786440 | tf_op jit(solution)/shard_map/ppermute | solution.py:376
  24.9 4.2 %collective-permute-start.2 = (bf16[128,128]{1,0:T(8,128)(2,1)S(1)}, bf16[128,128]{1,0:T(8,128)(2,1)S(1)}, u32[]{:S(2)}, u32[]{:S(2)}) collective-permute-start(bf16[128,128]{1,0:T(8,128)(2,1)S(1)} %get-tuple-element.69), channel_id=1, source_target_pairs={{0,128},{64,192},{1,129},{65,193},{2,130},{66,194},{3,131},{67,195... | collective-permute-start | bytes 98312 | tf_op jit(solution)/shard_map/ppermute | solution.py:343
  29.1 0.7 collective-permute-start.1
  29.7 1.9 %collective-permute-start = (bf16[128,128]{1,0:T(8,128)(2,1)S(1)}, bf16[128,128]{1,0:T(8,128)(2,1)S(1)}, u32[]{:S(2)}, u32[]{:S(2)}) collective-permute-start(bf16[128,128]{1,0:T(8,128)(2,1)S(1)} %get-tuple-element.69), channel_id=1, source_target_pairs={{0,64},{64,128},{128,192},{1,65},{65,129},{129,193},{2,66},{66,130... | collective-permute-start | bytes 98312 | tf_op jit(solution)/shard_map/ppermute | solution.py:343
  31.7 0.0 copy-done.1
  31.7 0.0 copy-done
  31.7 0.0 copy-done.7
  31.7 2.6 %shard_map.121 = (bf16[8,512,128]{2,1,0:T(8,128)(2,1)S(1)}, f32[8,512,128]{2,1,0:T(8,128)S(1)}, f32[8,512,128]{2,1,0:T(8,128)S(1)}) custom-call(bf16[512,8,128]{2,1,0:T(8,128)(2,1)S(1)} %copy-done, bf16[512,8,128]{2,1,0:T(8,128)(2,1)S(1)} %copy-done.1, f32[8,128]{1,0:T(8,128)S(1)} %copy-done.7, bf16[8,512,128]{2,1,0:T(8,128)(2,1)S(1)} %get-tuple-element.73.kh_ref, ...), custom_call_target="tpu_custom_call" | custom-call | flops 1073741824 | bytes 9441280 | tf_op jit(solution)/shard_map/pallas_call | solution.py:49
  34.3 0.0 collective-permute-done.2.refs_2_
  34.3 0.0 collective-permute-done.1.refs_1_
  34.3 1.2 collective-permute-done.refs_0_
  35.5 0.0 collective-permute-done.3.kv1
  35.6 0.1 shard_map.122
  35.6 13.3 %all_to_all.26.pre_ref = bf16[8,128,128]{2,1,0:T(8,128)(2,1)S(1)} all-to-all(bf16[8,128,128]{2,1,0:T(8,128)(2,1)S(1)} %shard_map.122), channel_id=1, replica_groups={{56,48,40,32,24,16,8,0},{57,49,41,33,25,17,9,1},{58,50,42,34,26,18,10,2..., dimensions={0} | all-to-all | bytes 524288 | tf_op jit(solution)/shard_map/all_to_all | solution.py:358
  48.9 3.1 %collective-permute-start.4 = (bf16[2,512,128]{2,1,0:T(8,128)(2,1)S(1)}, bf16[2,512,128]{2,1,0:T(8,128)(2,1)S(1)}, u32[]{:S(2)}, u32[]{:S(2)}) collective-permute-start(bf16[2,512,128]{2,1,0:T(8,128)(2,1)S(1)} %collective-permute-done.3.kv1), channel_id=1, source_target_pairs={{0,8},{8,16},{16,24},{24,32},{32,40},{40,48},{48,56},{56,64},{64,7... | collective-permute-start | bytes 786440 | tf_op jit(solution)/shard_map/ppermute | solution.py:376
  51.9 1.2 shard_map.123
  53.1 9.6 %all_to_all.27.g_ref = f32[8,2,512]{2,1,0:T(2,128)S(1)} all-to-all(f32[8,2,512]{2,1,0:T(2,128)S(1)} %get-tuple-element.84), channel_id=1, replica_groups=mesh['y'=4,'z'=8,'x'=4,'core'=2] {'x','core'}, dimensions={0} | all-to-all | bytes 65536 | tf_op jit(solution)/shard_map/all_to_all | solution.py:415
  62.7 0.0 collective-permute-done.4.kv2
  62.7 0.0 copy-start.4
  62.7 1.5 %shard_map.124 = (bf16[8,512,128]{2,1,0:T(8,128)(2,1)S(1)}, bf16[8,128,128]{2,1,0:T(8,128)(2,1)S(1)}, f32[512,128]{1,0:T(8,128)S(1)}) custom-call(f32[8,2,512]{2,1,0:T(2,128)S(1)} %all_to_all.27.g_ref, f32[8,512,128]{2,1,0:T(8,128)S(1)} %get-tuple-element.94.att_ref, f32[8,512,128]{2,1,0:T(8,128)S(1)} %get-tuple-element.78.gh_ref, ...), custom_call_target="tpu_custom_call" | custom-call | flops 134217728 | bytes 6848512 | tf_op jit(solution)/shard_map/pallas_call | solution.py:49
  64.2 13.8 %all_to_all.28.recv_ref = bf16[8,128,128]{2,1,0:T(8,128)(2,1)S(1)} all-to-all(bf16[8,128,128]{2,1,0:T(8,128)(2,1)S(1)} %get-tuple-element.88), channel_id=1, replica_groups={{56,48,40,32,24,16,8,0},{57,49,41,33,25,17,9,1},{58,50,42,34,26,18,10,2..., dimensions={0} | all-to-all | bytes 524288 | tf_op jit(solution)/shard_map/all_to_all | solution.py:358
  78.0 2.7 %collective-permute-start.5 = (bf16[128,128]{1,0:T(8,128)(2,1)S(1)}, bf16[128,128]{1,0:T(8,128)(2,1)S(1)}, u32[]{:S(2)}, u32[]{:S(2)}) collective-permute-start(bf16[128,128]{1,0:T(8,128)(2,1)S(1)} %shard_map.125.own_ref), channel_id=1, source_target_pairs={{64,0},{128,64},{192,128},{65,1},{129,65},{193,129},{66,2},{130,66... | collective-permute-start | bytes 98312 | tf_op jit(solution)/shard_map/ppermute | solution.py:343
  80.6 4.3 %collective-permute-start.7 = (bf16[2,512,128]{2,1,0:T(8,128)(2,1)S(1)}, bf16[2,512,128]{2,1,0:T(8,128)(2,1)S(1)}, u32[]{:S(2)}, u32[]{:S(2)}) collective-permute-start(bf16[2,512,128]{2,1,0:T(8,128)(2,1)S(1)} %collective-permute-done.4.kv2), channel_id=1, source_target_pairs={{0,8},{8,16},{16,24},{24,32},{32,40},{40,48},{48,56},{56,64},{64,7... | collective-permute-start | bytes 786440 | tf_op jit(solution)/shard_map/ppermute | solution.py:376
  85.0 0.0 copy-done.4
  85.0 3.6 %shard_map.126 = (bf16[512,8,128]{2,1,0:T(8,128)(2,1)S(1)}, bf16[512,8,128]{2,1,0:T(8,128)(2,1)S(1)}, bf16[4096,128]{1,0:T(8,128)(2,1)S(1)}) custom-call(bf16[8,512,128]{2,1,0:T(8,128)(2,1)S(1)} %get-tuple-element.73.kh_ref, bf16[8,512,128]{2,1,0:T(8,128)(2,1)S(1)} %get-tuple-element.74.vh_ref, bf16[8,512,128]{2,1,0:T(8,128)(2,1)S(1)} %get-tuple-element.98.da_ref, ...), custom_call_target="tpu_custom_call" | custom-call | flops 1073741824 | bytes 9965568 | tf_op jit(solution)/shard_map/pallas_call | solution.py:49
  88.6 0.0 collective-permute-done.5.other_ref.refs_0_
  88.6 1.5 %collective-permute-start.6 = (bf16[128,128]{1,0:T(8,128)(2,1)S(1)}, bf16[128,128]{1,0:T(8,128)(2,1)S(1)}, u32[]{:S(2)}, u32[]{:S(2)}) collective-permute-start(bf16[128,128]{1,0:T(8,128)(2,1)S(1)} %shard_map.127), channel_id=1, source_target_pairs={{128,0},{192,64},{129,1},{193,65},{130,2},{194,66},{131,3},{195,67... | collective-permute-start | bytes 98312 | tf_op jit(solution)/shard_map/ppermute | solution.py:343
  90.1 4.3 %shard_map.128 = (bf16[8,512,128]{2,1,0:T(8,128)(2,1)S(1)}, bf16[8,512,128]{2,1,0:T(8,128)(2,1)S(1)}) custom-call(bf16[8,512,128]{2,1,0:T(8,128)(2,1)S(1)} %get-tuple-element.77.qh_ref, bf16[8,512,128]{2,1,0:T(8,128)(2,1)S(1)} %get-tuple-element.73.kh_ref, bf16[8,512,128]{2,1,0:T(8,128)(2,1)S(1)} %get-tuple-element.74.vh_ref, ...), custom_call_target="tpu_custom_call" | custom-call | flops 2147483648 | bytes 6291456 | tf_op jit(solution)/shard_map/pallas_call | solution.py:49
  94.3 1.6 %collective-permute-done.6.refs_1_ = bf16[128,128]{1,0:T(8,128)(2,1)S(1)} collective-permute-done((bf16[128,128]{1,0:T(8,128)(2,1)S(1)}, bf16[128,128]{1,0:T(8,128)(2,1)S(1)}, u32[]{:S(2)}, u32[]{:S(2)}) %collective-permute-start.6) | collective-permute-done | bytes 32800 | tf_op jit(solution)/shard_map/ppermute | solution.py:343
  95.9 0.0 collective-permute-done.7.kv3
  96.0 13.3 %all_to_all.29.suf_ref = bf16[8,128,128]{2,1,0:T(8,128)(2,1)S(1)} all-to-all(bf16[8,128,128]{2,1,0:T(8,128)(2,1)S(1)} %shard_map.129), channel_id=1, replica_groups={{56,48,40,32,24,16,8,0},{57,49,41,33,25,17,9,1},{58,50,42,34,26,18,10,2..., dimensions={0} | all-to-all | bytes 524288 | tf_op jit(solution)/shard_map/all_to_all | solution.py:358
  109.2 15.5 %shard_map.130 = (bf16[512,8,128]{2,1,0:T(8,128)(2,1)}, bf16[512,8,128]{2,1,0:T(8,128)(2,1)}, bf16[512,8,128]{2,1,0:T(8,128)(2,1)}, bf16[512,8,128]{2,1,0:T(8,128)(2,1)}, bf16[512,8,128]{2,1,0:T(8,128)(2,1)}) custom-call(s32[1]{0:T(128)} %bitcast.pos_ref, bf16[4096,128]{1,0:T(8,128)(2,1)S(1)} %get-tuple-element.104.sq_ref, ...), custom_call_target="tpu_custom_call" | custom-call | flops 4831838208 | bytes 13893636 | tf_op jit(solution)/shard_map/pallas_call | solution.py:49
  (3 shorter events, 0.1 us)
Async XLA Ops:
  0.6 31.0 %copy-start.1 = (bf16[512,8,128]{2,1,0:T(8,128)(2,1)S(1)}, bf16[512,8,128]{2,1,0:T(8,128)(2,1)}, u32[]{:S(2)}) copy-start(bf16[512,8,128]{2,1,0:T(8,128)(2,1)} %c_ref) | copy-start | bytes 3145732
  0.6 31.0 %copy-start = (bf16[512,8,128]{2,1,0:T(8,128)(2,1)S(1)}, bf16[512,8,128]{2,1,0:T(8,128)(2,1)}, u32[]{:S(2)}) copy-start(bf16[512,8,128]{2,1,0:T(8,128)(2,1)} %q_ref) | copy-start | bytes 3145732
  0.7 1.4 %copy-start.2 = (bf16[512,8,128]{2,1,0:T(8,128)(2,1)S(1)}, bf16[512,8,128]{2,1,0:T(8,128)(2,1)}, u32[]{:S(2)}) copy-start(bf16[512,8,128]{2,1,0:T(8,128)(2,1)} %k_ref) | copy-start | bytes 3145732
  2.0 1.2 copy-start.3
  3.3 17.2 %copy-start.5 = (bf16[512,1,128]{2,0,1:T(8,128)(2,1)S(1)}, bf16[512,1,128]{2,0,1:T(8,128)(2,1)}, u32[]{:S(2)}) copy-start(bf16[512,1,128]{2,0,1:T(8,128)(2,1)} %param.14) | copy-start | bytes 393220
  3.3 17.2 %copy-start.6 = (bf16[512,1,128]{2,0,1:T(8,128)(2,1)S(1)}, bf16[512,1,128]{2,0,1:T(8,128)(2,1)}, u32[]{:S(2)}) copy-start(bf16[512,1,128]{2,0,1:T(8,128)(2,1)} %param.15) | copy-start | bytes 393220
  3.3 28.4 %copy-start.7 = (f32[8,128]{1,0:T(8,128)S(1)}, f32[8,128]{1,0:T(8,128)}, u32[]{:S(2)}) copy-start(f32[8,128]{1,0:T(8,128)} %gain_ref.3) | copy-start | bytes 12292
  20.5 15.0 %collective-permute-start.3 = (bf16[2,512,128]{2,1,0:T(8,128)(2,1)S(1)}, bf16[2,512,128]{2,1,0:T(8,128)(2,1)S(1)}, u32[]{:S(2)}, u32[]{:S(2)}) collective-permute-start(bf16[2,512,128]{2,1,0:T(8,128)(2,1)S(1)} %get-tuple-element.70.kv0), channel_id=1, source_target_pairs={{0,8},{8,16},{16,24},{24,32},{32,40},{40,48},{48,56},{56,64},{64,7... | collective-permute-start | bytes 786440 | tf_op jit(solution)/shard_map/ppermute | solution.py:376
  24.9 9.4 %collective-permute-start.2 = (bf16[128,128]{1,0:T(8,128)(2,1)S(1)}, bf16[128,128]{1,0:T(8,128)(2,1)S(1)}, u32[]{:S(2)}, u32[]{:S(2)}) collective-permute-start(bf16[128,128]{1,0:T(8,128)(2,1)S(1)} %get-tuple-element.69), channel_id=1, source_target_pairs={{0,128},{64,192},{1,129},{65,193},{2,130},{66,194},{3,131},{67,195... | collective-permute-start | bytes 98312 | tf_op jit(solution)/shard_map/ppermute | solution.py:343
  29.1 5.2 %collective-permute-start.1 = (bf16[128,128]{1,0:T(8,128)(2,1)S(1)}, bf16[128,128]{1,0:T(8,128)(2,1)S(1)}, u32[]{:S(2)}, u32[]{:S(2)}) collective-permute-start(bf16[128,128]{1,0:T(8,128)(2,1)S(1)} %get-tuple-element.69), channel_id=1, source_target_pairs={{0,192},{1,193},{2,194},{3,195},{4,196},{5,197},{6,198},{7,199},{8... | collective-permute-start | bytes 98312 | tf_op jit(solution)/shard_map/ppermute | solution.py:343
  29.7 5.8 %collective-permute-start = (bf16[128,128]{1,0:T(8,128)(2,1)S(1)}, bf16[128,128]{1,0:T(8,128)(2,1)S(1)}, u32[]{:S(2)}, u32[]{:S(2)}) collective-permute-start(bf16[128,128]{1,0:T(8,128)(2,1)S(1)} %get-tuple-element.69), channel_id=1, source_target_pairs={{0,64},{64,128},{128,192},{1,65},{65,129},{129,193},{2,66},{66,130... | collective-permute-start | bytes 98312 | tf_op jit(solution)/shard_map/ppermute | solution.py:343
  48.9 13.8 %collective-permute-start.4 = (bf16[2,512,128]{2,1,0:T(8,128)(2,1)S(1)}, bf16[2,512,128]{2,1,0:T(8,128)(2,1)S(1)}, u32[]{:S(2)}, u32[]{:S(2)}) collective-permute-start(bf16[2,512,128]{2,1,0:T(8,128)(2,1)S(1)} %collective-permute-done.3.kv1), channel_id=1, source_target_pairs={{0,8},{8,16},{16,24},{24,32},{32,40},{40,48},{48,56},{56,64},{64,7... | collective-permute-start | bytes 786440 | tf_op jit(solution)/shard_map/ppermute | solution.py:376
  62.7 22.3 %copy-start.4 = (bf16[512,8,128]{2,1,0:T(8,128)(2,1)S(1)}, bf16[512,8,128]{2,1,0:T(8,128)(2,1)}, u32[]{:S(2)}) copy-start(bf16[512,8,128]{2,1,0:T(8,128)(2,1)} %q2_ref.1) | copy-start | bytes 3145732
  78.0 10.6 %collective-permute-start.5 = (bf16[128,128]{1,0:T(8,128)(2,1)S(1)}, bf16[128,128]{1,0:T(8,128)(2,1)S(1)}, u32[]{:S(2)}, u32[]{:S(2)}) collective-permute-start(bf16[128,128]{1,0:T(8,128)(2,1)S(1)} %shard_map.125.own_ref), channel_id=1, source_target_pairs={{64,0},{128,64},{192,128},{65,1},{129,65},{193,129},{66,2},{130,66... | collective-permute-start | bytes 98312 | tf_op jit(solution)/shard_map/ppermute | solution.py:343
  80.6 15.3 %collective-permute-start.7 = (bf16[2,512,128]{2,1,0:T(8,128)(2,1)S(1)}, bf16[2,512,128]{2,1,0:T(8,128)(2,1)S(1)}, u32[]{:S(2)}, u32[]{:S(2)}) collective-permute-start(bf16[2,512,128]{2,1,0:T(8,128)(2,1)S(1)} %collective-permute-done.4.kv2), channel_id=1, source_target_pairs={{0,8},{8,16},{16,24},{24,32},{32,40},{40,48},{48,56},{56,64},{64,7... | collective-permute-start | bytes 786440 | tf_op jit(solution)/shard_map/ppermute | solution.py:376
  88.6 7.3 %collective-permute-start.6 = (bf16[128,128]{1,0:T(8,128)(2,1)S(1)}, bf16[128,128]{1,0:T(8,128)(2,1)S(1)}, u32[]{:S(2)}, u32[]{:S(2)}) collective-permute-start(bf16[128,128]{1,0:T(8,128)(2,1)S(1)} %shard_map.127), channel_id=1, source_target_pairs={{128,0},{192,64},{129,1},{193,65},{130,2},{194,66},{131,3},{195,67... | collective-permute-start | bytes 98312 | tf_op jit(solution)/shard_map/ppermute | solution.py:343

commit v4 on v3

--- a/solution.py
+++ b/solution.py
@@ -70,16 +70,20 @@
     return copies
 
 
-def state_kernel(k_ref, v_ref, kh_ref, vh_ref, st_ref, ks, vs):
-    tokens, heads, width = k_ref.shape
-    ks[...] = k_ref[...].astype(f32).reshape(tokens * heads, width)
+def head_major_kernel(x_ref, out_ref, flat):
+    tokens, heads, width = x_ref.shape
+    flat[...] = x_ref[...].astype(f32).reshape(tokens * heads, width)
+    for h in range(heads):
+        out_ref[h] = flat[pl.ds(h, tokens, stride=heads), :].astype(bf16)
+
+
+def state_kernel(kh_ref, v_ref, vh_ref, st_ref, vs):
+    tokens, heads, width = v_ref.shape
     vs[...] = v_ref[...].astype(f32).reshape(tokens * heads, width)
     for h in range(heads):
-        kh = ks[pl.ds(h, tokens, stride=heads), :].astype(bf16)
         vh = vs[pl.ds(h, tokens, stride=heads), :].astype(bf16)
-        kh_ref[h] = kh
         vh_ref[h] = vh
-        st_ref[h] = tn(kh, vh).astype(bf16)
+        st_ref[h] = tn(kh_ref[h], vh).astype(bf16)
 
 
 def each(count, body, unroll=8):
@@ -118,6 +122,15 @@
     each(heads, head)
 
 
+def terms(x):
+    parts = []
+    for _ in range(3):
+        high = x.astype(bf16)
+        parts.append(high)
+        x = x - high.astype(f32)
+    return parts
+
+
 def attention_kernel(loc_ref, qh_ref, gh_ref, pre_ref, att_ref, part_ref):
     heads, tokens, width = loc_ref.shape
     squares = jnp.zeros((tokens, width), f32)
@@ -127,21 +140,18 @@
         att_ref[h] = att
         squares = squares + att * att
         inner = inner + att * gh_ref[h]
-    ones = jnp.ones((8, width), f32)
+    ones = jnp.ones((8, width), bf16)
     rows = jnp.concatenate(
-        [
-            nt(ones, squares, lax.Precision.HIGHEST)[0:1],
-            nt(ones, inner, lax.Precision.HIGHEST)[0:1],
-        ]
+        [sum(nt(ones, part) for part in terms(x))[0:1] for x in (squares, inner)]
     )
     for j in range(part_ref.shape[0]):
         part_ref[j] = rows
 
 
 def row_scales(g_ref):
-    ones = jnp.ones((g_ref.shape[0], HEAD_WIDTH), f32)
-    squares = tn(g_ref[:, 0, :], ones, lax.Precision.HIGHEST)
-    inner = tn(g_ref[:, 1, :], ones, lax.Precision.HIGHEST)
+    ones = jnp.ones((g_ref.shape[0], HEAD_WIDTH), bf16)
+    squares = sum(tn(part, ones) for part in terms(g_ref[:, 0, :]))
+    inner = sum(tn(part, ones) for part in terms(g_ref[:, 1, :]))
     inverse = 1.0 / jnp.sqrt(squares / CHANNELS + EPSILON)
     return inverse, inverse * inner / CHANNELS
 
@@ -378,11 +388,12 @@
     have = jnp.minimum(lax.axis_index(CTX), WINDOW_BLOCKS - 1).astype(jnp.int32).reshape(1)
     key, value, have = tied(key, value, have)
 
-    kh, vh, states = call(
+    (kh,) = call(head_major_kernel, [shape(head_major, bf16)], [key], [flat_buffer])
+    vh, states = call(
         state_kernel,
-        [shape(head_major, bf16), shape(head_major, bf16), shape(square, bf16)],
-        [key, value],
-        [flat_buffer, flat_buffer],
+        [shape(head_major, bf16), shape(square, bf16)],
+        [kh, value],
+        [flat_buffer],
         unit // 4,
     )
     states, query, cotangent = tied(states, query, cotangent)

time: 126 us -> 125 us (level)
    pallas_call x12 -> x13, Pallas kernels: 30.1 us -> 29.9 us  [call(): pl.pallas_call(kernel, out_shape=out_shapes, in_specs=specs, out_specs=[p...]
where the time goes in v4:
time: 125 us; the launch traced here: 124 us
  blocking collectives  65.8 us (53%)
  Pallas kernels  29.9 us (24%)
  starting transfers between devices  22.6 us (18%)
  waiting for transfers between devices  2.81 us (2%)
  local copies, waits for them, and re-layouts  1.87 us (1%)
    all_to_all x4, blocking collectives, spread(): return lax.all_to_all(x, 'z', 0, 0, tiled=True, axis_index_groups=[members])  56.2 us
    pallas_call x13, Pallas kernels, call(): pl.pallas_call(kernel, out_shape=out_shapes, in_specs=specs, out_specs=[p...  29.9 us
    ppermute x3, starting transfers between devices, onward(): return lax.ppermute(x, CTX, [(i, i + 1) for i in range(ring - 1)])  11.7 us
    ppermute x5, starting transfers between devices, from_row(): lax.ppermute(x, 'y', [(i + d, i) if back else (i, i + d) for i in range(r...  10.9 us
    all_to_all x1, blocking collectives, local(): gathered = lax.all_to_all(part, HEADS, 0, 0, tiled=True)  9.57 us
    ppermute x5, waiting for transfers between devices, from_row(): lax.ppermute(x, 'y', [(i + d, i) if back else (i, i + d) for i in range(r...  2.81 us
  transfers between devices with their start and end apart: 8, of which 2 were waited for; matrix products, arithmetic and copies ran while one was open for 0% of the time, Pallas kernels for 9%

profile of v4, /device:TPU:8, one launch (start us, length us, event | category | flops | bytes accessed | tf_op | source)
XLA Modules:
  0.0 124.0 jit_solution(14039019561398689931)
XLA Ops:
  0.6 0.0 copy-start.2
  0.7 1.2 copy-done.2
  1.9 0.0 copy-start.3
  1.9 0.0 copy-start.5
  1.9 0.0 copy-start.6
  1.9 0.6 shard_map.119.kh_ref
  2.5 0.6 copy-done.3
  3.1 0.0 copy-start
  3.1 0.0 copy-start.1
  3.1 0.0 copy-start.7
  3.1 0.9 shard_map.120
  4.1 15.9 %all_to_all.25.recv_ref = bf16[8,128,128]{2,1,0:T(8,128)(2,1)S(1)} all-to-all(bf16[8,128,128]{2,1,0:T(8,128)(2,1)S(1)} %get-tuple-element.61), channel_id=1, replica_groups={{56,48,40,32,24,16,8,0},{57,49,41,33,25,17,9,1},{58,50,42,34,26,18,10,2..., dimensions={0} | all-to-all | bytes 524288 | tf_op jit(solution)/shard_map/all_to_all | solution.py:368
  20.0 0.0 copy-done.5
  20.0 0.0 copy-done.6
  20.0 0.1 shard_map.121
  20.0 4.3 %collective-permute-start.3 = (bf16[2,512,128]{2,1,0:T(8,128)(2,1)S(1)}, bf16[2,512,128]{2,1,0:T(8,128)(2,1)S(1)}, u32[]{:S(2)}, u32[]{:S(2)}) collective-permute-start(bf16[2,512,128]{2,1,0:T(8,128)(2,1)S(1)} %get-tuple-element.68.kv0), channel_id=1, source_target_pairs={{0,8},{8,16},{16,24},{24,32},{32,40},{40,48},{48,56},{56,64},{64,7... | collective-permute-start | bytes 786440 | tf_op jit(solution)/shard_map/ppermute | solution.py:386
  24.4 4.2 %collective-permute-start.2 = (bf16[128,128]{1,0:T(8,128)(2,1)S(1)}, bf16[128,128]{1,0:T(8,128)(2,1)S(1)}, u32[]{:S(2)}, u32[]{:S(2)}) collective-permute-start(bf16[128,128]{1,0:T(8,128)(2,1)S(1)} %get-tuple-element.67), channel_id=1, source_target_pairs={{0,128},{64,192},{1,129},{65,193},{2,130},{66,194},{3,131},{67,195... | collective-permute-start | bytes 98312 | tf_op jit(solution)/shard_map/ppermute | solution.py:353
  28.6 0.7 collective-permute-start.1
  29.3 1.9 %collective-permute-start = (bf16[128,128]{1,0:T(8,128)(2,1)S(1)}, bf16[128,128]{1,0:T(8,128)(2,1)S(1)}, u32[]{:S(2)}, u32[]{:S(2)}) collective-permute-start(bf16[128,128]{1,0:T(8,128)(2,1)S(1)} %get-tuple-element.67), channel_id=1, source_target_pairs={{0,64},{64,128},{128,192},{1,65},{65,129},{129,193},{2,66},{66,130... | collective-permute-start | bytes 98312 | tf_op jit(solution)/shard_map/ppermute | solution.py:353
  31.2 0.0 copy-done
  31.2 0.0 copy-done.1
  31.2 0.0 copy-done.7
  31.2 2.6 %shard_map.122 = (bf16[8,512,128]{2,1,0:T(8,128)(2,1)S(1)}, f32[8,512,128]{2,1,0:T(8,128)S(1)}, f32[8,512,128]{2,1,0:T(8,128)S(1)}) custom-call(bf16[512,8,128]{2,1,0:T(8,128)(2,1)S(1)} %copy-done, bf16[512,8,128]{2,1,0:T(8,128)(2,1)S(1)} %copy-done.1, f32[8,128]{1,0:T(8,128)S(1)} %copy-done.7, bf16[8,512,128]{2,1,0:T(8,128)(2,1)S(1)} %shard_map.119.kh_ref, ...), custom_call_target="tpu_custom_call" | custom-call | flops 1073741824 | bytes 9441280 | tf_op jit(solution)/shard_map/pallas_call | solution.py:49
  33.8 0.0 collective-permute-done.2.refs_2_
  33.8 0.0 collective-permute-done.1.refs_1_
  33.8 1.2 collective-permute-done.refs_0_
  35.1 0.0 collective-permute-done.3.kv1
  35.1 0.1 shard_map.123
  35.1 13.3 %all_to_all.26.pre_ref = bf16[8,128,128]{2,1,0:T(8,128)(2,1)S(1)} all-to-all(bf16[8,128,128]{2,1,0:T(8,128)(2,1)S(1)} %shard_map.123), channel_id=1, replica_groups={{56,48,40,32,24,16,8,0},{57,49,41,33,25,17,9,1},{58,50,42,34,26,18,10,2..., dimensions={0} | all-to-all | bytes 524288 | tf_op jit(solution)/shard_map/all_to_all | solution.py:368
  48.4 3.1 %collective-permute-start.4 = (bf16[2,512,128]{2,1,0:T(8,128)(2,1)S(1)}, bf16[2,512,128]{2,1,0:T(8,128)(2,1)S(1)}, u32[]{:S(2)}, u32[]{:S(2)}) collective-permute-start(bf16[2,512,128]{2,1,0:T(8,128)(2,1)S(1)} %collective-permute-done.3.kv1), channel_id=1, source_target_pairs={{0,8},{8,16},{16,24},{24,32},{32,40},{40,48},{48,56},{56,64},{64,7... | collective-permute-start | bytes 786440 | tf_op jit(solution)/shard_map/ppermute | solution.py:386
  51.5 0.9 shard_map.124
  52.4 9.6 %all_to_all.27.g_ref = f32[8,2,512]{2,1,0:T(2,128)S(1)} all-to-all(f32[8,2,512]{2,1,0:T(2,128)S(1)} %get-tuple-element.82), channel_id=1, replica_groups=mesh['y'=4,'z'=8,'x'=4,'core'=2] {'x','core'}, dimensions={0} | all-to-all | bytes 65536 | tf_op jit(solution)/shard_map/all_to_all | solution.py:426
  62.0 0.0 collective-permute-done.4.kv2
  62.0 0.0 copy-start.4
  62.0 1.2 %shard_map.125 = (bf16[8,512,128]{2,1,0:T(8,128)(2,1)S(1)}, bf16[8,128,128]{2,1,0:T(8,128)(2,1)S(1)}, f32[512,128]{1,0:T(8,128)S(1)}) custom-call(f32[8,2,512]{2,1,0:T(2,128)S(1)} %all_to_all.27.g_ref, f32[8,512,128]{2,1,0:T(8,128)S(1)} %get-tuple-element.92.att_ref, f32[8,512,128]{2,1,0:T(8,128)S(1)} %get-tuple-element.76.gh_ref, ...), custom_call_target="tpu_custom_call" | custom-call | flops 134217728 | bytes 6848512 | tf_op jit(solution)/shard_map/pallas_call | solution.py:49
  63.2 13.8 %all_to_all.28.recv_ref = bf16[8,128,128]{2,1,0:T(8,128)(2,1)S(1)} all-to-all(bf16[8,128,128]{2,1,0:T(8,128)(2,1)S(1)} %get-tuple-element.86), channel_id=1, replica_groups={{56,48,40,32,24,16,8,0},{57,49,41,33,25,17,9,1},{58,50,42,34,26,18,10,2..., dimensions={0} | all-to-all | bytes 524288 | tf_op jit(solution)/shard_map/all_to_all | solution.py:368
  77.0 2.7 %collective-permute-start.5 = (bf16[128,128]{1,0:T(8,128)(2,1)S(1)}, bf16[128,128]{1,0:T(8,128)(2,1)S(1)}, u32[]{:S(2)}, u32[]{:S(2)}) collective-permute-start(bf16[128,128]{1,0:T(8,128)(2,1)S(1)} %shard_map.126.own_ref), channel_id=1, source_target_pairs={{64,0},{128,64},{192,128},{65,1},{129,65},{193,129},{66,2},{130,66... | collective-permute-start | bytes 98312 | tf_op jit(solution)/shard_map/ppermute | solution.py:353
  79.7 4.3 %collective-permute-start.7 = (bf16[2,512,128]{2,1,0:T(8,128)(2,1)S(1)}, bf16[2,512,128]{2,1,0:T(8,128)(2,1)S(1)}, u32[]{:S(2)}, u32[]{:S(2)}) collective-permute-start(bf16[2,512,128]{2,1,0:T(8,128)(2,1)S(1)} %collective-permute-done.4.kv2), channel_id=1, source_target_pairs={{0,8},{8,16},{16,24},{24,32},{32,40},{40,48},{48,56},{56,64},{64,7... | collective-permute-start | bytes 786440 | tf_op jit(solution)/shard_map/ppermute | solution.py:386
  84.0 0.0 copy-done.4
  84.1 3.6 %shard_map.127 = (bf16[512,8,128]{2,1,0:T(8,128)(2,1)S(1)}, bf16[512,8,128]{2,1,0:T(8,128)(2,1)S(1)}, bf16[4096,128]{1,0:T(8,128)(2,1)S(1)}) custom-call(bf16[8,512,128]{2,1,0:T(8,128)(2,1)S(1)} %shard_map.119.kh_ref, bf16[8,512,128]{2,1,0:T(8,128)(2,1)S(1)} %get-tuple-element.72.vh_ref, bf16[8,512,128]{2,1,0:T(8,128)(2,1)S(1)} %get-tuple-element.96.da_ref, ...), custom_call_target="tpu_custom_call" | custom-call | flops 1073741824 | bytes 9965568 | tf_op jit(solution)/shard_map/pallas_call | solution.py:49
  87.6 0.0 collective-permute-done.5.other_ref.refs_0_
  87.7 1.5 %collective-permute-start.6 = (bf16[128,128]{1,0:T(8,128)(2,1)S(1)}, bf16[128,128]{1,0:T(8,128)(2,1)S(1)}, u32[]{:S(2)}, u32[]{:S(2)}) collective-permute-start(bf16[128,128]{1,0:T(8,128)(2,1)S(1)} %shard_map.128), channel_id=1, source_target_pairs={{128,0},{192,64},{129,1},{193,65},{130,2},{194,66},{131,3},{195,67... | collective-permute-start | bytes 98312 | tf_op jit(solution)/shard_map/ppermute | solution.py:353
  89.1 4.3 %shard_map.129 = (bf16[8,512,128]{2,1,0:T(8,128)(2,1)S(1)}, bf16[8,512,128]{2,1,0:T(8,128)(2,1)S(1)}) custom-call(bf16[8,512,128]{2,1,0:T(8,128)(2,1)S(1)} %get-tuple-element.75.qh_ref, bf16[8,512,128]{2,1,0:T(8,128)(2,1)S(1)} %shard_map.119.kh_ref, bf16[8,512,128]{2,1,0:T(8,128)(2,1)S(1)} %get-tuple-element.72.vh_ref, ...), custom_call_target="tpu_custom_call" | custom-call | flops 2147483648 | bytes 6291456 | tf_op jit(solution)/shard_map/pallas_call | solution.py:49
  93.4 1.6 %collective-permute-done.6.refs_1_ = bf16[128,128]{1,0:T(8,128)(2,1)S(1)} collective-permute-done((bf16[128,128]{1,0:T(8,128)(2,1)S(1)}, bf16[128,128]{1,0:T(8,128)(2,1)S(1)}, u32[]{:S(2)}, u32[]{:S(2)}) %collective-permute-start.6) | collective-permute-done | bytes 32800 | tf_op jit(solution)/shard_map/ppermute | solution.py:353
  95.0 0.0 collective-permute-done.7.kv3
  95.0 13.2 %all_to_all.29.suf_ref = bf16[8,128,128]{2,1,0:T(8,128)(2,1)S(1)} all-to-all(bf16[8,128,128]{2,1,0:T(8,128)(2,1)S(1)} %shard_map.130), channel_id=1, replica_groups={{56,48,40,32,24,16,8,0},{57,49,41,33,25,17,9,1},{58,50,42,34,26,18,10,2..., dimensions={0} | all-to-all | bytes 524288 | tf_op jit(solution)/shard_map/all_to_all | solution.py:368
  108.3 15.5 %shard_map.131 = (bf16[512,8,128]{2,1,0:T(8,128)(2,1)}, bf16[512,8,128]{2,1,0:T(8,128)(2,1)}, bf16[512,8,128]{2,1,0:T(8,128)(2,1)}, bf16[512,8,128]{2,1,0:T(8,128)(2,1)}, bf16[512,8,128]{2,1,0:T(8,128)(2,1)}) custom-call(s32[1]{0:T(128)} %bitcast.pos_ref, bf16[4096,128]{1,0:T(8,128)(2,1)S(1)} %get-tuple-element.102.sq_ref, ...), custom_call_target="tpu_custom_call" | custom-call | flops 4831838208 | bytes 13893636 | tf_op jit(solution)/shard_map/pallas_call | solution.py:49
  (3 shorter events, 0.1 us)
Async XLA Ops:
  0.6 1.2 copy-start.2
  1.9 1.2 copy-start.3
  1.9 18.1 %copy-start.5 = (bf16[512,1,128]{2,0,1:T(8,128)(2,1)S(1)}, bf16[512,1,128]{2,0,1:T(8,128)(2,1)}, u32[]{:S(2)}) copy-start(bf16[512,1,128]{2,0,1:T(8,128)(2,1)} %param.14) | copy-start | bytes 393220
  1.9 18.1 %copy-start.6 = (bf16[512,1,128]{2,0,1:T(8,128)(2,1)S(1)}, bf16[512,1,128]{2,0,1:T(8,128)(2,1)}, u32[]{:S(2)}) copy-start(bf16[512,1,128]{2,0,1:T(8,128)(2,1)} %param.15) | copy-start | bytes 393220
  3.1 28.1 %copy-start = (bf16[512,8,128]{2,1,0:T(8,128)(2,1)S(1)}, bf16[512,8,128]{2,1,0:T(8,128)(2,1)}, u32[]{:S(2)}) copy-start(bf16[512,8,128]{2,1,0:T(8,128)(2,1)} %q_ref) | copy-start | bytes 3145732
  3.1 28.1 %copy-start.1 = (bf16[512,8,128]{2,1,0:T(8,128)(2,1)S(1)}, bf16[512,8,128]{2,1,0:T(8,128)(2,1)}, u32[]{:S(2)}) copy-start(bf16[512,8,128]{2,1,0:T(8,128)(2,1)} %c_ref) | copy-start | bytes 3145732
  3.1 28.1 %copy-start.7 = (f32[8,128]{1,0:T(8,128)S(1)}, f32[8,128]{1,0:T(8,128)}, u32[]{:S(2)}) copy-start(f32[8,128]{1,0:T(8,128)} %gain_ref.3) | copy-start | bytes 12292
  20.0 15.0 %collective-permute-start.3 = (bf16[2,512,128]{2,1,0:T(8,128)(2,1)S(1)}, bf16[2,512,128]{2,1,0:T(8,128)(2,1)S(1)}, u32[]{:S(2)}, u32[]{:S(2)}) collective-permute-start(bf16[2,512,128]{2,1,0:T(8,128)(2,1)S(1)} %get-tuple-element.68.kv0), channel_id=1, source_target_pairs={{0,8},{8,16},{16,24},{24,32},{32,40},{40,48},{48,56},{56,64},{64,7... | collective-permute-start | bytes 786440 | tf_op jit(solution)/shard_map/ppermute | solution.py:386
  24.4 9.4 %collective-permute-start.2 = (bf16[128,128]{1,0:T(8,128)(2,1)S(1)}, bf16[128,128]{1,0:T(8,128)(2,1)S(1)}, u32[]{:S(2)}, u32[]{:S(2)}) collective-permute-start(bf16[128,128]{1,0:T(8,128)(2,1)S(1)} %get-tuple-element.67), channel_id=1, source_target_pairs={{0,128},{64,192},{1,129},{65,193},{2,130},{66,194},{3,131},{67,195... | collective-permute-start | bytes 98312 | tf_op jit(solution)/shard_map/ppermute | solution.py:353
  28.6 5.2 %collective-permute-start.1 = (bf16[128,128]{1,0:T(8,128)(2,1)S(1)}, bf16[128,128]{1,0:T(8,128)(2,1)S(1)}, u32[]{:S(2)}, u32[]{:S(2)}) collective-permute-start(bf16[128,128]{1,0:T(8,128)(2,1)S(1)} %get-tuple-element.67), channel_id=1, source_target_pairs={{0,192},{1,193},{2,194},{3,195},{4,196},{5,197},{6,198},{7,199},{8... | collective-permute-start | bytes 98312 | tf_op jit(solution)/shard_map/ppermute | solution.py:353
  29.3 5.8 %collective-permute-start = (bf16[128,128]{1,0:T(8,128)(2,1)S(1)}, bf16[128,128]{1,0:T(8,128)(2,1)S(1)}, u32[]{:S(2)}, u32[]{:S(2)}) collective-permute-start(bf16[128,128]{1,0:T(8,128)(2,1)S(1)} %get-tuple-element.67), channel_id=1, source_target_pairs={{0,64},{64,128},{128,192},{1,65},{65,129},{129,193},{2,66},{66,130... | collective-permute-start | bytes 98312 | tf_op jit(solution)/shard_map/ppermute | solution.py:353
  48.4 13.6 %collective-permute-start.4 = (bf16[2,512,128]{2,1,0:T(8,128)(2,1)S(1)}, bf16[2,512,128]{2,1,0:T(8,128)(2,1)S(1)}, u32[]{:S(2)}, u32[]{:S(2)}) collective-permute-start(bf16[2,512,128]{2,1,0:T(8,128)(2,1)S(1)} %collective-permute-done.3.kv1), channel_id=1, source_target_pairs={{0,8},{8,16},{16,24},{24,32},{32,40},{40,48},{48,56},{56,64},{64,7... | collective-permute-start | bytes 786440 | tf_op jit(solution)/shard_map/ppermute | solution.py:386
  62.0 22.1 %copy-start.4 = (bf16[512,8,128]{2,1,0:T(8,128)(2,1)S(1)}, bf16[512,8,128]{2,1,0:T(8,128)(2,1)}, u32[]{:S(2)}) copy-start(bf16[512,8,128]{2,1,0:T(8,128)(2,1)} %q2_ref.1) | copy-start | bytes 3145732
  77.0 10.6 %collective-permute-start.5 = (bf16[128,128]{1,0:T(8,128)(2,1)S(1)}, bf16[128,128]{1,0:T(8,128)(2,1)S(1)}, u32[]{:S(2)}, u32[]{:S(2)}) collective-permute-start(bf16[128,128]{1,0:T(8,128)(2,1)S(1)} %shard_map.126.own_ref), channel_id=1, source_target_pairs={{64,0},{128,64},{192,128},{65,1},{129,65},{193,129},{66,2},{130,66... | collective-permute-start | bytes 98312 | tf_op jit(solution)/shard_map/ppermute | solution.py:353
  79.7 15.3 %collective-permute-start.7 = (bf16[2,512,128]{2,1,0:T(8,128)(2,1)S(1)}, bf16[2,512,128]{2,1,0:T(8,128)(2,1)S(1)}, u32[]{:S(2)}, u32[]{:S(2)}) collective-permute-start(bf16[2,512,128]{2,1,0:T(8,128)(2,1)S(1)} %collective-permute-done.4.kv2), channel_id=1, source_target_pairs={{0,8},{8,16},{16,24},{24,32},{32,40},{40,48},{48,56},{56,64},{64,7... | collective-permute-start | bytes 786440 | tf_op jit(solution)/shard_map/ppermute | solution.py:386
  87.7 7.3 %collective-permute-start.6 = (bf16[128,128]{1,0:T(8,128)(2,1)S(1)}, bf16[128,128]{1,0:T(8,128)(2,1)S(1)}, u32[]{:S(2)}, u32[]{:S(2)}) collective-permute-start(bf16[128,128]{1,0:T(8,128)(2,1)S(1)} %shard_map.128), channel_id=1, source_target_pairs={{128,0},{192,64},{129,1},{193,65},{130,2},{194,66},{131,3},{195,67... | collective-permute-start | bytes 98312 | tf_op jit(solution)/shard_map/ppermute | solution.py:353

commit v5 on v4

--- a/solution.py
+++ b/solution.py
@@ -177,18 +177,28 @@
     copies = fetch([(norm_ref, norm_hbm), (gq_ref, gq_hbm)], done_sems)
     pieces = grad_sems.shape[0]
     rows = tokens // pieces
-    for i in range(pieces):
-        part, flat = pl.ds(i * rows, rows), pl.ds(i * rows * heads, rows * heads)
-        for h in range(heads):
-            suf = suf_ref[h]
-            target = pl.ds(i * rows * heads + h, rows, stride=heads)
-            ks[target, :] = pk_ref[h, part].astype(f32) + nt(vh_ref[h, part], suf)
-            vs[target, :] = pv_ref[h, part].astype(f32) + nn(kh_ref[h, part], suf)
-        for src, buffer in ((ks, kb), (vs, vb)):
-            buffer[part] = src[flat, :].astype(bf16).reshape(rows, heads, width)
-        copies += fetch(
-            [(kb.at[part], gk_hbm.at[part]), (vb.at[part], gv_hbm.at[part])], grad_sems.at[i]
-        )
+
+    def grad_copies(i):
+        part = pl.ds(i * rows, rows)
+        pairs = ((kb, gk_hbm), (vb, gv_hbm))
+        return [
+            pltpu.make_async_copy(b.at[part], target.at[part], grad_sems.at[i, j])
+            for j, (b, target) in enumerate(pairs)
+        ]
+
+    def finish():
+        for i in range(pieces):
+            part, flat = pl.ds(i * rows, rows), pl.ds(i * rows * heads, rows * heads)
+            for h in range(heads):
+                suf = suf_ref[h]
+                target = pl.ds(i * rows * heads + h, rows, stride=heads)
+                ks[target, :] = pk_ref[h, part].astype(f32) + nt(vh_ref[h, part], suf)
+                vs[target, :] = pv_ref[h, part].astype(f32) + nn(kh_ref[h, part], suf)
+            for src, buffer in ((ks, kb), (vs, vb)):
+                buffer[part] = src[flat, :].astype(bf16).reshape(rows, heads, width)
+            for copy in grad_copies(i):
+                copy.start()
+
     scale = LOG2E * HEAD_WIDTH ** (-0.5)
     ones = jnp.ones((tokens, width), bf16)
     quarters = 4
@@ -224,6 +234,7 @@
         return pltpu.make_async_copy(out.at[part], out_hbm.at[part], sems.at[i])
 
     def run(count):
+        finish()
         rows = 256
         per = quarter * heads // rows
 
@@ -254,6 +265,7 @@
             return carry
 
         put(0, 0)
+        finish()
         lax.fori_loop(0, quarters, body, 0)
 
     have = pos_ref[0]
@@ -262,6 +274,8 @@
     pl.when(have == WINDOW_BLOCKS - 1)(run_ahead)
     for i in range(quarters):
         store(i).wait()
+    for i in range(pieces):
+        copies += grad_copies(i)
     for copy in copies:
         copy.wait()
 

time: 125 us -> 125 us (level)
  no operation moved by 1% of the time
where the time goes in v5:
time: 125 us; the launch traced here: 124 us
  blocking collectives  65.8 us (53%)
  Pallas kernels  29.5 us (24%)
  starting transfers between devices  22.6 us (18%)
  waiting for transfers between devices  2.81 us (2%)
  local copies, waits for them, and re-layouts  1.87 us (1%)
    all_to_all x4, blocking collectives, spread(): return lax.all_to_all(x, 'z', 0, 0, tiled=True, axis_index_groups=[members])  56.2 us
    pallas_call x13, Pallas kernels, call(): pl.pallas_call(kernel, out_shape=out_shapes, in_specs=specs, out_specs=[p...  29.5 us
    ppermute x3, starting transfers between devices, onward(): return lax.ppermute(x, CTX, [(i, i + 1) for i in range(ring - 1)])  11.7 us
    ppermute x5, starting transfers between devices, from_row(): lax.ppermute(x, 'y', [(i + d, i) if back else (i, i + d) for i in range(r...  10.9 us
    all_to_all x1, blocking collectives, local(): gathered = lax.all_to_all(part, HEADS, 0, 0, tiled=True)  9.57 us
    ppermute x5, waiting for transfers between devices, from_row(): lax.ppermute(x, 'y', [(i + d, i) if back else (i, i + d) for i in range(r...  2.81 us
  transfers between devices with their start and end apart: 8, of which 2 were waited for; matrix products, arithmetic and copies ran while one was open for 0% of the time, Pallas kernels for 9%

profile of v5, /device:TPU:8, one launch (start us, length us, event | category | flops | bytes accessed | tf_op | source)
XLA Modules:
  0.0 123.6 jit_solution(17099649492812710421)
XLA Ops:
  0.6 0.0 copy-start.2
  0.7 1.2 copy-done.2
  1.9 0.0 copy-start.3
  1.9 0.0 copy-start.5
  1.9 0.0 copy-start.6
  1.9 0.6 shard_map.119.kh_ref
  2.5 0.6 copy-done.3
  3.1 0.0 copy-start
  3.1 0.0 copy-start.1
  3.1 0.0 copy-start.7
  3.1 0.9 shard_map.120
  4.1 15.9 %all_to_all.25.recv_ref = bf16[8,128,128]{2,1,0:T(8,128)(2,1)S(1)} all-to-all(bf16[8,128,128]{2,1,0:T(8,128)(2,1)S(1)} %get-tuple-element.61), channel_id=1, replica_groups={{56,48,40,32,24,16,8,0},{57,49,41,33,25,17,9,1},{58,50,42,34,26,18,10,2..., dimensions={0} | all-to-all | bytes 524288 | tf_op jit(solution)/shard_map/all_to_all | solution.py:382
  20.0 0.0 copy-done.5
  20.0 0.0 copy-done.6
  20.0 0.1 shard_map.121
  20.0 4.3 %collective-permute-start.3 = (bf16[2,512,128]{2,1,0:T(8,128)(2,1)S(1)}, bf16[2,512,128]{2,1,0:T(8,128)(2,1)S(1)}, u32[]{:S(2)}, u32[]{:S(2)}) collective-permute-start(bf16[2,512,128]{2,1,0:T(8,128)(2,1)S(1)} %get-tuple-element.68.kv0), channel_id=1, source_target_pairs={{0,8},{8,16},{16,24},{24,32},{32,40},{40,48},{48,56},{56,64},{64,7... | collective-permute-start | bytes 786440 | tf_op jit(solution)/shard_map/ppermute | solution.py:400
  24.4 4.2 %collective-permute-start.2 = (bf16[128,128]{1,0:T(8,128)(2,1)S(1)}, bf16[128,128]{1,0:T(8,128)(2,1)S(1)}, u32[]{:S(2)}, u32[]{:S(2)}) collective-permute-start(bf16[128,128]{1,0:T(8,128)(2,1)S(1)} %get-tuple-element.67), channel_id=1, source_target_pairs={{0,128},{64,192},{1,129},{65,193},{2,130},{66,194},{3,131},{67,195... | collective-permute-start | bytes 98312 | tf_op jit(solution)/shard_map/ppermute | solution.py:367
  28.6 0.7 collective-permute-start.1
  29.3 1.9 %collective-permute-start = (bf16[128,128]{1,0:T(8,128)(2,1)S(1)}, bf16[128,128]{1,0:T(8,128)(2,1)S(1)}, u32[]{:S(2)}, u32[]{:S(2)}) collective-permute-start(bf16[128,128]{1,0:T(8,128)(2,1)S(1)} %get-tuple-element.67), channel_id=1, source_target_pairs={{0,64},{64,128},{128,192},{1,65},{65,129},{129,193},{2,66},{66,130... | collective-permute-start | bytes 98312 | tf_op jit(solution)/shard_map/ppermute | solution.py:367
  31.2 0.0 copy-done
  31.2 0.0 copy-done.1
  31.2 0.0 copy-done.7
  31.2 2.6 %shard_map.122 = (bf16[8,512,128]{2,1,0:T(8,128)(2,1)S(1)}, f32[8,512,128]{2,1,0:T(8,128)S(1)}, f32[8,512,128]{2,1,0:T(8,128)S(1)}) custom-call(bf16[512,8,128]{2,1,0:T(8,128)(2,1)S(1)} %copy-done, bf16[512,8,128]{2,1,0:T(8,128)(2,1)S(1)} %copy-done.1, f32[8,128]{1,0:T(8,128)S(1)} %copy-done.7, bf16[8,512,128]{2,1,0:T(8,128)(2,1)S(1)} %shard_map.119.kh_ref, ...), custom_call_target="tpu_custom_call" | custom-call | flops 1073741824 | bytes 9441280 | tf_op jit(solution)/shard_map/pallas_call | solution.py:49
  33.8 0.0 collective-permute-done.2.refs_2_
  33.8 0.0 collective-permute-done.1.refs_1_
  33.8 1.2 collective-permute-done.refs_0_
  35.1 0.0 collective-permute-done.3.kv1
  35.1 0.1 shard_map.123
  35.1 13.3 %all_to_all.26.pre_ref = bf16[8,128,128]{2,1,0:T(8,128)(2,1)S(1)} all-to-all(bf16[8,128,128]{2,1,0:T(8,128)(2,1)S(1)} %shard_map.123), channel_id=1, replica_groups={{56,48,40,32,24,16,8,0},{57,49,41,33,25,17,9,1},{58,50,42,34,26,18,10,2..., dimensions={0} | all-to-all | bytes 524288 | tf_op jit(solution)/shard_map/all_to_all | solution.py:382
  48.4 3.1 %collective-permute-start.4 = (bf16[2,512,128]{2,1,0:T(8,128)(2,1)S(1)}, bf16[2,512,128]{2,1,0:T(8,128)(2,1)S(1)}, u32[]{:S(2)}, u32[]{:S(2)}) collective-permute-start(bf16[2,512,128]{2,1,0:T(8,128)(2,1)S(1)} %collective-permute-done.3.kv1), channel_id=1, source_target_pairs={{0,8},{8,16},{16,24},{24,32},{32,40},{40,48},{48,56},{56,64},{64,7... | collective-permute-start | bytes 786440 | tf_op jit(solution)/shard_map/ppermute | solution.py:400
  51.5 0.9 shard_map.124
  52.4 9.6 %all_to_all.27.g_ref = f32[8,2,512]{2,1,0:T(2,128)S(1)} all-to-all(f32[8,2,512]{2,1,0:T(2,128)S(1)} %get-tuple-element.82), channel_id=1, replica_groups=mesh['y'=4,'z'=8,'x'=4,'core'=2] {'x','core'}, dimensions={0} | all-to-all | bytes 65536 | tf_op jit(solution)/shard_map/all_to_all | solution.py:440
  62.0 0.0 collective-permute-done.4.kv2
  62.0 0.0 copy-start.4
  62.0 1.2 %shard_map.125 = (bf16[8,512,128]{2,1,0:T(8,128)(2,1)S(1)}, bf16[8,128,128]{2,1,0:T(8,128)(2,1)S(1)}, f32[512,128]{1,0:T(8,128)S(1)}) custom-call(f32[8,2,512]{2,1,0:T(2,128)S(1)} %all_to_all.27.g_ref, f32[8,512,128]{2,1,0:T(8,128)S(1)} %get-tuple-element.92.att_ref, f32[8,512,128]{2,1,0:T(8,128)S(1)} %get-tuple-element.76.gh_ref, ...), custom_call_target="tpu_custom_call" | custom-call | flops 134217728 | bytes 6848512 | tf_op jit(solution)/shard_map/pallas_call | solution.py:49
  63.2 13.8 %all_to_all.28.recv_ref = bf16[8,128,128]{2,1,0:T(8,128)(2,1)S(1)} all-to-all(bf16[8,128,128]{2,1,0:T(8,128)(2,1)S(1)} %get-tuple-element.86), channel_id=1, replica_groups={{56,48,40,32,24,16,8,0},{57,49,41,33,25,17,9,1},{58,50,42,34,26,18,10,2..., dimensions={0} | all-to-all | bytes 524288 | tf_op jit(solution)/shard_map/all_to_all | solution.py:382
  77.0 2.7 %collective-permute-start.5 = (bf16[128,128]{1,0:T(8,128)(2,1)S(1)}, bf16[128,128]{1,0:T(8,128)(2,1)S(1)}, u32[]{:S(2)}, u32[]{:S(2)}) collective-permute-start(bf16[128,128]{1,0:T(8,128)(2,1)S(1)} %shard_map.126.own_ref), channel_id=1, source_target_pairs={{64,0},{128,64},{192,128},{65,1},{129,65},{193,129},{66,2},{130,66... | collective-permute-start | bytes 98312 | tf_op jit(solution)/shard_map/ppermute | solution.py:367
  79.7 4.3 %collective-permute-start.7 = (bf16[2,512,128]{2,1,0:T(8,128)(2,1)S(1)}, bf16[2,512,128]{2,1,0:T(8,128)(2,1)S(1)}, u32[]{:S(2)}, u32[]{:S(2)}) collective-permute-start(bf16[2,512,128]{2,1,0:T(8,128)(2,1)S(1)} %collective-permute-done.4.kv2), channel_id=1, source_target_pairs={{0,8},{8,16},{16,24},{24,32},{32,40},{40,48},{48,56},{56,64},{64,7... | collective-permute-start | bytes 786440 | tf_op jit(solution)/shard_map/ppermute | solution.py:400
  84.0 0.0 copy-done.4
  84.1 3.6 %shard_map.127 = (bf16[512,8,128]{2,1,0:T(8,128)(2,1)S(1)}, bf16[512,8,128]{2,1,0:T(8,128)(2,1)S(1)}, bf16[4096,128]{1,0:T(8,128)(2,1)S(1)}) custom-call(bf16[8,512,128]{2,1,0:T(8,128)(2,1)S(1)} %shard_map.119.kh_ref, bf16[8,512,128]{2,1,0:T(8,128)(2,1)S(1)} %get-tuple-element.72.vh_ref, bf16[8,512,128]{2,1,0:T(8,128)(2,1)S(1)} %get-tuple-element.96.da_ref, ...), custom_call_target="tpu_custom_call" | custom-call | flops 1073741824 | bytes 9965568 | tf_op jit(solution)/shard_map/pallas_call | solution.py:49
  87.6 0.0 collective-permute-done.5.other_ref.refs_0_
  87.7 1.5 %collective-permute-start.6 = (bf16[128,128]{1,0:T(8,128)(2,1)S(1)}, bf16[128,128]{1,0:T(8,128)(2,1)S(1)}, u32[]{:S(2)}, u32[]{:S(2)}) collective-permute-start(bf16[128,128]{1,0:T(8,128)(2,1)S(1)} %shard_map.128), channel_id=1, source_target_pairs={{128,0},{192,64},{129,1},{193,65},{130,2},{194,66},{131,3},{195,67... | collective-permute-start | bytes 98312 | tf_op jit(solution)/shard_map/ppermute | solution.py:367
  89.1 4.3 %shard_map.129 = (bf16[8,512,128]{2,1,0:T(8,128)(2,1)S(1)}, bf16[8,512,128]{2,1,0:T(8,128)(2,1)S(1)}) custom-call(bf16[8,512,128]{2,1,0:T(8,128)(2,1)S(1)} %get-tuple-element.75.qh_ref, bf16[8,512,128]{2,1,0:T(8,128)(2,1)S(1)} %shard_map.119.kh_ref, bf16[8,512,128]{2,1,0:T(8,128)(2,1)S(1)} %get-tuple-element.72.vh_ref, ...), custom_call_target="tpu_custom_call" | custom-call | flops 2147483648 | bytes 6291456 | tf_op jit(solution)/shard_map/pallas_call | solution.py:49
  93.4 1.6 %collective-permute-done.6.refs_1_ = bf16[128,128]{1,0:T(8,128)(2,1)S(1)} collective-permute-done((bf16[128,128]{1,0:T(8,128)(2,1)S(1)}, bf16[128,128]{1,0:T(8,128)(2,1)S(1)}, u32[]{:S(2)}, u32[]{:S(2)}) %collective-permute-start.6) | collective-permute-done | bytes 32800 | tf_op jit(solution)/shard_map/ppermute | solution.py:367
  95.0 0.0 collective-permute-done.7.kv3
  95.0 13.2 %all_to_all.29.suf_ref = bf16[8,128,128]{2,1,0:T(8,128)(2,1)S(1)} all-to-all(bf16[8,128,128]{2,1,0:T(8,128)(2,1)S(1)} %shard_map.130), channel_id=1, replica_groups={{56,48,40,32,24,16,8,0},{57,49,41,33,25,17,9,1},{58,50,42,34,26,18,10,2..., dimensions={0} | all-to-all | bytes 524288 | tf_op jit(solution)/shard_map/all_to_all | solution.py:382
  108.3 15.2 %shard_map.131 = (bf16[512,8,128]{2,1,0:T(8,128)(2,1)}, bf16[512,8,128]{2,1,0:T(8,128)(2,1)}, bf16[512,8,128]{2,1,0:T(8,128)(2,1)}, bf16[512,8,128]{2,1,0:T(8,128)(2,1)}, bf16[512,8,128]{2,1,0:T(8,128)(2,1)}) custom-call(s32[1]{0:T(128)} %bitcast.pos_ref, bf16[4096,128]{1,0:T(8,128)(2,1)S(1)} %get-tuple-element.102.sq_ref, ...), custom_call_target="tpu_custom_call" | custom-call | flops 4831838208 | bytes 13893636 | tf_op jit(solution)/shard_map/pallas_call | solution.py:49
  (3 shorter events, 0.1 us)
Async XLA Ops:
  0.6 1.2 copy-start.2
  1.9 1.2 copy-start.3
  1.9 18.1 %copy-start.5 = (bf16[512,1,128]{2,0,1:T(8,128)(2,1)S(1)}, bf16[512,1,128]{2,0,1:T(8,128)(2,1)}, u32[]{:S(2)}) copy-start(bf16[512,1,128]{2,0,1:T(8,128)(2,1)} %param.14) | copy-start | bytes 393220
  1.9 18.1 %copy-start.6 = (bf16[512,1,128]{2,0,1:T(8,128)(2,1)S(1)}, bf16[512,1,128]{2,0,1:T(8,128)(2,1)}, u32[]{:S(2)}) copy-start(bf16[512,1,128]{2,0,1:T(8,128)(2,1)} %param.15) | copy-start | bytes 393220
  3.1 28.1 %copy-start = (bf16[512,8,128]{2,1,0:T(8,128)(2,1)S(1)}, bf16[512,8,128]{2,1,0:T(8,128)(2,1)}, u32[]{:S(2)}) copy-start(bf16[512,8,128]{2,1,0:T(8,128)(2,1)} %q_ref) | copy-start | bytes 3145732
  3.1 28.1 %copy-start.1 = (bf16[512,8,128]{2,1,0:T(8,128)(2,1)S(1)}, bf16[512,8,128]{2,1,0:T(8,128)(2,1)}, u32[]{:S(2)}) copy-start(bf16[512,8,128]{2,1,0:T(8,128)(2,1)} %c_ref) | copy-start | bytes 3145732
  3.1 28.1 %copy-start.7 = (f32[8,128]{1,0:T(8,128)S(1)}, f32[8,128]{1,0:T(8,128)}, u32[]{:S(2)}) copy-start(f32[8,128]{1,0:T(8,128)} %gain_ref.3) | copy-start | bytes 12292
  20.0 15.0 %collective-permute-start.3 = (bf16[2,512,128]{2,1,0:T(8,128)(2,1)S(1)}, bf16[2,512,128]{2,1,0:T(8,128)(2,1)S(1)}, u32[]{:S(2)}, u32[]{:S(2)}) collective-permute-start(bf16[2,512,128]{2,1,0:T(8,128)(2,1)S(1)} %get-tuple-element.68.kv0), channel_id=1, source_target_pairs={{0,8},{8,16},{16,24},{24,32},{32,40},{40,48},{48,56},{56,64},{64,7... | collective-permute-start | bytes 786440 | tf_op jit(solution)/shard_map/ppermute | solution.py:400
  24.4 9.4 %collective-permute-start.2 = (bf16[128,128]{1,0:T(8,128)(2,1)S(1)}, bf16[128,128]{1,0:T(8,128)(2,1)S(1)}, u32[]{:S(2)}, u32[]{:S(2)}) collective-permute-start(bf16[128,128]{1,0:T(8,128)(2,1)S(1)} %get-tuple-element.67), channel_id=1, source_target_pairs={{0,128},{64,192},{1,129},{65,193},{2,130},{66,194},{3,131},{67,195... | collective-permute-start | bytes 98312 | tf_op jit(solution)/shard_map/ppermute | solution.py:367
  28.6 5.2 %collective-permute-start.1 = (bf16[128,128]{1,0:T(8,128)(2,1)S(1)}, bf16[128,128]{1,0:T(8,128)(2,1)S(1)}, u32[]{:S(2)}, u32[]{:S(2)}) collective-permute-start(bf16[128,128]{1,0:T(8,128)(2,1)S(1)} %get-tuple-element.67), channel_id=1, source_target_pairs={{0,192},{1,193},{2,194},{3,195},{4,196},{5,197},{6,198},{7,199},{8... | collective-permute-start | bytes 98312 | tf_op jit(solution)/shard_map/ppermute | solution.py:367
  29.3 5.8 %collective-permute-start = (bf16[128,128]{1,0:T(8,128)(2,1)S(1)}, bf16[128,128]{1,0:T(8,128)(2,1)S(1)}, u32[]{:S(2)}, u32[]{:S(2)}) collective-permute-start(bf16[128,128]{1,0:T(8,128)(2,1)S(1)} %get-tuple-element.67), channel_id=1, source_target_pairs={{0,64},{64,128},{128,192},{1,65},{65,129},{129,193},{2,66},{66,130... | collective-permute-start | bytes 98312 | tf_op jit(solution)/shard_map/ppermute | solution.py:367
  48.4 13.6 %collective-permute-start.4 = (bf16[2,512,128]{2,1,0:T(8,128)(2,1)S(1)}, bf16[2,512,128]{2,1,0:T(8,128)(2,1)S(1)}, u32[]{:S(2)}, u32[]{:S(2)}) collective-permute-start(bf16[2,512,128]{2,1,0:T(8,128)(2,1)S(1)} %collective-permute-done.3.kv1), channel_id=1, source_target_pairs={{0,8},{8,16},{16,24},{24,32},{32,40},{40,48},{48,56},{56,64},{64,7... | collective-permute-start | bytes 786440 | tf_op jit(solution)/shard_map/ppermute | solution.py:400
  62.0 22.1 %copy-start.4 = (bf16[512,8,128]{2,1,0:T(8,128)(2,1)S(1)}, bf16[512,8,128]{2,1,0:T(8,128)(2,1)}, u32[]{:S(2)}) copy-start(bf16[512,8,128]{2,1,0:T(8,128)(2,1)} %q2_ref.1) | copy-start | bytes 3145732
  77.0 10.6 %collective-permute-start.5 = (bf16[128,128]{1,0:T(8,128)(2,1)S(1)}, bf16[128,128]{1,0:T(8,128)(2,1)S(1)}, u32[]{:S(2)}, u32[]{:S(2)}) collective-permute-start(bf16[128,128]{1,0:T(8,128)(2,1)S(1)} %shard_map.126.own_ref), channel_id=1, source_target_pairs={{64,0},{128,64},{192,128},{65,1},{129,65},{193,129},{66,2},{130,66... | collective-permute-start | bytes 98312 | tf_op jit(solution)/shard_map/ppermute | solution.py:367
  79.7 15.3 %collective-permute-start.7 = (bf16[2,512,128]{2,1,0:T(8,128)(2,1)S(1)}, bf16[2,512,128]{2,1,0:T(8,128)(2,1)S(1)}, u32[]{:S(2)}, u32[]{:S(2)}) collective-permute-start(bf16[2,512,128]{2,1,0:T(8,128)(2,1)S(1)} %collective-permute-done.4.kv2), channel_id=1, source_target_pairs={{0,8},{8,16},{16,24},{24,32},{32,40},{40,48},{48,56},{56,64},{64,7... | collective-permute-start | bytes 786440 | tf_op jit(solution)/shard_map/ppermute | solution.py:400
  87.7 7.3 %collective-permute-start.6 = (bf16[128,128]{1,0:T(8,128)(2,1)S(1)}, bf16[128,128]{1,0:T(8,128)(2,1)S(1)}, u32[]{:S(2)}, u32[]{:S(2)}) collective-permute-start(bf16[128,128]{1,0:T(8,128)(2,1)S(1)} %shard_map.128), channel_id=1, source_target_pairs={{128,0},{192,64},{129,1},{193,65},{130,2},{194,66},{131,3},{195,67... | collective-permute-start | bytes 98312 | tf_op jit(solution)/shard_map/ppermute | solution.py:367

commit v6 on v5

--- a/solution.py
+++ b/solution.py
@@ -201,7 +201,7 @@
 
     scale = LOG2E * HEAD_WIDTH ** (-0.5)
     ones = jnp.ones((tokens, width), bf16)
-    quarters = 4
+    quarters = 8
     quarter = tokens // quarters
 
     def scores(chunk, rows, count):
@@ -248,9 +248,9 @@
         lax.fori_loop(0, quarters, body, 0)
 
     def run_ahead():
-        rows = 512
-        per = quarter * heads // rows
-        last = quarters * per - 1
+        rows = quarter * heads
+        per = 2
+        last = quarters - 1
 
         def put(slot, chunk):
             for b, s in enumerate(scores(chunk, rows, WINDOW_BLOCKS)):
@@ -261,12 +261,12 @@
                 chunk = i * per + j
                 put((j + 1) % 2, jnp.minimum(chunk + 1, last))
                 weigh([ahead[j % 2, b] for b in range(WINDOW_BLOCKS)], chunk, rows)
-            store(i).start()
+                store(chunk).start()
             return carry
 
         put(0, 0)
         finish()
-        lax.fori_loop(0, quarters, body, 0)
+        lax.fori_loop(0, quarters // per, body, 0)
 
     have = pos_ref[0]
     for count in range(1, WINDOW_BLOCKS):
@@ -475,7 +475,7 @@
             flat_buffer,
             token_buffer,
             token_buffer,
-            sems(4),
+            sems(8),
             sems(2),
             pltpu.SemaphoreType.DMA((4, 2)),
         ],

time: 125 us -> 125 us (level)
  no operation moved by 1% of the time
where the time goes in v6:
time: 125 us; the launch traced here: 124 us
  blocking collectives  65.8 us (53%)
  Pallas kernels  29.5 us (24%)
  starting transfers between devices  22.6 us (18%)
  waiting for transfers between devices  2.81 us (2%)
  local copies, waits for them, and re-layouts  1.87 us (1%)
    all_to_all x4, blocking collectives, spread(): return lax.all_to_all(x, 'z', 0, 0, tiled=True, axis_index_groups=[members])  56.2 us
    pallas_call x13, Pallas kernels, call(): pl.pallas_call(kernel, out_shape=out_shapes, in_specs=specs, out_specs=[p...  29.5 us
    ppermute x3, starting transfers between devices, onward(): return lax.ppermute(x, CTX, [(i, i + 1) for i in range(ring - 1)])  11.7 us
    ppermute x5, starting transfers between devices, from_row(): lax.ppermute(x, 'y', [(i + d, i) if back else (i, i + d) for i in range(r...  10.9 us
    all_to_all x1, blocking collectives, local(): gathered = lax.all_to_all(part, HEADS, 0, 0, tiled=True)  9.57 us
    ppermute x5, waiting for transfers between devices, from_row(): lax.ppermute(x, 'y', [(i + d, i) if back else (i, i + d) for i in range(r...  2.81 us
  transfers between devices with their start and end apart: 8, of which 2 were waited for; matrix products, arithmetic and copies ran while one was open for 0% of the time, Pallas kernels for 9%

profile of v6, /device:TPU:8, one launch (start us, length us, event | category | flops | bytes accessed | tf_op | source)
XLA Modules:
  0.0 123.6 jit_solution(13966766380862113564)
XLA Ops:
  0.6 0.0 copy-start.2
  0.7 1.2 copy-done.2
  1.9 0.0 copy-start.3
  1.9 0.0 copy-start.5
  1.9 0.0 copy-start.6
  1.9 0.6 shard_map.119.kh_ref
  2.5 0.6 copy-done.3
  3.1 0.0 copy-start
  3.1 0.0 copy-start.1
  3.1 0.0 copy-start.7
  3.1 0.9 shard_map.120
  4.1 15.9 %all_to_all.25.recv_ref = bf16[8,128,128]{2,1,0:T(8,128)(2,1)S(1)} all-to-all(bf16[8,128,128]{2,1,0:T(8,128)(2,1)S(1)} %get-tuple-element.61), channel_id=1, replica_groups={{56,48,40,32,24,16,8,0},{57,49,41,33,25,17,9,1},{58,50,42,34,26,18,10,2..., dimensions={0} | all-to-all | bytes 524288 | tf_op jit(solution)/shard_map/all_to_all | solution.py:382
  20.0 0.0 copy-done.5
  20.0 0.0 copy-done.6
  20.0 0.1 shard_map.121
  20.0 4.3 %collective-permute-start.3 = (bf16[2,512,128]{2,1,0:T(8,128)(2,1)S(1)}, bf16[2,512,128]{2,1,0:T(8,128)(2,1)S(1)}, u32[]{:S(2)}, u32[]{:S(2)}) collective-permute-start(bf16[2,512,128]{2,1,0:T(8,128)(2,1)S(1)} %get-tuple-element.68.kv0), channel_id=1, source_target_pairs={{0,8},{8,16},{16,24},{24,32},{32,40},{40,48},{48,56},{56,64},{64,7... | collective-permute-start | bytes 786440 | tf_op jit(solution)/shard_map/ppermute | solution.py:400
  24.4 4.2 %collective-permute-start.2 = (bf16[128,128]{1,0:T(8,128)(2,1)S(1)}, bf16[128,128]{1,0:T(8,128)(2,1)S(1)}, u32[]{:S(2)}, u32[]{:S(2)}) collective-permute-start(bf16[128,128]{1,0:T(8,128)(2,1)S(1)} %get-tuple-element.67), channel_id=1, source_target_pairs={{0,128},{64,192},{1,129},{65,193},{2,130},{66,194},{3,131},{67,195... | collective-permute-start | bytes 98312 | tf_op jit(solution)/shard_map/ppermute | solution.py:367
  28.6 0.7 collective-permute-start.1
  29.3 1.9 %collective-permute-start = (bf16[128,128]{1,0:T(8,128)(2,1)S(1)}, bf16[128,128]{1,0:T(8,128)(2,1)S(1)}, u32[]{:S(2)}, u32[]{:S(2)}) collective-permute-start(bf16[128,128]{1,0:T(8,128)(2,1)S(1)} %get-tuple-element.67), channel_id=1, source_target_pairs={{0,64},{64,128},{128,192},{1,65},{65,129},{129,193},{2,66},{66,130... | collective-permute-start | bytes 98312 | tf_op jit(solution)/shard_map/ppermute | solution.py:367
  31.2 0.0 copy-done
  31.2 0.0 copy-done.1
  31.2 0.0 copy-done.7
  31.2 2.6 %shard_map.122 = (bf16[8,512,128]{2,1,0:T(8,128)(2,1)S(1)}, f32[8,512,128]{2,1,0:T(8,128)S(1)}, f32[8,512,128]{2,1,0:T(8,128)S(1)}) custom-call(bf16[512,8,128]{2,1,0:T(8,128)(2,1)S(1)} %copy-done, bf16[512,8,128]{2,1,0:T(8,128)(2,1)S(1)} %copy-done.1, f32[8,128]{1,0:T(8,128)S(1)} %copy-done.7, bf16[8,512,128]{2,1,0:T(8,128)(2,1)S(1)} %shard_map.119.kh_ref, ...), custom_call_target="tpu_custom_call" | custom-call | flops 1073741824 | bytes 9441280 | tf_op jit(solution)/shard_map/pallas_call | solution.py:49
  33.8 0.0 collective-permute-done.2.refs_2_
  33.8 0.0 collective-permute-done.1.refs_1_
  33.8 1.2 collective-permute-done.refs_0_
  35.1 0.0 collective-permute-done.3.kv1
  35.1 0.1 shard_map.123
  35.1 13.3 %all_to_all.26.pre_ref = bf16[8,128,128]{2,1,0:T(8,128)(2,1)S(1)} all-to-all(bf16[8,128,128]{2,1,0:T(8,128)(2,1)S(1)} %shard_map.123), channel_id=1, replica_groups={{56,48,40,32,24,16,8,0},{57,49,41,33,25,17,9,1},{58,50,42,34,26,18,10,2..., dimensions={0} | all-to-all | bytes 524288 | tf_op jit(solution)/shard_map/all_to_all | solution.py:382
  48.4 3.1 %collective-permute-start.4 = (bf16[2,512,128]{2,1,0:T(8,128)(2,1)S(1)}, bf16[2,512,128]{2,1,0:T(8,128)(2,1)S(1)}, u32[]{:S(2)}, u32[]{:S(2)}) collective-permute-start(bf16[2,512,128]{2,1,0:T(8,128)(2,1)S(1)} %collective-permute-done.3.kv1), channel_id=1, source_target_pairs={{0,8},{8,16},{16,24},{24,32},{32,40},{40,48},{48,56},{56,64},{64,7... | collective-permute-start | bytes 786440 | tf_op jit(solution)/shard_map/ppermute | solution.py:400
  51.5 0.9 shard_map.124
  52.4 9.6 %all_to_all.27.g_ref = f32[8,2,512]{2,1,0:T(2,128)S(1)} all-to-all(f32[8,2,512]{2,1,0:T(2,128)S(1)} %get-tuple-element.82), channel_id=1, replica_groups=mesh['y'=4,'z'=8,'x'=4,'core'=2] {'x','core'}, dimensions={0} | all-to-all | bytes 65536 | tf_op jit(solution)/shard_map/all_to_all | solution.py:440
  62.0 0.0 collective-permute-done.4.kv2
  62.0 0.0 copy-start.4
  62.0 1.2 %shard_map.125 = (bf16[8,512,128]{2,1,0:T(8,128)(2,1)S(1)}, bf16[8,128,128]{2,1,0:T(8,128)(2,1)S(1)}, f32[512,128]{1,0:T(8,128)S(1)}) custom-call(f32[8,2,512]{2,1,0:T(2,128)S(1)} %all_to_all.27.g_ref, f32[8,512,128]{2,1,0:T(8,128)S(1)} %get-tuple-element.92.att_ref, f32[8,512,128]{2,1,0:T(8,128)S(1)} %get-tuple-element.76.gh_ref, ...), custom_call_target="tpu_custom_call" | custom-call | flops 134217728 | bytes 6848512 | tf_op jit(solution)/shard_map/pallas_call | solution.py:49
  63.2 13.8 %all_to_all.28.recv_ref = bf16[8,128,128]{2,1,0:T(8,128)(2,1)S(1)} all-to-all(bf16[8,128,128]{2,1,0:T(8,128)(2,1)S(1)} %get-tuple-element.86), channel_id=1, replica_groups={{56,48,40,32,24,16,8,0},{57,49,41,33,25,17,9,1},{58,50,42,34,26,18,10,2..., dimensions={0} | all-to-all | bytes 524288 | tf_op jit(solution)/shard_map/all_to_all | solution.py:382
  77.0 2.7 %collective-permute-start.5 = (bf16[128,128]{1,0:T(8,128)(2,1)S(1)}, bf16[128,128]{1,0:T(8,128)(2,1)S(1)}, u32[]{:S(2)}, u32[]{:S(2)}) collective-permute-start(bf16[128,128]{1,0:T(8,128)(2,1)S(1)} %shard_map.126.own_ref), channel_id=1, source_target_pairs={{64,0},{128,64},{192,128},{65,1},{129,65},{193,129},{66,2},{130,66... | collective-permute-start | bytes 98312 | tf_op jit(solution)/shard_map/ppermute | solution.py:367
  79.7 4.3 %collective-permute-start.7 = (bf16[2,512,128]{2,1,0:T(8,128)(2,1)S(1)}, bf16[2,512,128]{2,1,0:T(8,128)(2,1)S(1)}, u32[]{:S(2)}, u32[]{:S(2)}) collective-permute-start(bf16[2,512,128]{2,1,0:T(8,128)(2,1)S(1)} %collective-permute-done.4.kv2), channel_id=1, source_target_pairs={{0,8},{8,16},{16,24},{24,32},{32,40},{40,48},{48,56},{56,64},{64,7... | collective-permute-start | bytes 786440 | tf_op jit(solution)/shard_map/ppermute | solution.py:400
  84.0 0.0 copy-done.4
  84.1 3.6 %shard_map.127 = (bf16[512,8,128]{2,1,0:T(8,128)(2,1)S(1)}, bf16[512,8,128]{2,1,0:T(8,128)(2,1)S(1)}, bf16[4096,128]{1,0:T(8,128)(2,1)S(1)}) custom-call(bf16[8,512,128]{2,1,0:T(8,128)(2,1)S(1)} %shard_map.119.kh_ref, bf16[8,512,128]{2,1,0:T(8,128)(2,1)S(1)} %get-tuple-element.72.vh_ref, bf16[8,512,128]{2,1,0:T(8,128)(2,1)S(1)} %get-tuple-element.96.da_ref, ...), custom_call_target="tpu_custom_call" | custom-call | flops 1073741824 | bytes 9965568 | tf_op jit(solution)/shard_map/pallas_call | solution.py:49
  87.6 0.0 collective-permute-done.5.other_ref.refs_0_
  87.7 1.5 %collective-permute-start.6 = (bf16[128,128]{1,0:T(8,128)(2,1)S(1)}, bf16[128,128]{1,0:T(8,128)(2,1)S(1)}, u32[]{:S(2)}, u32[]{:S(2)}) collective-permute-start(bf16[128,128]{1,0:T(8,128)(2,1)S(1)} %shard_map.128), channel_id=1, source_target_pairs={{128,0},{192,64},{129,1},{193,65},{130,2},{194,66},{131,3},{195,67... | collective-permute-start | bytes 98312 | tf_op jit(solution)/shard_map/ppermute | solution.py:367
  89.1 4.3 %shard_map.129 = (bf16[8,512,128]{2,1,0:T(8,128)(2,1)S(1)}, bf16[8,512,128]{2,1,0:T(8,128)(2,1)S(1)}) custom-call(bf16[8,512,128]{2,1,0:T(8,128)(2,1)S(1)} %get-tuple-element.75.qh_ref, bf16[8,512,128]{2,1,0:T(8,128)(2,1)S(1)} %shard_map.119.kh_ref, bf16[8,512,128]{2,1,0:T(8,128)(2,1)S(1)} %get-tuple-element.72.vh_ref, ...), custom_call_target="tpu_custom_call" | custom-call | flops 2147483648 | bytes 6291456 | tf_op jit(solution)/shard_map/pallas_call | solution.py:49
  93.4 1.6 %collective-permute-done.6.refs_1_ = bf16[128,128]{1,0:T(8,128)(2,1)S(1)} collective-permute-done((bf16[128,128]{1,0:T(8,128)(2,1)S(1)}, bf16[128,128]{1,0:T(8,128)(2,1)S(1)}, u32[]{:S(2)}, u32[]{:S(2)}) %collective-permute-start.6) | collective-permute-done | bytes 32800 | tf_op jit(solution)/shard_map/ppermute | solution.py:367
  95.0 0.0 collective-permute-done.7.kv3
  95.0 13.2 %all_to_all.29.suf_ref = bf16[8,128,128]{2,1,0:T(8,128)(2,1)S(1)} all-to-all(bf16[8,128,128]{2,1,0:T(8,128)(2,1)S(1)} %shard_map.130), channel_id=1, replica_groups={{56,48,40,32,24,16,8,0},{57,49,41,33,25,17,9,1},{58,50,42,34,26,18,10,2..., dimensions={0} | all-to-all | bytes 524288 | tf_op jit(solution)/shard_map/all_to_all | solution.py:382
  108.3 15.2 %shard_map.131 = (bf16[512,8,128]{2,1,0:T(8,128)(2,1)}, bf16[512,8,128]{2,1,0:T(8,128)(2,1)}, bf16[512,8,128]{2,1,0:T(8,128)(2,1)}, bf16[512,8,128]{2,1,0:T(8,128)(2,1)}, bf16[512,8,128]{2,1,0:T(8,128)(2,1)}) custom-call(s32[1]{0:T(128)} %bitcast.pos_ref, bf16[4096,128]{1,0:T(8,128)(2,1)S(1)} %get-tuple-element.102.sq_ref, ...), custom_call_target="tpu_custom_call" | custom-call | flops 4831838208 | bytes 13893636 | tf_op jit(solution)/shard_map/pallas_call | solution.py:49
  (3 shorter events, 0.1 us)
Async XLA Ops:
  0.6 1.2 copy-start.2
  1.9 1.2 copy-start.3
  1.9 18.1 %copy-start.5 = (bf16[512,1,128]{2,0,1:T(8,128)(2,1)S(1)}, bf16[512,1,128]{2,0,1:T(8,128)(2,1)}, u32[]{:S(2)}) copy-start(bf16[512,1,128]{2,0,1:T(8,128)(2,1)} %param.14) | copy-start | bytes 393220
  1.9 18.1 %copy-start.6 = (bf16[512,1,128]{2,0,1:T(8,128)(2,1)S(1)}, bf16[512,1,128]{2,0,1:T(8,128)(2,1)}, u32[]{:S(2)}) copy-start(bf16[512,1,128]{2,0,1:T(8,128)(2,1)} %param.15) | copy-start | bytes 393220
  3.1 28.1 %copy-start = (bf16[512,8,128]{2,1,0:T(8,128)(2,1)S(1)}, bf16[512,8,128]{2,1,0:T(8,128)(2,1)}, u32[]{:S(2)}) copy-start(bf16[512,8,128]{2,1,0:T(8,128)(2,1)} %q_ref) | copy-start | bytes 3145732
  3.1 28.1 %copy-start.1 = (bf16[512,8,128]{2,1,0:T(8,128)(2,1)S(1)}, bf16[512,8,128]{2,1,0:T(8,128)(2,1)}, u32[]{:S(2)}) copy-start(bf16[512,8,128]{2,1,0:T(8,128)(2,1)} %c_ref) | copy-start | bytes 3145732
  3.1 28.1 %copy-start.7 = (f32[8,128]{1,0:T(8,128)S(1)}, f32[8,128]{1,0:T(8,128)}, u32[]{:S(2)}) copy-start(f32[8,128]{1,0:T(8,128)} %gain_ref.3) | copy-start | bytes 12292
  20.0 15.0 %collective-permute-start.3 = (bf16[2,512,128]{2,1,0:T(8,128)(2,1)S(1)}, bf16[2,512,128]{2,1,0:T(8,128)(2,1)S(1)}, u32[]{:S(2)}, u32[]{:S(2)}) collective-permute-start(bf16[2,512,128]{2,1,0:T(8,128)(2,1)S(1)} %get-tuple-element.68.kv0), channel_id=1, source_target_pairs={{0,8},{8,16},{16,24},{24,32},{32,40},{40,48},{48,56},{56,64},{64,7... | collective-permute-start | bytes 786440 | tf_op jit(solution)/shard_map/ppermute | solution.py:400
  24.4 9.4 %collective-permute-start.2 = (bf16[128,128]{1,0:T(8,128)(2,1)S(1)}, bf16[128,128]{1,0:T(8,128)(2,1)S(1)}, u32[]{:S(2)}, u32[]{:S(2)}) collective-permute-start(bf16[128,128]{1,0:T(8,128)(2,1)S(1)} %get-tuple-element.67), channel_id=1, source_target_pairs={{0,128},{64,192},{1,129},{65,193},{2,130},{66,194},{3,131},{67,195... | collective-permute-start | bytes 98312 | tf_op jit(solution)/shard_map/ppermute | solution.py:367
  28.6 5.2 %collective-permute-start.1 = (bf16[128,128]{1,0:T(8,128)(2,1)S(1)}, bf16[128,128]{1,0:T(8,128)(2,1)S(1)}, u32[]{:S(2)}, u32[]{:S(2)}) collective-permute-start(bf16[128,128]{1,0:T(8,128)(2,1)S(1)} %get-tuple-element.67), channel_id=1, source_target_pairs={{0,192},{1,193},{2,194},{3,195},{4,196},{5,197},{6,198},{7,199},{8... | collective-permute-start | bytes 98312 | tf_op jit(solution)/shard_map/ppermute | solution.py:367
  29.3 5.8 %collective-permute-start = (bf16[128,128]{1,0:T(8,128)(2,1)S(1)}, bf16[128,128]{1,0:T(8,128)(2,1)S(1)}, u32[]{:S(2)}, u32[]{:S(2)}) collective-permute-start(bf16[128,128]{1,0:T(8,128)(2,1)S(1)} %get-tuple-element.67), channel_id=1, source_target_pairs={{0,64},{64,128},{128,192},{1,65},{65,129},{129,193},{2,66},{66,130... | collective-permute-start | bytes 98312 | tf_op jit(solution)/shard_map/ppermute | solution.py:367
  48.4 13.6 %collective-permute-start.4 = (bf16[2,512,128]{2,1,0:T(8,128)(2,1)S(1)}, bf16[2,512,128]{2,1,0:T(8,128)(2,1)S(1)}, u32[]{:S(2)}, u32[]{:S(2)}) collective-permute-start(bf16[2,512,128]{2,1,0:T(8,128)(2,1)S(1)} %collective-permute-done.3.kv1), channel_id=1, source_target_pairs={{0,8},{8,16},{16,24},{24,32},{32,40},{40,48},{48,56},{56,64},{64,7... | collective-permute-start | bytes 786440 | tf_op jit(solution)/shard_map/ppermute | solution.py:400
  62.0 22.1 %copy-start.4 = (bf16[512,8,128]{2,1,0:T(8,128)(2,1)S(1)}, bf16[512,8,128]{2,1,0:T(8,128)(2,1)}, u32[]{:S(2)}) copy-start(bf16[512,8,128]{2,1,0:T(8,128)(2,1)} %q2_ref.1) | copy-start | bytes 3145732
  77.0 10.6 %collective-permute-start.5 = (bf16[128,128]{1,0:T(8,128)(2,1)S(1)}, bf16[128,128]{1,0:T(8,128)(2,1)S(1)}, u32[]{:S(2)}, u32[]{:S(2)}) collective-permute-start(bf16[128,128]{1,0:T(8,128)(2,1)S(1)} %shard_map.126.own_ref), channel_id=1, source_target_pairs={{64,0},{128,64},{192,128},{65,1},{129,65},{193,129},{66,2},{130,66... | collective-permute-start | bytes 98312 | tf_op jit(solution)/shard_map/ppermute | solution.py:367
  79.7 15.3 %collective-permute-start.7 = (bf16[2,512,128]{2,1,0:T(8,128)(2,1)S(1)}, bf16[2,512,128]{2,1,0:T(8,128)(2,1)S(1)}, u32[]{:S(2)}, u32[]{:S(2)}) collective-permute-start(bf16[2,512,128]{2,1,0:T(8,128)(2,1)S(1)} %collective-permute-done.4.kv2), channel_id=1, source_target_pairs={{0,8},{8,16},{16,24},{24,32},{32,40},{40,48},{48,56},{56,64},{64,7... | collective-permute-start | bytes 786440 | tf_op jit(solution)/shard_map/ppermute | solution.py:400
  87.7 7.3 %collective-permute-start.6 = (bf16[128,128]{1,0:T(8,128)(2,1)S(1)}, bf16[128,128]{1,0:T(8,128)(2,1)S(1)}, u32[]{:S(2)}, u32[]{:S(2)}) collective-permute-start(bf16[128,128]{1,0:T(8,128)(2,1)S(1)} %shard_map.128), channel_id=1, source_target_pairs={{128,0},{192,64},{129,1},{193,65},{130,2},{194,66},{131,3},{195,67... | collective-permute-start | bytes 98312 | tf_op jit(solution)/shard_map/ppermute | solution.py:367
